TPU v7x, 32 devices: a whole 2x2x4 slice. The times are simulated.
32 devices in a mesh: dp: 4 (over z), seq: 8 (over y, x, core).
Axes of the slice: x: 2, y: 2, z: 4, core: 2. Of those that a mesh axis runs over, the one named last changes fastest.
Arguments:
- source_tokens: bfloat16 [2048, 8, 1024], P('seq', 'dp'), may hold values from -6 to 6
- target_tokens: bfloat16 [128, 8, 1024], P('seq', 'dp'), may hold values from -6 to 6
- source_lengths: int32 [8], P('dp'), may hold values from 512 to 2048, as said below
- target_lengths: int32 [8], P('dp'), may hold values from 32 to 128, as said below
- encoder_query: bfloat16 [1024, 1024], replicated, may hold values from -0.25 to 0.25
- encoder_key: bfloat16 [1024, 1024], replicated, may hold values from -0.1875 to 0.1875
- encoder_value: bfloat16 [1024, 1024], replicated, may hold values from -0.1875 to 0.1875
- encoder_mix: bfloat16 [1024, 1024], replicated, may hold values from -3 to 3
- attend_gain: float32 [1024], replicated, may hold values from 0.5 to 1.5
- attend_shift: float32 [1024], replicated, may hold values from -1.75 to 1.75
- encoder_expand: bfloat16 [1024, 4096], P(None, 'seq'), may hold values from -0.1875 to 0.1875
- encoder_contract: bfloat16 [4096, 1024], P('seq'), may hold values from -0.09375 to 0.09375
- encoder_gain: float32 [1024], replicated, may hold values from 0.5 to 1.5
- encoder_shift: float32 [1024], replicated, may hold values from -1.75 to 1.75
- decoder_query: bfloat16 [1024, 1024], replicated, may hold values from -0.25 to 0.25
- decoder_key: bfloat16 [1024, 1024], replicated, may hold values from -0.1875 to 0.1875
- decoder_value: bfloat16 [1024, 1024], replicated, may hold values from -0.1875 to 0.1875
- decoder_mix: bfloat16 [1024, 1024], replicated, may hold values from -0.5 to 0.5
- self_gain: float32 [1024], replicated, may hold values from 0.5 to 1.5
- self_shift: float32 [1024], replicated, may hold values from -1.75 to 1.75
- cross_query: bfloat16 [1024, 1024], replicated, may hold values from -0.25 to 0.25
- cross_key: bfloat16 [1024, 1024], replicated, may hold values from -0.1875 to 0.1875
- cross_value: bfloat16 [1024, 1024], replicated, may hold values from -0.1875 to 0.1875
- cross_mix: bfloat16 [1024, 1024], replicated, may hold values from -3 to 3
- cross_gain: float32 [1024], replicated, may hold values from 0.5 to 1.5
- cross_shift: float32 [1024], replicated, may hold values from -1.75 to 1.75
- decoder_expand: bfloat16 [1024, 4096], P(None, 'seq'), may hold values from -0.1875 to 0.1875
- decoder_contract: bfloat16 [4096, 1024], P('seq'), may hold values from -0.09375 to 0.09375
- decoder_gain: float32 [1024], replicated, may hold values from 0.5 to 1.5
- decoder_shift: float32 [1024], replicated, may hold values from -1.75 to 1.75
- source_cotangent: bfloat16 [2048, 8, 1024], P('seq', 'dp'), may hold values from -6 to 6
- target_cotangent: bfloat16 [128, 8, 1024], P('seq', 'dp'), may hold values from -6 to 6
Outputs:
- encoded: bfloat16 [2048, 8, 1024], P('seq', 'dp')
- decoded: bfloat16 [128, 8, 1024], P('seq', 'dp')
- grad_source: float32 [2048, 8, 1024], P('seq', 'dp')
- grad_target: float32 [128, 8, 1024], P('seq', 'dp')
- grad_encoder_query: float32 [1024, 1024], P('seq')
- grad_encoder_key: float32 [1024, 1024], P('seq')
- grad_encoder_value: float32 [1024, 1024], P('seq')
- grad_encoder_mix: float32 [1024, 1024], P('seq')
- grad_attend_gain: float32 [1024], P('seq')
- grad_attend_shift: float32 [1024], P('seq')
- grad_encoder_expand: float32 [1024, 4096], P(None, 'seq')
- grad_encoder_contract: float32 [4096, 1024], P('seq')
- grad_encoder_gain: float32 [1024], P('seq')
- grad_encoder_shift: float32 [1024], P('seq')
- grad_decoder_query: float32 [1024, 1024], P('seq')
- grad_decoder_key: float32 [1024, 1024], P('seq')
- grad_decoder_value: float32 [1024, 1024], P('seq')
- grad_decoder_mix: float32 [1024, 1024], P('seq')
- grad_self_gain: float32 [1024], P('seq')
- grad_self_shift: float32 [1024], P('seq')
- grad_cross_query: float32 [1024, 1024], P('seq')
- grad_cross_key: float32 [1024, 1024], P('seq')
- grad_cross_value: float32 [1024, 1024], P('seq')
- grad_cross_mix: float32 [1024, 1024], P('seq')
- grad_cross_gain: float32 [1024], P('seq')
- grad_cross_shift: float32 [1024], P('seq')
- grad_decoder_expand: float32 [1024, 4096], P(None, 'seq')
- grad_decoder_contract: float32 [4096, 1024], P('seq')
- grad_decoder_gain: float32 [1024], P('seq')
- grad_decoder_shift: float32 [1024], P('seq')
Inputs may be any that keep to these rules, and one draw needn't show every extreme that they name: `source_lengths`: in each aligned group of 2 tables (one index of dp) one table, drawn from the seed, has exactly 2048 used slots. `target_lengths`: in each aligned group of 2 tables one table, drawn from the seed, has exactly 128 used slots.
All inputs are finite; a program needn't handle non-finite values.
Results may differ from a plain program's by a relative error of at most 0.034.
Values may be sent and summed in bfloat16 or wider, within the bound.
A program may use at most 320 MiB of HBM per device.

v0:
```python
import jax
import jax.numpy as jnp
from jax import lax
from jax.sharding import PartitionSpec as P

HEADS = 16


masked_fill = -1e30
norm_epsilon = 1e-05


def layer_norm(rows, gain, shift):
    centre = jnp.mean(rows, -1, keepdims=True)
    centred = rows - centre
    spread = jnp.mean(centred * centred, -1, keepdims=True)
    return centred * lax.rsqrt(spread + norm_epsilon) * gain + shift


def gelu_exact(values):
    return jax.nn.gelu(values, approximate=False)


def project(rows, weight):
    return jnp.dot(rows, weight, preferred_element_type=jnp.float32)


def project_back(grads, weight):
    return jnp.einsum("re,de->rd", grads, weight, preferred_element_type=jnp.float32)


def outer_sum(rows, grads):
    return jnp.einsum("rd,re->de", rows, grads, preferred_element_type=jnp.float32)


def by_heads(array):
    return array.reshape(array.shape[0], HEADS, -1)


def head_scale(width):
    return (width // HEADS) ** (-0.5)


def score_block(queries, keys):
    scores = jnp.einsum(
        "qhd,khd->hqk", by_heads(queries), by_heads(keys), preferred_element_type=jnp.float32
    )
    return scores * head_scale(queries.shape[-1])


def allowed_keys(query_rows, key_rows, length, causal):
    allowed = key_rows[None, :] < length
    if causal:
        allowed = allowed & (key_rows[None, :] <= query_rows[:, None])
    return allowed


def table_of(array, table):
    return lax.dynamic_index_in_dim(array, table, 1, keepdims=False)


def gather_pair(keys, values):
    return (
        lax.all_gather(keys, "seq", axis=0, tiled=True),
        lax.all_gather(values, "seq", axis=0, tiled=True),
    )


def gather_rows(rows):
    return lax.all_gather(rows, "seq", axis=0, tiled=True)


def sum_rows(terms, count):
    return lax.psum_scatter(
        terms(jnp.int32(0), count * lax.axis_size("seq")).astype(jnp.bfloat16),
        "seq",
        scatter_dimension=0,
        tiled=True,
    ).astype(jnp.float32)


def projections(from_rows, to_rows, w_query, w_key, w_value):
    qlen, tables, width = from_rows.shape
    klen = to_rows.shape[0]
    to_flat = to_rows.reshape(-1, width)
    queries = (
        project(from_rows.reshape(-1, width), w_query)
        .astype(jnp.bfloat16)
        .reshape(qlen, tables, width)
    )
    keys = project(to_flat, w_key).astype(jnp.bfloat16).reshape(klen, tables, width)
    values = project(to_flat, w_value).astype(jnp.bfloat16).reshape(klen, tables, width)
    return (queries, keys, values)


def finish_grads(from_rows, to_rows, w_query, w_key, w_value, d_queries, d_keys, d_values):
    width = from_rows.shape[-1]
    from_flat = from_rows.reshape(-1, width)
    to_flat = to_rows.reshape(-1, width)
    query_low = d_queries.astype(jnp.bfloat16).reshape(-1, width)
    key_low = d_keys.astype(jnp.bfloat16).reshape(-1, width)
    value_low = d_values.astype(jnp.bfloat16).reshape(-1, width)
    grad_query = outer_sum(from_flat, query_low)
    grad_key = outer_sum(to_flat, key_low)
    grad_value = outer_sum(to_flat, value_low)
    d_from = project_back(query_low, w_query)
    d_to = project_back(key_low, w_key) + project_back(value_low, w_value)
    return (d_from, d_to, grad_query, grad_key, grad_value)


def attend_forward(from_rows, to_rows, w_query, w_key, w_value, lengths, causal):
    qlen, tables, width = from_rows.shape
    queries, keys, values = projections(from_rows, to_rows, w_query, w_key, w_value)
    gathered = gather_pair(keys, values)
    all_keys, all_values = gathered
    query_rows = lax.axis_index("seq") * qlen + jnp.arange(qlen)
    key_rows = jnp.arange(all_keys.shape[0])

    def one_table(table):
        scores = score_block(table_of(queries, table), table_of(all_keys, table))
        allowed = allowed_keys(query_rows, key_rows, lengths[table], causal)
        scores = jnp.where(allowed[None], scores, masked_fill)
        top = jnp.max(scores, -1)
        weights = jnp.exp(scores - top[..., None])
        total = jnp.sum(weights, -1)
        probs = (weights / total[..., None]).astype(jnp.bfloat16)
        context = jnp.einsum(
            "hqk,khd->qhd",
            probs,
            by_heads(table_of(all_values, table)),
            preferred_element_type=jnp.float32,
        )
        return (context.reshape(qlen, width), top + jnp.log(total))

    context, logsum = lax.map(one_table, jnp.arange(tables))
    return (queries, keys, values, gathered, jnp.swapaxes(context, 0, 1), logsum)


def key_value_terms(
    query_part,
    grads_part,
    logsum_part,
    delta_part,
    key_part,
    value_part,
    query_rows,
    part_rows,
    length,
    causal,
    scale,
):
    scores = score_block(query_part, key_part)
    allowed = allowed_keys(query_rows, part_rows, length, causal)
    probs = jnp.where(allowed[None], jnp.exp(scores - logsum_part[..., None]), 0.0)
    grads_here = by_heads(grads_part)
    d_values = jnp.einsum(
        "hqk,qhd->khd", probs.astype(jnp.bfloat16), grads_here, preferred_element_type=jnp.float32
    )
    d_probs = jnp.einsum(
        "qhd,khd->hqk", grads_here, by_heads(value_part), preferred_element_type=jnp.float32
    )
    d_scores = (probs * (d_probs - delta_part.T[..., None])).astype(jnp.bfloat16)
    d_keys = (
        jnp.einsum(
            "hqk,qhd->khd", d_scores, by_heads(query_part), preferred_element_type=jnp.float32
        )
        * scale
    )
    count = key_part.shape[0]
    width = key_part.shape[-1]
    return jnp.concatenate([d_keys.reshape(count, width), d_values.reshape(count, width)], -1)


def attend_backward(state, from_rows, to_rows, w_query, w_key, w_value, lengths, causal, d_context):
    queries, keys, values, gathered, context, logsum = state
    qlen, tables, width = queries.shape
    klen = keys.shape[0]
    all_keys, all_values = gather_pair(keys, values)
    scale = head_scale(width)
    d_low = d_context.reshape(qlen, tables, width).astype(jnp.bfloat16)
    delta = jnp.sum((d_low.astype(jnp.float32) * context).reshape(qlen, tables, HEADS, -1), -1)
    query_rows = lax.axis_index("seq") * qlen + jnp.arange(qlen)
    key_rows = jnp.arange(all_keys.shape[0])

    def query_table(table):
        scores = score_block(table_of(queries, table), table_of(all_keys, table))
        allowed = allowed_keys(query_rows, key_rows, lengths[table], causal)
        probs = jnp.where(allowed[None], jnp.exp(scores - logsum[table][..., None]), 0.0)
        d_probs = jnp.einsum(
            "qhd,khd->hqk",
            by_heads(table_of(d_low, table)),
            by_heads(table_of(all_values, table)),
            preferred_element_type=jnp.float32,
        )
        d_scores = (probs * (d_probs - delta[:, table].T[..., None])).astype(jnp.bfloat16)
        d_query = jnp.einsum(
            "hqk,khd->qhd",
            d_scores,
            by_heads(table_of(all_keys, table)),
            preferred_element_type=jnp.float32,
        )
        return (d_query * scale).reshape(qlen, width)

    d_queries = jnp.swapaxes(lax.map(query_table, jnp.arange(tables)), 0, 1)
    part_rows = jnp.arange(klen * lax.axis_size("seq"))

    def key_table(table, terms):
        piece = key_value_terms(
            table_of(queries, table),
            table_of(d_low, table),
            logsum[table],
            delta[:, table],
            table_of(all_keys, table),
            table_of(all_values, table),
            query_rows,
            part_rows,
            lengths[table],
            causal,
            scale,
        )
        return lax.dynamic_update_index_in_dim(terms, piece, table, 1)

    summed = lax.psum_scatter(
        lax.fori_loop(
            0,
            tables,
            key_table,
            jnp.zeros((klen * lax.axis_size("seq"), tables, 2 * width), jnp.float32),
        ).astype(jnp.bfloat16),
        "seq",
        scatter_dimension=0,
        tiled=True,
    ).astype(jnp.float32)
    return finish_grads(
        from_rows,
        to_rows,
        w_query,
        w_key,
        w_value,
        d_queries,
        summed[..., :width],
        summed[..., width:],
    )


def token_forward(rows, w_expand, w_contract):
    all_rows = gather_rows(rows)
    acts = gelu_exact(project(all_rows, w_expand)).astype(jnp.bfloat16)

    def contract_terms(start, count):
        return project(acts, w_contract)

    return (sum_rows(contract_terms, rows.shape[0]), all_rows)


def token_backward(all_rows, d_out, w_expand, w_contract):
    all_grads = gather_rows(d_out.astype(jnp.bfloat16))
    acts, gelu_back = jax.vjp(gelu_exact, project(all_rows, w_expand))
    d_hidden = gelu_back(project_back(all_grads, w_contract))[0].astype(jnp.bfloat16)
    grad_expand = outer_sum(all_rows, d_hidden)
    grad_contract = outer_sum(acts.astype(jnp.bfloat16), all_grads)

    def expand_terms(start, count):
        return project_back(d_hidden, w_expand)

    return (sum_rows(expand_terms, d_out.shape[0]), grad_expand, grad_contract)


def body(
    source_tokens,
    target_tokens,
    source_lengths,
    target_lengths,
    encoder_query,
    encoder_key,
    encoder_value,
    encoder_mix,
    attend_gain,
    attend_shift,
    encoder_expand,
    encoder_contract,
    encoder_gain,
    encoder_shift,
    decoder_query,
    decoder_key,
    decoder_value,
    decoder_mix,
    self_gain,
    self_shift,
    cross_query,
    cross_key,
    cross_value,
    cross_mix,
    cross_gain,
    cross_shift,
    decoder_expand,
    decoder_contract,
    decoder_gain,
    decoder_shift,
    source_cotangent,
    target_cotangent,
):
    slots, tables, width = source_tokens.shape
    places = target_tokens.shape[0]
    source_flat = source_tokens.reshape(-1, width)
    target_flat = target_tokens.reshape(-1, width)
    encoder_state = attend_forward(
        source_tokens,
        source_tokens,
        encoder_query,
        encoder_key,
        encoder_value,
        source_lengths,
        False,
    )
    encoder_context = encoder_state[4].reshape(-1, width).astype(jnp.bfloat16)
    first, first_back = jax.vjp(
        layer_norm,
        source_flat.astype(jnp.float32) + project(encoder_context, encoder_mix),
        attend_gain,
        attend_shift,
    )
    first_low = first.astype(jnp.bfloat16)
    widened, encoder_kept = token_forward(first_low, encoder_expand, encoder_contract)
    second, second_back = jax.vjp(layer_norm, first + widened, encoder_gain, encoder_shift)
    encoded = second.astype(jnp.bfloat16).reshape(slots, tables, width)
    decoder_state = attend_forward(
        target_tokens,
        target_tokens,
        decoder_query,
        decoder_key,
        decoder_value,
        target_lengths,
        True,
    )
    decoder_context = decoder_state[4].reshape(-1, width).astype(jnp.bfloat16)
    third, third_back = jax.vjp(
        layer_norm,
        target_flat.astype(jnp.float32) + project(decoder_context, decoder_mix),
        self_gain,
        self_shift,
    )
    third_blocks = third.astype(jnp.bfloat16).reshape(places, tables, width)
    cross_state = attend_forward(
        third_blocks, encoded, cross_query, cross_key, cross_value, source_lengths, False
    )
    cross_context = cross_state[4].reshape(-1, width).astype(jnp.bfloat16)
    fourth, fourth_back = jax.vjp(
        layer_norm, third + project(cross_context, cross_mix), cross_gain, cross_shift
    )
    fourth_low = fourth.astype(jnp.bfloat16)
    narrowed, decoder_kept = token_forward(fourth_low, decoder_expand, decoder_contract)
    fifth, fifth_back = jax.vjp(layer_norm, fourth + narrowed, decoder_gain, decoder_shift)
    decoded = fifth.astype(jnp.bfloat16).reshape(places, tables, width)
    d_fifth, grad_decoder_gain, grad_decoder_shift = fifth_back(
        target_cotangent.reshape(-1, width).astype(jnp.float32)
    )
    d_rows, grad_decoder_expand, grad_decoder_contract = token_backward(
        decoder_kept, d_fifth, decoder_expand, decoder_contract
    )
    d_fourth, grad_cross_gain, grad_cross_shift = fourth_back(d_fifth + d_rows)
    cross_low = d_fourth.astype(jnp.bfloat16)
    grad_cross_mix = outer_sum(cross_context, cross_low)
    d_cross_context = project_back(cross_low, cross_mix)
    d_third_cross, d_encoded, grad_cross_query, grad_cross_key, grad_cross_value = attend_backward(
        cross_state,
        third_blocks,
        encoded,
        cross_query,
        cross_key,
        cross_value,
        source_lengths,
        False,
        d_cross_context,
    )
    d_third, grad_self_gain, grad_self_shift = third_back(d_fourth + d_third_cross)
    self_low = d_third.astype(jnp.bfloat16)
    grad_decoder_mix = outer_sum(decoder_context, self_low)
    d_from, d_to, grad_decoder_query, grad_decoder_key, grad_decoder_value = attend_backward(
        decoder_state,
        target_tokens,
        target_tokens,
        decoder_query,
        decoder_key,
        decoder_value,
        target_lengths,
        True,
        project_back(self_low, decoder_mix),
    )
    grad_target = (d_third + d_from + d_to).reshape(places, tables, width)
    d_second, grad_encoder_gain, grad_encoder_shift = second_back(
        source_cotangent.reshape(-1, width).astype(jnp.float32) + d_encoded
    )
    d_rows, grad_encoder_expand, grad_encoder_contract = token_backward(
        encoder_kept, d_second, encoder_expand, encoder_contract
    )
    d_first, grad_attend_gain, grad_attend_shift = first_back(d_second + d_rows)
    encoder_low = d_first.astype(jnp.bfloat16)
    grad_encoder_mix = outer_sum(encoder_context, encoder_low)
    d_from, d_to, grad_encoder_query, grad_encoder_key, grad_encoder_value = attend_backward(
        encoder_state,
        source_tokens,
        source_tokens,
        encoder_query,
        encoder_key,
        encoder_value,
        source_lengths,
        False,
        project_back(encoder_low, encoder_mix),
    )
    grad_source = (d_first + d_from + d_to).reshape(slots, tables, width)
    shards = (
        lax.psum_scatter(
            grad_encoder_query.astype(jnp.bfloat16), "seq", scatter_dimension=0, tiled=True
        ).astype(jnp.float32),
        lax.psum_scatter(
            grad_encoder_key.astype(jnp.bfloat16), "seq", scatter_dimension=0, tiled=True
        ).astype(jnp.float32),
        lax.psum_scatter(
            grad_encoder_value.astype(jnp.bfloat16), "seq", scatter_dimension=0, tiled=True
        ).astype(jnp.float32),
        lax.psum_scatter(
            grad_encoder_mix.astype(jnp.bfloat16), "seq", scatter_dimension=0, tiled=True
        ).astype(jnp.float32),
        lax.psum_scatter(
            grad_decoder_query.astype(jnp.bfloat16), "seq", scatter_dimension=0, tiled=True
        ).astype(jnp.float32),
        lax.psum_scatter(
            grad_decoder_key.astype(jnp.bfloat16), "seq", scatter_dimension=0, tiled=True
        ).astype(jnp.float32),
        lax.psum_scatter(
            grad_decoder_value.astype(jnp.bfloat16), "seq", scatter_dimension=0, tiled=True
        ).astype(jnp.float32),
        lax.psum_scatter(
            grad_decoder_mix.astype(jnp.bfloat16), "seq", scatter_dimension=0, tiled=True
        ).astype(jnp.float32),
        lax.psum_scatter(
            grad_cross_query.astype(jnp.bfloat16), "seq", scatter_dimension=0, tiled=True
        ).astype(jnp.float32),
        lax.psum_scatter(
            grad_cross_key.astype(jnp.bfloat16), "seq", scatter_dimension=0, tiled=True
        ).astype(jnp.float32),
        lax.psum_scatter(
            grad_cross_value.astype(jnp.bfloat16), "seq", scatter_dimension=0, tiled=True
        ).astype(jnp.float32),
        lax.psum_scatter(
            grad_cross_mix.astype(jnp.bfloat16), "seq", scatter_dimension=0, tiled=True
        ).astype(jnp.float32),
        lax.psum_scatter(
            grad_attend_gain.astype(jnp.bfloat16), "seq", scatter_dimension=0, tiled=True
        ).astype(jnp.float32),
        lax.psum_scatter(
            grad_attend_shift.astype(jnp.bfloat16), "seq", scatter_dimension=0, tiled=True
        ).astype(jnp.float32),
        lax.psum_scatter(
            grad_encoder_gain.astype(jnp.bfloat16), "seq", scatter_dimension=0, tiled=True
        ).astype(jnp.float32),
        lax.psum_scatter(
            grad_encoder_shift.astype(jnp.bfloat16), "seq", scatter_dimension=0, tiled=True
        ).astype(jnp.float32),
        lax.psum_scatter(
            grad_self_gain.astype(jnp.bfloat16), "seq", scatter_dimension=0, tiled=True
        ).astype(jnp.float32),
        lax.psum_scatter(
            grad_self_shift.astype(jnp.bfloat16), "seq", scatter_dimension=0, tiled=True
        ).astype(jnp.float32),
        lax.psum_scatter(
            grad_cross_gain.astype(jnp.bfloat16), "seq", scatter_dimension=0, tiled=True
        ).astype(jnp.float32),
        lax.psum_scatter(
            grad_cross_shift.astype(jnp.bfloat16), "seq", scatter_dimension=0, tiled=True
        ).astype(jnp.float32),
        lax.psum_scatter(
            grad_decoder_gain.astype(jnp.bfloat16), "seq", scatter_dimension=0, tiled=True
        ).astype(jnp.float32),
        lax.psum_scatter(
            grad_decoder_shift.astype(jnp.bfloat16), "seq", scatter_dimension=0, tiled=True
        ).astype(jnp.float32),
    )
    totals = (
        lax.psum(shards[0].astype(jnp.bfloat16), "dp").astype(jnp.float32),
        lax.psum(shards[1].astype(jnp.bfloat16), "dp").astype(jnp.float32),
        lax.psum(shards[2].astype(jnp.bfloat16), "dp").astype(jnp.float32),
        lax.psum(shards[3].astype(jnp.bfloat16), "dp").astype(jnp.float32),
        lax.psum(shards[4].astype(jnp.bfloat16), "dp").astype(jnp.float32),
        lax.psum(shards[5].astype(jnp.bfloat16), "dp").astype(jnp.float32),
        lax.psum(shards[6].astype(jnp.bfloat16), "dp").astype(jnp.float32),
        lax.psum(shards[7].astype(jnp.bfloat16), "dp").astype(jnp.float32),
        lax.psum(shards[8].astype(jnp.bfloat16), "dp").astype(jnp.float32),
        lax.psum(shards[9].astype(jnp.bfloat16), "dp").astype(jnp.float32),
        lax.psum(shards[10].astype(jnp.bfloat16), "dp").astype(jnp.float32),
        lax.psum(shards[11].astype(jnp.bfloat16), "dp").astype(jnp.float32),
        lax.psum(shards[12].astype(jnp.bfloat16), "dp").astype(jnp.float32),
        lax.psum(shards[13].astype(jnp.bfloat16), "dp").astype(jnp.float32),
        lax.psum(shards[14].astype(jnp.bfloat16), "dp").astype(jnp.float32),
        lax.psum(shards[15].astype(jnp.bfloat16), "dp").astype(jnp.float32),
        lax.psum(shards[16].astype(jnp.bfloat16), "dp").astype(jnp.float32),
        lax.psum(shards[17].astype(jnp.bfloat16), "dp").astype(jnp.float32),
        lax.psum(shards[18].astype(jnp.bfloat16), "dp").astype(jnp.float32),
        lax.psum(shards[19].astype(jnp.bfloat16), "dp").astype(jnp.float32),
        lax.psum(shards[20].astype(jnp.bfloat16), "dp").astype(jnp.float32),
        lax.psum(shards[21].astype(jnp.bfloat16), "dp").astype(jnp.float32),
        lax.psum(grad_encoder_expand.astype(jnp.bfloat16), "dp").astype(jnp.float32),
        lax.psum(grad_encoder_contract.astype(jnp.bfloat16), "dp").astype(jnp.float32),
        lax.psum(grad_decoder_expand.astype(jnp.bfloat16), "dp").astype(jnp.float32),
        lax.psum(grad_decoder_contract.astype(jnp.bfloat16), "dp").astype(jnp.float32),
    )
    return (
        encoded,
        decoded,
        grad_source,
        grad_target,
        totals[0],
        totals[1],
        totals[2],
        totals[3],
        totals[12],
        totals[13],
        totals[22],
        totals[23],
        totals[14],
        totals[15],
        totals[4],
        totals[5],
        totals[6],
        totals[7],
        totals[16],
        totals[17],
        totals[8],
        totals[9],
        totals[10],
        totals[11],
        totals[18],
        totals[19],
        totals[24],
        totals[25],
        totals[20],
        totals[21],
    )


def solution(mesh):
    in_specs = (
        P("seq", "dp", None),
        P("seq", "dp", None),
        P("dp"),
        P("dp"),
        P(),
        P(),
        P(),
        P(),
        P(),
        P(),
        P(None, "seq"),
        P("seq", None),
        P(),
        P(),
        P(),
        P(),
        P(),
        P(),
        P(),
        P(),
        P(),
        P(),
        P(),
        P(),
        P(),
        P(),
        P(None, "seq"),
        P("seq", None),
        P(),
        P(),
        P("seq", "dp", None),
        P("seq", "dp", None),
    )
    out_specs = (
        P("seq", "dp", None),
        P("seq", "dp", None),
        P("seq", "dp", None),
        P("seq", "dp", None),
        P("seq", None),
        P("seq", None),
        P("seq", None),
        P("seq", None),
        P("seq"),
        P("seq"),
        P(None, "seq"),
        P("seq", None),
        P("seq"),
        P("seq"),
        P("seq", None),
        P("seq", None),
        P("seq", None),
        P("seq", None),
        P("seq"),
        P("seq"),
        P("seq", None),
        P("seq", None),
        P("seq", None),
        P("seq", None),
        P("seq"),
        P("seq"),
        P(None, "seq"),
        P("seq", None),
        P("seq"),
        P("seq"),
    )
    return jax.shard_map(body, mesh=mesh, in_specs=in_specs, out_specs=out_specs, check_vma=False)
```

profile of v0, /device:TPU:0, one launch (start us, length us, event | category | flops | bytes accessed | tf_op | source)
XLA Modules:
  0.0 2150.2 jit_solution(17138693065958069852)
XLA Ops:
  32.9 43.2 %all-gather.7.cloned.1.call-done = bf16[2048,2,1024]{0,2,1:T(8,128)(2,1)} async-done(((bf16[256,2,1024]{0,2,1:T(8,128)(2,1)}), bf16[2048,2,1024]{0,2,1:T(8,128)(2,1)}) %all-gather.7.cloned.1.call-update) | async-done | bytes 8388624 | tf_op jit(solution)/shard_map/all_gather | solution.py:65
  76.2 58.4 %all-gather.9.cloned.1.call-done = bf16[2048,2,1024]{0,2,1:T(8,128)(2,1)} async-done(((bf16[256,2,1024]{0,2,1:T(8,128)(2,1)}), bf16[2048,2,1024]{0,2,1:T(8,128)(2,1)}) %all-gather.9.cloned.1.call-update) | async-done | bytes 8388624 | tf_op jit(solution)/shard_map/all_gather | solution.py:64
  134.6 114.8 %while.126 = (s32[]{:T(128)}, f32[2,256,1024]{1,2,0:T(8,128)}, f32[2,16,256]{2,1,0:T(8,128)S(1)}, s32[2]{0:T(128)S(1)}, bf16[2048,2,1024]{0,2,1:T(8,128)(2,1)}, ...) while((s32[]{:T(128)}, f32[2,256,1024]{1,2,0:T(8,128)}, ...), condition=%wide.region_3.4_spmd.clone.clone, body=%wide.region_0.3_spmd.clone.sunk.clone | while | flops 2248144896 | bytes 130687640 | solution.py:135
  145.1 13.3 fusion.412
  158.4 14.4 fusion.413
  172.9 16.9 fusion.414
  202.5 13.3 fusion.412
  215.8 14.4 fusion.413
  230.2 16.9 fusion.414
  264.7 54.5 %all-gather.11.cloned.1.call-done = bf16[4096,1024]{1,0:T(8,128)(2,1)} async-done(((bf16[512,1024]{1,0:T(8,128)(2,1)}), bf16[4096,1024]{1,0:T(8,128)(2,1)}) %all-gather.11.cloned.1.call-update) | async-done | bytes 8388624 | tf_op jit(solution)/shard_map/all_gather | solution.py:70
  319.2 25.7 %multiply_convert_fusion.2 = (bf16[4096,512]{1,0:T(8,128)(2,1)S(1)}, f32[4096,512]{1,0:T(8,128)}, f32[4096,512]{1,0:T(8,128)}) fusion(bf16[4096,1024]{1,0:T(8,128)(2,1)} %all-gather.11.cloned.1.call-done, bf16[1024,512]{1,0:T(8,128)(2,1)} %param.60), kind=kOutput, calls=%fused_computation.189 | convolution fusion | flops 4431282176 | bytes 30408704 | tf_op jit(solution)/shard_map/dot_general | solution.py:25
  354.9 71.4 %reduce-scatter.32.cloned.1.call-done = bf16[512,1024]{1,0:T(8,128)(2,1)} async-done(((bf16[4096,1024]{1,0:T(8,128)(2,1)}), bf16[512,1024]{1,0:T(8,128)(2,1)}) %reduce-scatter.32.cloned.1.call-update) | async-done | bytes 1048592 | tf_op jit(solution)/shard_map/reduce_scatter | solution.py:74
  498.0 58.5 %all-gather.15.cloned.1.call-done = bf16[2048,2,1024]{0,2,1:T(8,128)(2,1)} async-done(((bf16[256,2,1024]{0,2,1:T(8,128)(2,1)}), bf16[2048,2,1024]{0,2,1:T(8,128)(2,1)}) %all-gather.15.cloned.1.call-update) | async-done | bytes 8388624 | tf_op jit(solution)/shard_map/all_gather | solution.py:64
  556.5 34.8 %while.127 = (s32[]{:T(128)}, f32[2,16,1024]{2,1,0:T(8,128)S(1)}, f32[2,16,16]{2,1,0:T(8,128)S(1)}, s32[2]{0:T(128)S(1)}, bf16[2048,2,1024]{0,2,1:T(8,128)(2,1)}...) while((s32[]{:T(128)}, f32[2,16,1024]{2,1,0:T(8,128)S(1)}, ...), condition=%wide.region_18.19_spmd.clone.clone, body=%wide.region_15.18_spmd.clone.sunk.clone | while | flops 138413824 | bytes 48891068 | solution.py:135
  609.0 34.2 %reduce-scatter.34.cloned.1.call-done = bf16[32,1024]{1,0:T(8,128)(2,1)} async-done(((bf16[256,1024]{1,0:T(8,128)(2,1)}), bf16[32,1024]{1,0:T(8,128)(2,1)}) %reduce-scatter.34.cloned.1.call-update) | async-done | bytes 65552 | tf_op jit(solution)/shard_map/reduce_scatter | solution.py:74
  660.7 34.2 %reduce-scatter.36.cloned.1.call-done = bf16[32,1024]{1,0:T(8,128)(2,1)} async-done(((bf16[256,1024]{1,0:T(8,128)(2,1)}), bf16[32,1024]{1,0:T(8,128)(2,1)}) %reduce-scatter.36.cloned.1.call-update) | async-done | bytes 65552 | tf_op jit(solution)/shard_map/reduce_scatter | solution.py:74
  706.5 60.8 %while.128 = (s32[]{:T(128)}, bf16[2048,2,2048]{0,2,1:T(8,128)(2,1)}, bf16[16,2,1024]{2,0,1:T(8,128)(2,1)S(1)}, s32[2]{0:T(128)S(1)}, bf16[2048,2,1024]{0,2,1:T(...) while((s32[]{:T(128)}, ...), condition=%wide.region_31.32_spmd.clone.clone, body=%wide.region_30.31_spmd.clone.sunk.clone | while | flops 293079040 | bytes 57027196 | solution.py:224
  770.6 113.4 %reduce-scatter.38.cloned.1.call-done = bf16[256,2,2048]{0,2,1:T(8,128)(2,1)} async-done(((bf16[2048,2,2048]{0,2,1:T(8,128)(2,1)}), bf16[256,2,2048]{0,2,1:T(8,128)(2,1)}) %reduce-scatter.38.cloned.1.call-update) | async-done | bytes 2097168 | tf_op jit(solution)/shard_map/reduce_scatter | solution.py:223
  906.9 54.5 %all-gather.17.cloned.1.call-done = bf16[4096,1024]{1,0:T(8,128)(2,1)} async-done(((bf16[512,1024]{1,0:T(8,128)(2,1)}), bf16[4096,1024]{1,0:T(8,128)(2,1)}) %all-gather.17.cloned.1.call-update) | async-done | bytes 8388624 | tf_op jit(solution)/shard_map/all_gather | solution.py:70
  961.4 14.9 add_convert_fusion
  986.2 44.2 %while.131 = (s32[]{:T(128)}, bf16[2,16,1024]{2,1,0:T(8,128)(2,1)S(1)}, s32[2]{0:T(128)S(1)}, bf16[2048,2,1024]{0,2,1:T(8,128)(2,1)}, s32[2]{0:T(128)S(1)}, /*in...) while((s32[]{:T(128)}, ...), condition=%wide.region_45.46_spmd.clone.clone, body=%wide.region_44.45_spmd.clone.sunk.clone | while | flops 204507136 | bytes 34121908 | solution.py:204
  1074.5 127.8 %while.130 = (s32[]{:T(128)}, bf16[2048,2,2048]{0,2,1:T(8,128)(2,1)}, bf16[256,2,1024]{0,2,1:T(8,128)(2,1)S(1)}, s32[2]{0:T(128)S(1)}, bf16[2048,2,1024]{0,2,1:T...) while((s32[]{:T(128)}, ...), condition=%wide.region_42.43_spmd.clone.clone, body=%wide.region_41.42_spmd.clone.sunk.clone | while | flops 4399826944 | bytes 155310736 | solution.py:224
  1081.3 13.2 fusion.443
  1095.8 18.6 broadcast_multiply_fusion.8
  1114.4 15.7 fusion.444
  1145.3 13.1 fusion.443
  1159.6 18.6 broadcast_multiply_fusion.8
  1178.3 15.7 fusion.444
  1203.3 12.2 while.133
  1236.3 89.9 %while.129 = (s32[]{:T(128)}, bf16[2,256,1024]{1,2,0:T(8,128)(2,1)}, s32[2]{0:T(128)S(1)}, bf16[2048,2,1024]{0,2,1:T(8,128)(2,1)}, s32[2]{0:T(128)S(1)}, /*index...) while((s32[]{:T(128)}, bf16[2,256,1024]{1,2,0:T(8,128)(2,1)}, ...), condition=%wide.region_40.41_spmd.clone.clone, body=%wide.region_39.40_spmd.clone.sunk.clone | while | flops 3272083456 | bytes 118067912 | solution.py:204
  1245.8 14.1 fusion.434
  1261.1 19.6 fusion.435
  1291.1 13.8 fusion.434
  1306.2 19.1 fusion.435
  1370.9 36.8 %reduce-scatter.66.cloned.1.call-done = bf16[128,1024]{1,0:T(8,128)(2,1)} async-done(((bf16[1024,1024]{1,0:T(8,128)(2,1)}), bf16[128,1024]{1,0:T(8,128)(2,1)}) %reduce-scatter.66.cloned.1.call-update) | async-done | bytes 262160
  1409.5 42.6 %reduce-scatter.68.cloned.1.call-done = bf16[128,1024]{1,0:T(8,128)(2,1)} async-done(((bf16[1024,1024]{1,0:T(8,128)(2,1)}), bf16[128,1024]{1,0:T(8,128)(2,1)}) %reduce-scatter.68.cloned.1.call-update) | async-done | bytes 262160
  1472.4 24.9 %reduce-scatter.58.cloned.1.call-done = bf16[128,1024]{1,0:T(8,128)(2,1)} async-done(((bf16[1024,1024]{1,0:T(8,128)(2,1)}), bf16[128,1024]{1,0:T(8,128)(2,1)}) %reduce-scatter.58.cloned.1.call-update) | async-done | bytes 262160
  1499.2 43.2 %reduce-scatter.60.cloned.1.call-done = bf16[128,1024]{1,0:T(8,128)(2,1)} async-done(((bf16[1024,1024]{1,0:T(8,128)(2,1)}), bf16[128,1024]{1,0:T(8,128)(2,1)}) %reduce-scatter.60.cloned.1.call-update) | async-done | bytes 262160
  1544.1 43.7 %reduce-scatter.62.cloned.1.call-done = bf16[128,1024]{1,0:T(8,128)(2,1)} async-done(((bf16[1024,1024]{1,0:T(8,128)(2,1)}), bf16[128,1024]{1,0:T(8,128)(2,1)}) %reduce-scatter.62.cloned.1.call-update) | async-done | bytes 262160
  1589.6 42.6 %reduce-scatter.56.cloned.1.call-done = bf16[128,1024]{1,0:T(8,128)(2,1)} async-done(((bf16[1024,1024]{1,0:T(8,128)(2,1)}), bf16[128,1024]{1,0:T(8,128)(2,1)}) %reduce-scatter.56.cloned.1.call-update) | async-done | bytes 262160 | tf_op jit(solution)/shard_map/reduce_scatter | solution.py:446
  1632.2 44.9 %reduce-scatter.48.cloned.1.call-done = bf16[128,1024]{1,0:T(8,128)(2,1)} async-done(((bf16[1024,1024]{1,0:T(8,128)(2,1)}), bf16[128,1024]{1,0:T(8,128)(2,1)}) %reduce-scatter.48.cloned.1.call-update) | async-done | bytes 262160 | tf_op jit(solution)/shard_map/reduce_scatter | solution.py:434
  1677.1 44.5 %reduce-scatter.50.cloned.1.call-done = bf16[128,1024]{1,0:T(8,128)(2,1)} async-done(((bf16[1024,1024]{1,0:T(8,128)(2,1)}), bf16[128,1024]{1,0:T(8,128)(2,1)}) %reduce-scatter.50.cloned.1.call-update) | async-done | bytes 262160 | tf_op jit(solution)/shard_map/reduce_scatter | solution.py:437
  1721.6 44.9 %reduce-scatter.52.cloned.1.call-done = bf16[128,1024]{1,0:T(8,128)(2,1)} async-done(((bf16[1024,1024]{1,0:T(8,128)(2,1)}), bf16[128,1024]{1,0:T(8,128)(2,1)}) %reduce-scatter.52.cloned.1.call-update) | async-done | bytes 262160 | tf_op jit(solution)/shard_map/reduce_scatter | solution.py:440
  1766.5 44.4 %reduce-scatter.54.cloned.1.call-done = bf16[128,1024]{1,0:T(8,128)(2,1)} async-done(((bf16[1024,1024]{1,0:T(8,128)(2,1)}), bf16[128,1024]{1,0:T(8,128)(2,1)}) %reduce-scatter.54.cloned.1.call-update) | async-done | bytes 262160 | tf_op jit(solution)/shard_map/reduce_scatter | solution.py:443
  1810.8 45.5 %reduce-scatter.46.cloned.1.call-done = bf16[128,1024]{1,0:T(8,128)(2,1)} async-done(((bf16[1024,1024]{1,0:T(8,128)(2,1)}), bf16[128,1024]{1,0:T(8,128)(2,1)}) %reduce-scatter.46.cloned.1.call-update) | async-done | bytes 262160 | tf_op jit(solution)/shard_map/reduce_scatter | solution.py:422
  1868.1 24.4 %all-reduce.10 = (bf16[1024]{0:T(1024)(128)(2,1)S(1)}, bf16[1024]{0:T(1024)(128)(2,1)S(1)}, bf16[1024]{0:T(1024)(128)(2,1)S(1)}, bf16[1024]{0:T(1024)(128)(2,1)S...) all-reduce(bf16[1024]{0:T(1024)(128)(2,1)S(1)} %copy-done.126, ...), channel_id=13, replica_groups=mesh['dp'=4,'seq'=8] {'seq'}, use_global_device_ids=true, to_apply=%region_63.64.clone | all-reduce | flops 10240 | bytes 40960
  1893.2 12.5 all-reduce.11
  1930.7 192.1 %all-reduce.15.cloned.1.call-done = (bf16[128,1024]{0,1:T(8,128)(2,1)}, bf16[128,1024]{0,1:T(8,128)(2,1)}, bf16[128,1024]{0,1:T(8,128)(2,1)}, bf16[128,1024]{0,1...) async-done(((bf16[128,1024]{0,1:T(8,128)(2,1)}, ...) | async-done | bytes 7340048 | tf_op jit(solution)/shard_map/psum | solution.py:481
  (826 shorter events, 629.7 us)
Async XLA Ops:
  7.2 423.5 %copy-start = (bf16[1024,1024]{1,0:T(8,128)(2,1)S(1)}, bf16[1024,1024]{1,0:T(8,128)(2,1)}, u32[]{:S(2)}) copy-start(bf16[1024,1024]{1,0:T(8,128)(2,1)} %param.72) | copy-start | bytes 6291460
  7.2 68.9 %all-gather.7.cloned.1.call-start = ((), (), s32[]{:S(2)}) async-start(), calls=%async_computation.19 | async-start | bytes 9437184 | tf_op jit(solution)/shard_map/all_gather | solution.py:65
  17.4 117.3 %all-gather.9.cloned.1.call-start = ((), (), s32[]{:S(2)}) async-start(), calls=%async_computation.20 | async-start | bytes 9437184 | tf_op jit(solution)/shard_map/all_gather | solution.py:64
  25.2 293.9 %all-gather.11.cloned.1.call-start = ((), (), s32[]{:S(2)}) async-start(), calls=%async_computation.21 | async-start | bytes 9437184 | tf_op jit(solution)/shard_map/all_gather | solution.py:70
  25.3 109.3 %copy-start.152 = (s32[2]{0:T(128)S(1)}, s32[2]{0:T(128)}, u32[]{:S(2)}) copy-start(s32[2]{0:T(128)} %param.52) | copy-start | bytes 28
  261.9 164.4 %copy-start.98 = (f32[512]{0:T(512)}, f32[512]{0:T(512)S(1)}, u32[]{:S(2)}) copy-start(f32[512]{0:T(512)S(1)} %broadcast_multiply_fusion.2) | copy-start | bytes 6148
  262.3 82.6 %copy-start.113 = (f32[512]{0:T(512)}, f32[512]{0:T(512)S(1)}, u32[]{:S(2)}) copy-start(f32[512]{0:T(512)S(1)} %multiply_reduce_fusion.5) | copy-start | bytes 6148
  263.2 163.1 %copy-start.103 = (f32[512]{0:T(512)}, f32[512]{0:T(512)S(1)}, u32[]{:S(2)}) copy-start(f32[512]{0:T(512)S(1)} %fusion.132) | copy-start | bytes 6148
  264.6 161.7 %reduce-scatter.32.cloned.1.call-start = ((), (), s32[]{:S(2)}) async-start(), calls=%async_computation.22 | async-start | bytes 9437184 | tf_op jit(solution)/shard_map/reduce_scatter | solution.py:74
  354.9 75.4 %copy-start.107 = (f32[1024]{0:T(1024)S(1)}, f32[1024]{0:T(1024)}, u32[]{:S(2)}) copy-start(f32[1024]{0:T(1024)} %param.62) | copy-start | bytes 12292
  354.9 75.4 %copy-start.142 = (f32[1024]{0:T(1024)S(1)}, f32[1024]{0:T(1024)}, u32[]{:S(2)}) copy-start(f32[1024]{0:T(1024)} %param.63) | copy-start | bytes 12292
  354.9 143.1 %all-gather.13.cloned.1.call-start = ((), (), s32[]{:S(2)}) async-start(), calls=%async_computation.23 | async-start | bytes 9437184 | tf_op jit(solution)/shard_map/all_gather | solution.py:65
  438.8 117.6 %all-gather.15.cloned.1.call-start = ((), (), s32[]{:S(2)}) async-start(), calls=%async_computation.24 | async-start | bytes 9437184 | tf_op jit(solution)/shard_map/all_gather | solution.py:64
  446.4 196.8 %reduce-scatter.34.cloned.1.call-start = ((), (), s32[]{:S(2)}) async-start(), calls=%async_computation.25 | async-start | bytes 589824 | tf_op jit(solution)/shard_map/reduce_scatter | solution.py:74
  489.9 66.5 %copy-start.75 = (f32[2,16,16]{2,1,0:T(8,128)}, f32[2,16,16]{2,1,0:T(8,128)S(1)}, u32[]{:S(2)}) copy-start(f32[2,16,16]{2,1,0:T(8,128)S(1)} %get-tuple-element.2911) | copy-start | bytes 6148
  489.9 66.5 %copy-start.20 = (bf16[16,2,1024]{2,0,1:T(8,128)(2,1)}, bf16[16,2,1024]{2,0,1:T(8,128)(2,1)S(1)}, u32[]{:S(2)}) copy-start(bf16[16,2,1024]{2,0,1:T(8,128)(2,1)S(1)} %get-tuple-element.3034) | copy-start | bytes 196612
  490.0 66.5 %copy-start.46 = (f32[2,16,1024]{2,1,0:T(8,128)}, f32[2,16,1024]{2,1,0:T(8,128)S(1)}, u32[]{:S(2)}) copy-start(f32[2,16,1024]{2,1,0:T(8,128)S(1)} %get-tuple-element.887) | copy-start | bytes 393220
  490.1 66.4 %copy-start.67 = (bf16[32,1024]{1,0:T(8,128)(2,1)}, bf16[32,1024]{1,0:T(8,128)(2,1)S(1)}, u32[]{:S(2)}) copy-start(bf16[32,1024]{1,0:T(8,128)(2,1)S(1)} %convert_element_type.487) | copy-start | bytes 196612
  492.3 99.2 %copy-start.17 = (f32[32,1024]{1,0:T(8,128)}, f32[32,1024]{1,0:T(8,128)S(1)}, u32[]{:S(2)}) copy-start(f32[32,1024]{1,0:T(8,128)S(1)} %get-tuple-element.1859) | copy-start | bytes 393220
  492.3 99.2 %copy-start.117 = (f32[32]{0:T(128)}, f32[32]{0:T(128)S(1)}, u32[]{:S(2)}) copy-start(f32[32]{0:T(128)S(1)} %broadcast_multiply_fusion.5) | copy-start | bytes 388
  492.5 63.9 %copy-start.144 = (f32[32]{0:T(128)}, f32[32]{0:T(128)S(1)}, u32[]{:S(2)}) copy-start(f32[32]{0:T(128)S(1)} %multiply_reduce_fusion.14) | copy-start | bytes 388
  492.6 98.9 %copy-start.123 = (f32[32]{0:T(128)}, f32[32]{0:T(128)S(1)}, u32[]{:S(2)}) copy-start(f32[32]{0:T(128)S(1)} %fusion.134) | copy-start | bytes 388
  608.9 86.0 %reduce-scatter.36.cloned.1.call-start = ((), (), s32[]{:S(2)}) async-start(), calls=%async_computation.26 | async-start | bytes 589824 | tf_op jit(solution)/shard_map/reduce_scatter | solution.py:74
  659.4 47.1 %copy-start.53 = (bf16[256,512]{1,0:T(8,128)(2,1)}, bf16[256,512]{1,0:T(8,128)(2,1)S(1)}, u32[]{:S(2)}) copy-start(bf16[256,512]{1,0:T(8,128)(2,1)S(1)} %add_convert_fusion.4) | copy-start | bytes 786436
  660.7 223.3 %reduce-scatter.38.cloned.1.call-start = ((), (), s32[]{:S(2)}) async-start(), calls=%async_computation.27 | async-start | bytes 18874368 | tf_op jit(solution)/shard_map/reduce_scatter | solution.py:223
  767.9 193.5 %all-gather.17.cloned.1.call-start = ((), (), s32[]{:S(2)}) async-start(), calls=%async_computation.28 | async-start | bytes 9437184 | tf_op jit(solution)/shard_map/all_gather | solution.py:70
  905.5 70.8 %copy-start.10 = (f32[512,1024]{1,0:T(8,128)}, f32[512,1024]{1,0:T(8,128)S(1)}, u32[]{:S(2)}) copy-start(f32[512,1024]{1,0:T(8,128)S(1)} %get-tuple-element.1797) | copy-start | bytes 6291460
  906.9 149.9 %reduce-scatter.40.cloned.1.call-start = ((), (), s32[]{:S(2)}) async-start(), calls=%async_computation.29 | async-start | bytes 9437184 | tf_op jit(solution)/shard_map/reduce_scatter | solution.py:74
  985.3 236.6 %reduce-scatter.44.cloned.1.call-start = ((), (), s32[]{:S(2)}) async-start(), calls=%async_computation.31 | async-start | bytes 1179648 | tf_op jit(solution)/shard_map/reduce_scatter | solution.py:223
  986.0 47.6 %copy-start.145 = (f32[32]{0:T(128)S(1)}, f32[32]{0:T(128)}, u32[]{:S(2)}) copy-start(f32[32]{0:T(128)} %copy-done.144) | copy-start | bytes 388
  1046.3 285.7 %reduce-scatter.42.cloned.1.call-start = ((), (), s32[]{:S(2)}) async-start(), calls=%async_computation.30 | async-start | bytes 18874368 | tf_op jit(solution)/shard_map/reduce_scatter | solution.py:223
  1202.4 166.7 %reduce-scatter.64.cloned.1.call-start = ((), (), s32[]{:S(2)}) async-start(), calls=%async_computation.41 | async-start | bytes 2359296
  1221.8 185.8 %reduce-scatter.66.cloned.1.call-start = ((), (), s32[]{:S(2)}) async-start(), calls=%async_computation.42 | async-start | bytes 2359296
  1229.1 223.0 %reduce-scatter.68.cloned.1.call-start = ((), (), s32[]{:S(2)}) async-start(), calls=%async_computation.43 | async-start | bytes 2359296
  1236.2 261.1 %reduce-scatter.58.cloned.1.call-start = ((), (), s32[]{:S(2)}) async-start(), calls=%async_computation.38 | async-start | bytes 2359296
  1331.7 210.6 %reduce-scatter.60.cloned.1.call-start = ((), (), s32[]{:S(2)}) async-start(), calls=%async_computation.39 | async-start | bytes 2359296
  1340.1 247.7 %reduce-scatter.62.cloned.1.call-start = ((), (), s32[]{:S(2)}) async-start(), calls=%async_computation.40 | async-start | bytes 2359296
  1346.8 285.3 %reduce-scatter.56.cloned.1.call-start = ((), (), s32[]{:S(2)}) async-start(), calls=%async_computation.37 | async-start | bytes 2359296 | tf_op jit(solution)/shard_map/reduce_scatter | solution.py:446
  1349.0 328.0 %reduce-scatter.48.cloned.1.call-start = ((), (), s32[]{:S(2)}) async-start(), calls=%async_computation.33 | async-start | bytes 2359296 | tf_op jit(solution)/shard_map/reduce_scatter | solution.py:434
  1351.3 370.3 %reduce-scatter.50.cloned.1.call-start = ((), (), s32[]{:S(2)}) async-start(), calls=%async_computation.34 | async-start | bytes 2359296 | tf_op jit(solution)/shard_map/reduce_scatter | solution.py:437
  1353.6 412.9 %reduce-scatter.52.cloned.1.call-start = ((), (), s32[]{:S(2)}) async-start(), calls=%async_computation.35 | async-start | bytes 2359296 | tf_op jit(solution)/shard_map/reduce_scatter | solution.py:440
  1357.5 453.3 %reduce-scatter.54.cloned.1.call-start = ((), (), s32[]{:S(2)}) async-start(), calls=%async_computation.36 | async-start | bytes 2359296 | tf_op jit(solution)/shard_map/reduce_scatter | solution.py:443
  1361.6 494.7 %reduce-scatter.46.cloned.1.call-start = ((), (), s32[]{:S(2)}) async-start(), calls=%async_computation.32 | async-start | bytes 2359296 | tf_op jit(solution)/shard_map/reduce_scatter | solution.py:422
  1365.7 757.1 %all-reduce.15.cloned.1.call-start = ((), (), s32[]{:S(2)}) async-start(), calls=%async_computation.44 | async-start | bytes 14680064 | tf_op jit(solution)/shard_map/psum | solution.py:481
  1499.2 357.2 %copy-start.94 = (bf16[16,2,1024]{2,1,0:T(2,128)(2,1)S(1)}, bf16[16,2,1024]{2,1,0:T(2,128)(2,1)}, u32[]{:S(2)}) copy-start(bf16[16,2,1024]{2,1,0:T(2,128)(2,1)} %param.81) | copy-start | bytes 196612
  1499.2 357.3 %copy-start.155 = (u32[32]{0:T(128)S(1)}, u32[32]{0:T(128)}, u32[]{:S(2)}) copy-start(u32[32]{0:T(128)} %constant.450) | copy-start | bytes 388
  1499.2 358.5 %copy-start.27 = (bf16[512,1024]{1,0:T(8,128)(2,1)S(1)}, bf16[512,1024]{1,0:T(8,128)(2,1)}, u32[]{:S(2)}) copy-start(bf16[512,1024]{1,0:T(8,128)(2,1)} %copy-done.25) | copy-start | bytes 3145732
  1860.6 50.1 %copy-start.29 = (bf16[2,256,1024]{1,2,0:T(8,128)(2,1)S(1)}, bf16[2,256,1024]{1,2,0:T(8,128)(2,1)}, u32[]{:S(2)}) copy-start(bf16[2,256,1024]{1,2,0:T(8,128)(2,1)} %get-tuple-element.892) | copy-start | bytes 3145732
  (139 other events, 1221.1 us)
Sparse Core Ops, SparseCore 0:
  17.5 58.6 all-gather.6
  78.6 55.9 all-gather.8
  264.7 54.3 all-gather.10
  355.0 71.2 reduce-scatter.31
  439.0 58.9 all-gather.12
  500.4 55.9 all-gather.14
  609.1 34.1 reduce-scatter.33
  660.8 34.1 reduce-scatter.35
  768.0 115.9 reduce-scatter.37
  907.0 54.3 all-gather.16
  985.4 71.2 reduce-scatter.39
  1060.3 35.9 reduce-scatter.43
  1202.5 115.9 reduce-scatter.41
  1321.7 41.1 reduce-scatter.63
  1366.4 41.2 reduce-scatter.65
  1410.8 41.1 reduce-scatter.67
  1456.1 41.2 reduce-scatter.57
  1501.1 41.1 reduce-scatter.59
  1546.5 41.2 reduce-scatter.61
  1590.9 41.1 reduce-scatter.55
  1635.8 41.2 reduce-scatter.47
  1680.3 41.1 reduce-scatter.49
  1725.2 41.2 reduce-scatter.51
  1769.6 41.1 reduce-scatter.53
  1815.0 41.2 reduce-scatter.45
  1860.3 262.4 all-reduce.14
where the time goes:
time: 2160 us; the launch traced here: 2150 us
  waiting for transfers between devices  1190 us (55%)
  matrix products  469 us (22%)
  local copies, waits for them, and re-layouts  254 us (12%)
  other arithmetic  118 us (5%)
  blocking collectives  79.1 us (4%)
  loops' own time  24.5 us (1%)
    psum x1, waiting for transfers between devices, body(): lax.psum(shards[0].astype(jnp.bfloat16), 'dp').astype(jnp.float32)  192 us
    unnamed x32, waiting for transfers between devices  192 us
    reduce_scatter x4, waiting for transfers between devices, sum_rows(): lax.psum_scatter(terms(jnp.int32(0), count * lax.axis_size('seq')).astype...  150 us
    all_gather x2, waiting for transfers between devices, gather_pair(): lax.all_gather(keys, 'seq', axis=0, tiled=True)  117 us
    reduce_scatter x3, waiting for transfers between devices, attend_backward(): lax.psum_scatter(lax.fori_loop(0, tables, key_table, jnp.zeros((klen * la...  113 us
    all_gather x2, waiting for transfers between devices, gather_rows(): return lax.all_gather(rows, 'seq', axis=0, tiled=True)  109 us
    dot_general x18, matrix products, score_block(): jnp.einsum('qhd,khd->hqk', by_heads(queries), by_heads(keys), preferred_e...  98.8 us
    dynamic_slice x36, local copies, waits for them, and re-layouts, table_of(): return lax.dynamic_index_in_dim(array, table, 1, keepdims=False)  96.8 us
  transfers between devices with their start and end apart: 26, of which 23 were waited for; matrix products, arithmetic and copies ran while one was open for 22% of the time, Pallas kernels for 0%

commit v1 on v0

--- a/solution.py
+++ b/solution.py
@@ -1,6 +1,10 @@
+import functools
+
 import jax
 import jax.numpy as jnp
 from jax import lax
+from jax.experimental import pallas as pl
+from jax.experimental.pallas import tpu as pltpu
 from jax.sharding import PartitionSpec as P
 
 HEADS = 16
@@ -266,7 +270,7 @@
     return (sum_rows(expand_terms, d_out.shape[0]), grad_expand, grad_contract)
 
 
-def body(
+def general_body(
     source_tokens,
     target_tokens,
     source_lengths,
@@ -539,7 +543,1006 @@
     )
 
 
+MESH = pl.DeviceIdType.MESH
+PEERS = (6, 7, 2, 3, 4, 5, 1)
+low = jnp.bfloat16
+wide = jnp.float32
+VMEM_BYTES = 60 * 2**20
+
+
+def fits_plane(mesh):
+    return mesh.shape["seq"] == 8
+
+
+def nt(left, right):
+    return lax.dot_general(left, right, (((1,), (1,)), ((), ())), preferred_element_type=wide)
+
+
+def nn(left, right):
+    return lax.dot_general(left, right, (((1,), (0,)), ((), ())), preferred_element_type=wide)
+
+
+def tn(left, right):
+    return lax.dot_general(left, right, (((0,), (0,)), ((), ())), preferred_element_type=wide)
+
+
+def lane_head(shape, size):
+    return lax.broadcasted_iota(jnp.int32, shape, len(shape) - 1) // size
+
+
+def vmem_spec():
+    return pl.BlockSpec(memory_space=pltpu.VMEM)
+
+
+def any_spec():
+    return pl.BlockSpec(memory_space=pl.ANY)
+
+
+def greet(masks):
+    me = lax.axis_index("seq")
+    barrier = pltpu.get_barrier_semaphore()
+    for mask in masks:
+        pl.semaphore_signal(barrier, inc=1, device_id={"seq": me ^ mask}, device_id_type=MESH)
+    pl.semaphore_wait(barrier, len(masks))
+
+
+def remote(src, dst, send, recv, to):
+    return pltpu.make_async_remote_copy(
+        src_ref=src, dst_ref=dst, send_sem=send, recv_sem=recv, device_id={"seq": to}, device_id_type=MESH
+    )
+
+
+def params(collective_id):
+    return pltpu.CompilerParams(
+        collective_id=collective_id, has_side_effects=True, vmem_limit_bytes=VMEM_BYTES
+    )
+
+
+def gather_table_kernel(rows, out, send, recv, keep):
+    me = lax.axis_index("seq")
+    mine = me // 4
+    greet((1, 2, 4, 6))
+    local = pltpu.make_async_copy(rows.at[mine], out.at[me], keep)
+    local.start()
+    started = []
+    for slot, mask, table in ((0, 6, 1 - mine), (1, 2, mine), (2, 4, 1 - mine), (3, 1, mine)):
+        copy = remote(rows.at[table], out.at[me], send.at[slot], recv.at[slot], me ^ mask)
+        copy.start()
+        started.append(copy)
+    for slot, mask in ((1, 2), (2, 4), (0, 6)):
+        owner = me ^ mask
+        remote(rows.at[0], out.at[owner], send.at[slot], recv.at[slot], me ^ 1).wait_recv()
+        copy = remote(out.at[owner], out.at[owner], send.at[4 + slot], recv.at[4 + slot], me ^ 1)
+        copy.start()
+        started.append(copy)
+    remote(rows.at[0], out.at[me ^ 1], send.at[3], recv.at[3], me ^ 1).wait_recv()
+    for slot, mask in ((1, 2), (2, 4), (0, 6)):
+        remote(rows.at[0], out.at[me ^ mask ^ 1], send.at[4 + slot], recv.at[4 + slot], me ^ 1).wait_recv()
+    for copy in started:
+        copy.wait_send()
+    local.wait()
+
+
+def gather_table(rows):
+    return pl.pallas_call(
+        gather_table_kernel,
+        out_shape=jax.ShapeDtypeStruct((8,) + rows.shape[1:], rows.dtype),
+        in_specs=[any_spec()],
+        out_specs=any_spec(),
+        scratch_shapes=[
+            pltpu.SemaphoreType.DMA((7,)),
+            pltpu.SemaphoreType.DMA((7,)),
+            pltpu.SemaphoreType.DMA,
+        ],
+        compiler_params=params(1),
+    )(rows)
+
+
+def heads_to_rows_kernel(blocks, out, send, recv, keep):
+    me = lax.axis_index("seq")
+    width = blocks.shape[2]
+    greet(PEERS)
+
+    def place(owner):
+        return out.at[owner // 4, :, pl.ds(pl.multiple_of((owner % 4) * width, width), width)]
+
+    local = pltpu.make_async_copy(blocks.at[me], place(me), keep)
+    local.start()
+    started = []
+    for mask in PEERS:
+        copy = remote(blocks.at[me ^ mask], place(me), send.at[mask], recv.at[mask], me ^ mask)
+        copy.start()
+        started.append(copy)
+    for mask in PEERS:
+        remote(blocks.at[0], place(me ^ mask), send.at[mask], recv.at[mask], me ^ mask).wait_recv()
+    for copy in started:
+        copy.wait_send()
+    local.wait()
+
+
+def heads_to_rows(blocks):
+    _, rows, width = blocks.shape
+    return pl.pallas_call(
+        heads_to_rows_kernel,
+        out_shape=jax.ShapeDtypeStruct((2, rows, 4 * width), blocks.dtype),
+        in_specs=[any_spec()],
+        out_specs=any_spec(),
+        scratch_shapes=[
+            pltpu.SemaphoreType.DMA((8,)),
+            pltpu.SemaphoreType.DMA((8,)),
+            pltpu.SemaphoreType.DMA,
+        ],
+        compiler_params=params(2),
+    )(blocks)
+
+
+def rows_to_heads_kernel(rows, out, send, recv, keep):
+    me = lax.axis_index("seq")
+    width = out.shape[2]
+    greet(PEERS)
+
+    def part(owner):
+        return rows.at[owner // 4, :, pl.ds(pl.multiple_of((owner % 4) * width, width), width)]
+
+    local = pltpu.make_async_copy(part(me), out.at[me], keep)
+    local.start()
+    started = []
+    for mask in PEERS:
+        copy = remote(part(me ^ mask), out.at[me], send.at[mask], recv.at[mask], me ^ mask)
+        copy.start()
+        started.append(copy)
+    for mask in PEERS:
+        remote(part(me), out.at[me ^ mask], send.at[mask], recv.at[mask], me ^ mask).wait_recv()
+    for copy in started:
+        copy.wait_send()
+    local.wait()
+
+
+def rows_to_heads(rows):
+    _, count, width = rows.shape
+    return pl.pallas_call(
+        rows_to_heads_kernel,
+        out_shape=jax.ShapeDtypeStruct((8, count, width // 4), rows.dtype),
+        in_specs=[any_spec()],
+        out_specs=any_spec(),
+        scratch_shapes=[
+            pltpu.SemaphoreType.DMA((8,)),
+            pltpu.SemaphoreType.DMA((8,)),
+            pltpu.SemaphoreType.DMA,
+        ],
+        compiler_params=params(3),
+    )(rows)
+
+
+def sum_small_kernel(terms, out, mine, came, send, recv, send_back, recv_back):
+    me = lax.axis_index("seq")
+    greet(PEERS)
+    mine[...] = terms[...].astype(low)
+    started = []
+    for mask in PEERS:
+        copy = remote(mine.at[me ^ mask], came.at[mask], send.at[mask], recv.at[mask], me ^ mask)
+        copy.start()
+        started.append(copy)
+    total = terms[me].astype(wide)
+    for mask in PEERS:
+        remote(mine.at[0], came.at[mask], send.at[mask], recv.at[mask], me ^ mask).wait_recv()
+        total = total + came[mask].astype(wide)
+    out[me] = total.astype(low)
+    for mask in PEERS:
+        copy = remote(out.at[me], out.at[me], send_back.at[mask], recv_back.at[mask], me ^ mask)
+        copy.start()
+        started.append(copy)
+    for mask in PEERS:
+        remote(mine.at[0], out.at[me ^ mask], send_back.at[mask], recv_back.at[mask], me ^ mask).wait_recv()
+    for copy in started:
+        copy.wait_send()
+
+
+def sum_small(terms):
+    count, width = terms.shape
+    blocks = (8, count // 8, width)
+    return pl.pallas_call(
+        sum_small_kernel,
+        out_shape=jax.ShapeDtypeStruct(blocks, low),
+        in_specs=[vmem_spec()],
+        out_specs=vmem_spec(),
+        scratch_shapes=[pltpu.VMEM(blocks, low), pltpu.VMEM(blocks, low)]
+        + [pltpu.SemaphoreType.DMA((8,))] * 4,
+        compiler_params=params(4),
+    )(terms.reshape(blocks)).reshape(count, width)
+
+
+def merge_parts_kernel(terms, stats, out, logsum, came, came_stats, send, recv, send_st, recv_st, back, recv_back, back_st, recv_back_st):
+    me = lax.axis_index("seq")
+    width = out.shape[2]
+    greet(PEERS)
+    started = []
+    for mask in PEERS:
+        for src, dst, s, r in ((stats, came_stats, send_st, recv_st), (terms, came, send, recv)):
+            copy = remote(src.at[me ^ mask], dst.at[mask], s.at[mask], r.at[mask], me ^ mask)
+            copy.start()
+            started.append(copy)
+    for mask in PEERS:
+        remote(stats.at[0], came_stats.at[mask], send_st.at[mask], recv_st.at[mask], me ^ mask).wait_recv()
+    tops = [stats[me, 0]] + [came_stats[mask, 0] for mask in PEERS]
+    sums = [stats[me, 1]] + [came_stats[mask, 1] for mask in PEERS]
+    top = functools.reduce(jnp.maximum, tops)
+    weights = [s * jnp.exp(t - top) for t, s in zip(tops, sums)]
+    total = functools.reduce(jnp.add, weights)
+    logsum[me] = top + jnp.log(total)
+    size = width // HEADS
+    spread = (
+        lax.broadcasted_iota(jnp.int32, (128, width), 1) // size
+        == lax.broadcasted_iota(jnp.int32, (128, width), 0)
+    ).astype(wide)
+    scaled = jnp.concatenate([w / total for w in weights], 0)
+    scaled = lax.dot_general(
+        scaled, spread, (((1,), (0,)), ((), ())), precision=lax.Precision.HIGHEST, preferred_element_type=wide
+    )
+    rows = tops[0].shape[0]
+    result = scaled[:rows] * terms[me].astype(wide)
+    for place, mask in enumerate(PEERS):
+        remote(terms.at[0], came.at[mask], send.at[mask], recv.at[mask], me ^ mask).wait_recv()
+        result = result + scaled[(place + 1) * rows : (place + 2) * rows] * came[mask].astype(wide)
+    out[me] = result.astype(low)
+    for mask in PEERS:
+        for ref, s, r in ((out, back, recv_back), (logsum, back_st, recv_back_st)):
+            copy = remote(ref.at[me], ref.at[me], s.at[mask], r.at[mask], me ^ mask)
+            copy.start()
+            started.append(copy)
+    for mask in PEERS:
+        for ref, s, r in ((out, back, recv_back), (logsum, back_st, recv_back_st)):
+            remote(ref.at[me], ref.at[me ^ mask], s.at[mask], r.at[mask], me ^ mask).wait_recv()
+    for copy in started:
+        copy.wait_send()
+
+
+def merge_parts(terms, tops, sums):
+    count, width = terms.shape
+    rows = count // 8
+    stats = jnp.stack([tops.reshape(8, rows, 128), sums.reshape(8, rows, 128)], 1)
+    out, logsum = pl.pallas_call(
+        merge_parts_kernel,
+        out_shape=(
+            jax.ShapeDtypeStruct((8, rows, width), low),
+            jax.ShapeDtypeStruct((8, rows, 128), wide),
+        ),
+        in_specs=[vmem_spec()] * 2,
+        out_specs=(vmem_spec(), vmem_spec()),
+        scratch_shapes=[pltpu.VMEM((8, rows, width), low), pltpu.VMEM((8, 2, rows, 128), wide)]
+        + [pltpu.SemaphoreType.DMA((8,))] * 8,
+        compiler_params=params(5),
+    )(terms.reshape(8, rows, width), stats)
+    return out.reshape(count, width), logsum.reshape(count, 128)
+
+
+def scatter_rows_kernel(terms, grads, out, out_grads, sib, pair, came, send, recv, send_pair, recv_pair, send_grad, recv_grad, keep):
+    me = lax.axis_index("seq")
+    mine = me // 4
+    core = me % 2
+    greet(PEERS)
+    local = pltpu.make_async_copy(grads.at[me], out_grads.at[me], keep)
+    local.start()
+    started = []
+    chips = (6, 2, 4, 0)
+    for slot, mask in enumerate(chips):
+        copy = remote(terms.at[me ^ 1 ^ mask], sib.at[slot], send.at[slot], recv.at[slot], me ^ 1)
+        copy.start()
+        started.append(copy)
+    for slot, mask in enumerate(chips):
+        remote(terms.at[0], sib.at[slot], send.at[slot], recv.at[slot], me ^ 1).wait_recv()
+        if mask:
+            pair[slot] = (terms[me ^ mask].astype(wide) + sib[slot].astype(wide)).astype(low)
+            copy = remote(pair.at[slot], came.at[slot], send_pair.at[slot], recv_pair.at[slot], me ^ mask)
+            copy.start()
+            started.append(copy)
+    for mask in PEERS:
+        copy = remote(grads.at[me ^ mask], out_grads.at[me], send_grad.at[mask], recv_grad.at[mask], me ^ mask)
+        copy.start()
+        started.append(copy)
+    for slot, mask in enumerate(chips[:3]):
+        remote(pair.at[0], came.at[slot], send_pair.at[slot], recv_pair.at[slot], me ^ mask).wait_recv()
+    out[mine] = terms[me].astype(wide) + sib[3].astype(wide) + came[1].astype(wide)
+    out[1 - mine] = came[2].astype(wide) + came[0].astype(wide)
+    for mask in PEERS:
+        remote(grads.at[0], out_grads.at[me ^ mask], send_grad.at[mask], recv_grad.at[mask], me ^ mask).wait_recv()
+    for copy in started:
+        copy.wait_send()
+    local.wait()
+
+
+def scatter_rows(terms, grads):
+    _, rows, width = terms.shape
+    return pl.pallas_call(
+        scatter_rows_kernel,
+        out_shape=(
+            jax.ShapeDtypeStruct((2, rows, width), wide),
+            jax.ShapeDtypeStruct(grads.shape, low),
+        ),
+        in_specs=[vmem_spec(), any_spec()],
+        out_specs=(vmem_spec(), any_spec()),
+        scratch_shapes=[
+            pltpu.VMEM((4, rows, width), low),
+            pltpu.VMEM((3, rows, width), low),
+            pltpu.VMEM((3, rows, width), low),
+            pltpu.SemaphoreType.DMA((4,)),
+            pltpu.SemaphoreType.DMA((4,)),
+            pltpu.SemaphoreType.DMA((3,)),
+            pltpu.SemaphoreType.DMA((3,)),
+            pltpu.SemaphoreType.DMA((8,)),
+            pltpu.SemaphoreType.DMA((8,)),
+            pltpu.SemaphoreType.DMA,
+        ],
+        compiler_params=params(6),
+    )(terms, grads)
+
+
+def plain(**more):
+    return pltpu.CompilerParams(vmem_limit_bytes=VMEM_BYTES, **more)
+
+
+def flash_forward_kernel(length, queries, keys, values, context, logsum):
+    rows, width = queries.shape
+    count = keys.shape[0]
+    heads = width // 64
+    of_head = lane_head((1, width), 64)
+    q = queries[...] * jnp.asarray(0.125, low)
+    k = keys[...]
+    v = values[...]
+    total = jnp.zeros((rows, width), wide)
+    logs = jnp.zeros((rows, 128), wide)
+    lanes = lax.broadcasted_iota(jnp.int32, (1, 128), 1)
+    fill = jnp.where(lax.broadcasted_iota(jnp.int32, (1, count), 1) < length[0], 0.0, masked_fill)
+    for head in range(heads):
+        scores = nt(jnp.where(of_head == head, q, jnp.zeros_like(q)), k) + fill
+        top = jnp.max(scores, -1, keepdims=True)
+        weights = jnp.exp(scores - top)
+        summed = jnp.sum(weights, -1, keepdims=True)
+        probs = (weights * (1.0 / summed)).astype(low)
+        part = nn(probs, v)
+        total = jnp.where(of_head == head, part, total)
+        logs = jnp.where(lanes == head, top + jnp.log(summed), logs)
+    context[...] = total.astype(low)
+    logsum[...] = logs
+
+
+def flash_forward(length, queries, keys, values, block):
+    count, width = queries.shape
+    return pl.pallas_call(
+        flash_forward_kernel,
+        out_shape=(
+            jax.ShapeDtypeStruct((count, width), low),
+            jax.ShapeDtypeStruct((count, 128), wide),
+        ),
+        grid_spec=pltpu.PrefetchScalarGridSpec(
+            num_scalar_prefetch=1,
+            grid=(count // block,),
+            in_specs=[
+                pl.BlockSpec((block, width), lambda i, n: (i, 0)),
+                pl.BlockSpec((count, width), lambda i, n: (0, 0)),
+                pl.BlockSpec((count, width), lambda i, n: (0, 0)),
+            ],
+            out_specs=[
+                pl.BlockSpec((block, width), lambda i, n: (i, 0)),
+                pl.BlockSpec((block, 128), lambda i, n: (i, 0)),
+            ],
+        ),
+        compiler_params=plain(),
+        cost_estimate=pl.CostEstimate(
+            flops=16 * count * count * width, bytes_accessed=8 * count * width, transcendentals=0
+        ),
+    )(length, queries, keys, values)
+
+
+def flash_backward_kernel(chunk, length, queries, grads, logsum, delta, keys, keys_t, values, dq_t, dk, dv, q_stack, g_stack, p_stack, s_stack, k_sum, v_sum):
+    step = pl.program_id(0)
+    rows, width = queries.shape
+    count = keys.shape[0]
+    heads = width // 64
+    of_head = lane_head((1, width), 64)
+
+    @pl.when(step == 0)
+    def _():
+        k_sum[...] = jnp.zeros_like(k_sum)
+        v_sum[...] = jnp.zeros_like(v_sum)
+
+    q = queries[...] * jnp.asarray(0.125, low)
+    g = grads[...]
+    for head in range(heads):
+        place = pl.ds(head * rows, rows)
+        q_stack[place] = jnp.where(of_head == head, q, jnp.zeros_like(q))
+        g_stack[place] = jnp.where(of_head == head, g, jnp.zeros_like(g))
+    dq_sums = [jnp.zeros((64, rows), wide)] * heads
+    for start in range(0, count, chunk):
+        part = pl.ds(start, chunk)
+        k = keys[part]
+        v = values[part]
+        allowed = start + lax.broadcasted_iota(jnp.int32, (chunk, 1), 0) < length[0]
+        fill = jnp.where(allowed, 0.0, masked_fill)
+        for head in range(heads):
+            place = pl.ds(head * rows, rows)
+            scores = nt(k, q_stack[place])
+            probs = jnp.exp(scores - logsum[head : head + 1, :] + fill)
+            p_stack[:, place] = probs.astype(low)
+            d_probs = nt(v, g_stack[place])
+            d_scores = (probs * (d_probs - delta[head : head + 1, :])).astype(low)
+            s_stack[:, place] = d_scores
+            dq_sums[head] = dq_sums[head] + nn(keys_t[head * 64 : head * 64 + 64, part], d_scores)
+        v_sum[part] += nn(p_stack[...], g_stack[...])
+        k_sum[part] += nn(s_stack[...], q_stack[...])
+    for head in range(heads):
+        dq_t[head * 64 : head * 64 + 64, :] = (dq_sums[head] * 0.125).astype(low)
+
+    @pl.when(step == pl.num_programs(0) - 1)
+    def _():
+        dk[...] = k_sum[...].astype(low)
+        dv[...] = v_sum[...].astype(low)
+
+
+def flash_backward(length, queries, grads, logsum, delta, keys, values, block, chunk):
+    count, width = queries.shape
+    heads = width // 64
+    return pl.pallas_call(
+        functools.partial(flash_backward_kernel, chunk),
+        out_shape=(
+            jax.ShapeDtypeStruct((width, count), low),
+            jax.ShapeDtypeStruct((count, width), low),
+            jax.ShapeDtypeStruct((count, width), low),
+        ),
+        grid_spec=pltpu.PrefetchScalarGridSpec(
+            num_scalar_prefetch=1,
+            grid=(count // block,),
+            in_specs=[
+                pl.BlockSpec((block, width), lambda i, n: (i, 0)),
+                pl.BlockSpec((block, width), lambda i, n: (i, 0)),
+                pl.BlockSpec((heads, block), lambda i, n: (0, i)),
+                pl.BlockSpec((heads, block), lambda i, n: (0, i)),
+                pl.BlockSpec((count, width), lambda i, n: (0, 0)),
+                pl.BlockSpec((width, count), lambda i, n: (0, 0)),
+                pl.BlockSpec((count, width), lambda i, n: (0, 0)),
+            ],
+            out_specs=[
+                pl.BlockSpec((width, block), lambda i, n: (0, i)),
+                pl.BlockSpec((count, width), lambda i, n: (0, 0)),
+                pl.BlockSpec((count, width), lambda i, n: (0, 0)),
+            ],
+            scratch_shapes=[
+                pltpu.VMEM((heads * block, width), low),
+                pltpu.VMEM((heads * block, width), low),
+                pltpu.VMEM((chunk, heads * block), low),
+                pltpu.VMEM((chunk, heads * block), low),
+                pltpu.VMEM((count, width), wide),
+                pltpu.VMEM((count, width), wide),
+            ],
+        ),
+        compiler_params=plain(),
+        cost_estimate=pl.CostEstimate(
+            flops=40 * count * count * width, bytes_accessed=14 * count * width, transcendentals=0
+        ),
+    )(length, queries, grads, logsum, delta, keys, keys.T, values)
+
+
+def small_forward_kernel(causal, length, queries, keys, values, context, tops, sums):
+    table = pl.program_id(0)
+    rows, width = queries.shape
+    count = keys.shape[0]
+    half = lane_head((1, 128), 64)
+    lanes = lax.broadcasted_iota(jnp.int32, (1, 128), 1)
+    allowed = lax.broadcasted_iota(jnp.int32, (rows, count), 1) < length[table]
+    if causal:
+        allowed = allowed & (
+            lax.broadcasted_iota(jnp.int32, (rows, count), 1)
+            <= lax.broadcasted_iota(jnp.int32, (rows, count), 0)
+        )
+    top_all = jnp.zeros((rows, 128), wide)
+    sum_all = jnp.ones((rows, 128), wide)
+    for two in range(width // 128):
+        place = pl.ds(two * 128, 128)
+        q = queries[:, place] * jnp.asarray(0.125, low)
+        k = keys[:, place]
+        v = values[:, place]
+        total = jnp.zeros((rows, 128), wide)
+        for side in range(2):
+            scores = nt(jnp.where(half == side, q, jnp.zeros_like(q)), k)
+            scores = jnp.where(allowed, scores, masked_fill)
+            top = jnp.max(scores, -1, keepdims=True)
+            weights = jnp.exp(scores - top)
+            summed = jnp.sum(weights, -1, keepdims=True)
+            probs = (weights * (1.0 / summed)).astype(low)
+            total = jnp.where(half == side, nn(probs, v), total)
+            top_all = jnp.where(lanes == 2 * two + side, top, top_all)
+            sum_all = jnp.where(lanes == 2 * two + side, summed, sum_all)
+        context[:, place] = total.astype(low)
+    tops[...] = top_all
+    sums[...] = sum_all
+
+
+def small_forward(length, queries, keys, values, causal):
+    tables = length.shape[0]
+    rows, width = queries.shape[0] // tables, queries.shape[1]
+    count = keys.shape[0] // tables
+
+    def block(size, last):
+        return pl.BlockSpec((size, last), lambda t, n: (t, 0))
+
+    return pl.pallas_call(
+        functools.partial(small_forward_kernel, causal),
+        out_shape=(
+            jax.ShapeDtypeStruct(queries.shape, low),
+            jax.ShapeDtypeStruct((queries.shape[0], 128), wide),
+            jax.ShapeDtypeStruct((queries.shape[0], 128), wide),
+        ),
+        grid_spec=pltpu.PrefetchScalarGridSpec(
+            num_scalar_prefetch=1,
+            grid=(tables,),
+            in_specs=[block(rows, width), block(count, width), block(count, width)],
+            out_specs=[block(rows, width), block(rows, 128), block(rows, 128)],
+        ),
+        compiler_params=plain(),
+        cost_estimate=pl.CostEstimate(
+            flops=16 * tables * rows * count * width, bytes_accessed=6 * tables * count * width, transcendentals=0
+        ),
+    )(length, queries, keys, values)
+
+
+def small_backward_kernel(causal, length, queries, keys, values, grads, context, logsum, dq, dk, dv):
+    table = pl.program_id(0)
+    rows, width = queries.shape
+    count = keys.shape[0]
+    half = lane_head((1, 128), 64)
+    allowed = lax.broadcasted_iota(jnp.int32, (rows, count), 1) < length[table]
+    if causal:
+        allowed = allowed & (
+            lax.broadcasted_iota(jnp.int32, (rows, count), 1)
+            <= lax.broadcasted_iota(jnp.int32, (rows, count), 0)
+        )
+    logs = logsum[...]
+    for two in range(width // 128):
+        place = pl.ds(two * 128, 128)
+        q = queries[:, place] * jnp.asarray(0.125, low)
+        k = keys[:, place]
+        v = values[:, place]
+        g = grads[:, place]
+        both = g.astype(wide) * context[:, place].astype(wide)
+        dq_here = jnp.zeros((rows, 128), wide)
+        dk_here = jnp.zeros((count, 128), wide)
+        dv_here = jnp.zeros((count, 128), wide)
+        for side in range(2):
+            head = 2 * two + side
+            q_one = jnp.where(half == side, q, jnp.zeros_like(q))
+            g_one = jnp.where(half == side, g, jnp.zeros_like(g))
+            delta = jnp.sum(jnp.where(half == side, both, 0.0), -1, keepdims=True)
+            scores = nt(q_one, k)
+            probs = jnp.where(allowed, jnp.exp(scores - logs[:, head : head + 1]), 0.0)
+            d_probs = nt(g_one, v)
+            d_scores = (probs * (d_probs - delta)).astype(low)
+            dq_here = jnp.where(half == side, nn(d_scores, k), dq_here)
+            dk_here = dk_here + tn(d_scores, q_one)
+            dv_here = dv_here + tn(probs.astype(low), g_one)
+        dq[:, place] = dq_here * 0.125
+        dk[:, place] = dk_here.astype(low)
+        dv[:, place] = dv_here.astype(low)
+
+
+def small_backward(length, queries, keys, values, grads, context, logsum, causal):
+    tables = length.shape[0]
+    rows, width = queries.shape[0] // tables, queries.shape[1]
+    count = keys.shape[0] // tables
+
+    def block(size, last):
+        return pl.BlockSpec((size, last), lambda t, n: (t, 0))
+
+    return pl.pallas_call(
+        functools.partial(small_backward_kernel, causal),
+        out_shape=(
+            jax.ShapeDtypeStruct(queries.shape, wide),
+            jax.ShapeDtypeStruct(keys.shape, low),
+            jax.ShapeDtypeStruct(keys.shape, low),
+        ),
+        grid_spec=pltpu.PrefetchScalarGridSpec(
+            num_scalar_prefetch=1,
+            grid=(tables,),
+            in_specs=[
+                block(rows, width),
+                block(count, width),
+                block(count, width),
+                block(rows, width),
+                block(rows, width),
+                block(rows, 128),
+            ],
+            out_specs=[block(rows, width), block(count, width), block(count, width)],
+        ),
+        compiler_params=plain(),
+        cost_estimate=pl.CostEstimate(
+            flops=40 * tables * rows * count * width, bytes_accessed=10 * tables * count * width, transcendentals=0
+        ),
+    )(length, queries, keys, values, grads, context, logsum)
+
+
+def gelu_parts(values):
+    bell = 0.5 * (1.0 + lax.erf(values * 0.7071067811865476))
+    slope = bell + values * (0.3989422804014327 * jnp.exp(-0.5 * values * values))
+    return values * bell, slope
+
+
+def feed_forward_kernel(rows, expand, contract, out, acts, slopes):
+    act, slope = gelu_parts(nn(rows[...], expand[0]))
+    act = act.astype(low)
+    acts[0] = act
+    slopes[0] = slope.astype(low)
+    term = nn(act, contract[0])
+
+    @pl.when(pl.program_id(0) == 0)
+    def _():
+        out[...] = term
+
+    @pl.when(pl.program_id(0) > 0)
+    def _():
+        out[...] += term
+
+
+def feed_forward(rows, expand, contract):
+    count, width = rows.shape
+    parts, _, hidden = expand.shape
+    return pl.pallas_call(
+        feed_forward_kernel,
+        out_shape=(
+            jax.ShapeDtypeStruct((count, width), wide),
+            jax.ShapeDtypeStruct((parts, count, hidden), low),
+            jax.ShapeDtypeStruct((parts, count, hidden), low),
+        ),
+        grid=(parts,),
+        in_specs=[
+            pl.BlockSpec((count, width), lambda j: (0, 0)),
+            pl.BlockSpec((1, width, hidden), lambda j: (j, 0, 0)),
+            pl.BlockSpec((1, hidden, width), lambda j: (j, 0, 0)),
+        ],
+        out_specs=[
+            pl.BlockSpec((count, width), lambda j: (0, 0)),
+            pl.BlockSpec((1, count, hidden), lambda j: (j, 0, 0)),
+            pl.BlockSpec((1, count, hidden), lambda j: (j, 0, 0)),
+        ],
+        compiler_params=plain(),
+        cost_estimate=pl.CostEstimate(
+            flops=4 * count * width * hidden * parts, bytes_accessed=4 * width * hidden * parts, transcendentals=0
+        ),
+    )(rows, expand, contract)
+
+
+def feed_backward_kernel(rows_t, grads, acts, slopes, expand, contract, out, d_expand, d_contract):
+    g = grads[...]
+    act = acts[0]
+    d_hidden = (nt(g, contract[0]) * slopes[0].astype(wide)).astype(low)
+    d_contract[0] = tn(act, g).astype(low)
+    d_expand[0] = nn(rows_t[...], d_hidden).astype(low)
+    term = nt(d_hidden, expand[0])
+
+    @pl.when(pl.program_id(0) == 0)
+    def _():
+        out[...] = term
+
+    @pl.when(pl.program_id(0) > 0)
+    def _():
+        out[...] += term
+
+
+def feed_backward(rows, grads, acts, slopes, expand, contract):
+    count, width = rows.shape
+    parts, _, hidden = expand.shape
+    return pl.pallas_call(
+        feed_backward_kernel,
+        out_shape=(
+            jax.ShapeDtypeStruct((count, width), wide),
+            jax.ShapeDtypeStruct((parts, width, hidden), low),
+            jax.ShapeDtypeStruct((parts, hidden, width), low),
+        ),
+        grid=(parts,),
+        in_specs=[
+            pl.BlockSpec((width, count), lambda j: (0, 0)),
+            pl.BlockSpec((count, width), lambda j: (0, 0)),
+            pl.BlockSpec((1, count, hidden), lambda j: (j, 0, 0)),
+            pl.BlockSpec((1, count, hidden), lambda j: (j, 0, 0)),
+            pl.BlockSpec((1, width, hidden), lambda j: (j, 0, 0)),
+            pl.BlockSpec((1, hidden, width), lambda j: (j, 0, 0)),
+        ],
+        out_specs=[
+            pl.BlockSpec((count, width), lambda j: (0, 0)),
+            pl.BlockSpec((1, width, hidden), lambda j: (j, 0, 0)),
+            pl.BlockSpec((1, hidden, width), lambda j: (j, 0, 0)),
+        ],
+        compiler_params=plain(),
+        cost_estimate=pl.CostEstimate(
+            flops=8 * count * width * hidden * parts, bytes_accessed=10 * width * hidden * parts, transcendentals=0
+        ),
+    )(rows.T, grads, acts, slopes, expand, contract)
+
+
+def plane_body(
+    source_tokens,
+    target_tokens,
+    source_lengths,
+    target_lengths,
+    encoder_query,
+    encoder_key,
+    encoder_value,
+    encoder_mix,
+    attend_gain,
+    attend_shift,
+    encoder_expand,
+    encoder_contract,
+    encoder_gain,
+    encoder_shift,
+    decoder_query,
+    decoder_key,
+    decoder_value,
+    decoder_mix,
+    self_gain,
+    self_shift,
+    cross_query,
+    cross_key,
+    cross_value,
+    cross_mix,
+    cross_gain,
+    cross_shift,
+    decoder_expand,
+    decoder_contract,
+    decoder_gain,
+    decoder_shift,
+    source_cotangent,
+    target_cotangent,
+):
+    slots, tables, width = source_tokens.shape
+    places = target_tokens.shape[0]
+    me = lax.axis_index("seq")
+    quarter = width // 4
+    slice_rows = width // 8
+
+    def flat(array):
+        return jnp.swapaxes(array, 0, 1).reshape(-1, width)
+
+    def unflat(array):
+        return jnp.swapaxes(array.reshape(tables, -1, width), 0, 1)
+
+    def columns(weight):
+        return lax.dynamic_slice_in_dim(weight, (me % 4) * quarter, quarter, 1)
+
+    def own(rows):
+        return lax.dynamic_slice_in_dim(rows, me * slice_rows, slice_rows, 1)
+
+    def own_places(rows):
+        return lax.dynamic_slice_in_dim(rows.reshape(tables, 8 * places, width), me * places, places, 1)
+
+    def own_vector(vector):
+        return lax.dynamic_slice_in_dim(vector, me * slice_rows, slice_rows, 0)
+
+    source_flat = flat(source_tokens)
+    target_all = lax.all_gather(
+        jnp.stack([jnp.swapaxes(target_tokens, 0, 1), jnp.swapaxes(target_cotangent, 0, 1)], 0), "seq", axis=2, tiled=True
+    )
+    target_flat = target_all[0].reshape(-1, width)
+    target_grad = target_all[1].reshape(-1, width)
+    all_expand = lax.all_gather(encoder_expand, "seq", axis=0)
+    all_contract = lax.all_gather(encoder_contract, "seq", axis=0)
+
+    rows = gather_table(source_flat.reshape(tables, slots, width))
+    rows = rows.reshape(-1, width)
+    w_query, w_key, w_value = columns(encoder_query), columns(encoder_key), columns(encoder_value)
+    length = lax.dynamic_slice_in_dim(source_lengths, me // 4, 1, 0)
+    queries = project(rows, w_query).astype(low)
+    keys = project(rows, w_key).astype(low)
+    values = project(rows, w_value).astype(low)
+    context, logsum = flash_forward(length, queries, keys, values, 256)
+    encoder_context = heads_to_rows(context.reshape(8, slots, quarter)).reshape(-1, width)
+    first, first_back = jax.vjp(
+        layer_norm, source_flat.astype(wide) + project(encoder_context, encoder_mix), attend_gain, attend_shift
+    )
+    first_low = first.astype(low)
+    widened, acts, slopes = feed_forward(first_low, all_expand, all_contract)
+    second, second_back = jax.vjp(layer_norm, first + widened, encoder_gain, encoder_shift)
+    encoded = second.astype(low)
+
+    self_queries = project(target_flat, decoder_query).astype(low)
+    self_keys = project(target_flat, decoder_key).astype(low)
+    self_values = project(target_flat, decoder_value).astype(low)
+    decoder_context, self_tops, self_sums = small_forward(
+        target_lengths, self_queries, self_keys, self_values, True
+    )
+    self_logs = self_tops + jnp.log(self_sums)
+    third, third_back = jax.vjp(
+        layer_norm, target_flat.astype(wide) + project(decoder_context, decoder_mix), self_gain, self_shift
+    )
+    third_low = third.astype(low)
+    cross_queries = project(third_low, cross_query).astype(low)
+
+    cross_keys = project(encoded, cross_key).astype(low)
+    cross_values = project(encoded, cross_value).astype(low)
+    here = source_lengths - me * slots
+    part, part_tops, part_sums = small_forward(here, cross_queries, cross_keys, cross_values, False)
+    cross_context, cross_logs = merge_parts(part, part_tops, part_sums)
+    fourth, fourth_back = jax.vjp(
+        layer_norm, third + project(cross_context, cross_mix), cross_gain, cross_shift
+    )
+    fourth_low = fourth.astype(low)
+    hidden = project(fourth_low, decoder_expand)
+    decoder_acts, gelu_back = jax.vjp(gelu_exact, hidden)
+    decoder_acts = decoder_acts.astype(low)
+    narrowed = sum_small(project(decoder_acts, decoder_contract)).astype(wide)
+    fifth, fifth_back = jax.vjp(layer_norm, fourth + narrowed, decoder_gain, decoder_shift)
+    decoded = jnp.swapaxes(own_places(fifth.astype(low)), 0, 1)
+
+    d_fifth, grad_decoder_gain, grad_decoder_shift = fifth_back(target_grad.astype(wide))
+    fifth_low = d_fifth.astype(low)
+    d_hidden = gelu_back(project_back(fifth_low, decoder_contract))[0].astype(low)
+    grad_decoder_expand = outer_sum(fourth_low, d_hidden)
+    grad_decoder_contract = outer_sum(decoder_acts, fifth_low)
+    d_rows = sum_small(project_back(d_hidden, decoder_expand)).astype(wide)
+    d_fourth, grad_cross_gain, grad_cross_shift = fourth_back(d_fifth + d_rows)
+    cross_low = d_fourth.astype(low)
+    grad_cross_mix = outer_sum(own(cross_context), cross_low)
+    d_cross = project_back(cross_low, cross_mix).astype(low)
+    dq_part, dk_cross, dv_cross = small_backward(
+        here, cross_queries, cross_keys, cross_values, d_cross, cross_context, cross_logs, False
+    )
+    d_encoded = project_back(dk_cross, cross_key) + project_back(dv_cross, cross_value)
+    cross_pair = outer_sum(encoded, jnp.concatenate([dk_cross, dv_cross], 1)).astype(low)
+    cross_pair = lax.psum_scatter(cross_pair, "seq", scatter_dimension=0, tiled=True)
+
+    d_second, grad_encoder_gain, grad_encoder_shift = second_back(flat(source_cotangent).astype(wide) + d_encoded)
+    d_rows, d_expand, d_contract = feed_backward(
+        first_low, d_second.astype(low), acts, slopes, all_expand, all_contract
+    )
+    d_expand = lax.psum_scatter(d_expand, "seq", scatter_dimension=0, tiled=False)
+    d_contract = lax.psum_scatter(d_contract, "seq", scatter_dimension=0, tiled=False)
+    d_first, grad_attend_gain, grad_attend_shift = first_back(d_second + d_rows)
+    encoder_low = d_first.astype(low)
+    encoder_mix_part = outer_sum(encoder_context, encoder_low).astype(low)
+    encoder_mix_part = lax.psum_scatter(encoder_mix_part, "seq", scatter_dimension=0, tiled=True)
+    d_context = rows_to_heads(project_back(encoder_low, encoder_mix).astype(low).reshape(tables, slots, width))
+    d_context = d_context.reshape(-1, quarter)
+    delta = jnp.sum(
+        (d_context.astype(wide) * context.astype(wide)).reshape(-1, quarter // 64, 64), -1
+    )
+    dq_t, dk, dv = flash_backward(
+        length, queries, d_context, logsum[:, : quarter // 64].T, delta.T, keys, values, 256, 512
+    )
+    term = (
+        lax.dot_general(dq_t, w_query, (((0,), (1,)), ((), ())), preferred_element_type=wide)
+        + project_back(dk, w_key)
+        + project_back(dv, w_value)
+    ).astype(low)
+    weight_terms = jnp.concatenate(
+        [
+            lax.dot_general(rows, dq_t, (((0,), (1,)), ((), ())), preferred_element_type=wide).astype(low),
+            outer_sum(rows, dk).astype(low),
+            outer_sum(rows, dv).astype(low),
+        ],
+        1,
+    )
+    vectors = jnp.stack(
+        [grad_attend_gain, grad_attend_shift, grad_encoder_gain, grad_encoder_shift], 0
+    ).astype(low)
+    vectors = jnp.swapaxes(vectors.reshape(4, 8, slice_rows), 0, 1)
+    vectors = jnp.pad(vectors, ((0, 0), (0, 12), (0, 3 * quarter - slice_rows)))
+    grads = jnp.concatenate([weight_terms.reshape(8, slice_rows, 3 * quarter), vectors], 1)
+    d_source, came = scatter_rows(term.reshape(8, slots, width), grads)
+    came = jnp.sum(came.reshape(2, 4, slice_rows + 16, 3 * quarter).astype(wide), 0)
+    grad_source = unflat(d_first + d_source.reshape(-1, width))
+    encoder_three = jnp.moveaxis(came[:, :slice_rows].reshape(4, slice_rows, 3, quarter), (2, 1), (0, 1))
+    encoder_three = encoder_three.reshape(3, slice_rows, width)
+    encoder_vectors = jnp.sum(came[:, slice_rows : slice_rows + 4, :slice_rows], 0)
+
+    dq_cross = sum_small(dq_part)
+    grad_cross_query = outer_sum(own(third_low), dq_cross)
+    d_third, grad_self_gain, grad_self_shift = third_back(d_fourth + project_back(dq_cross, cross_query))
+    self_low = d_third.astype(low)
+    grad_decoder_mix = outer_sum(own(decoder_context), self_low)
+    dq_self, dk_self, dv_self = small_backward(
+        target_lengths,
+        self_queries,
+        self_keys,
+        self_values,
+        project_back(self_low, decoder_mix).astype(low),
+        decoder_context,
+        self_logs,
+        True,
+    )
+    dq_self = dq_self.astype(low)
+    target_own = own(target_flat)
+    grad_decoder_query = outer_sum(target_own, dq_self)
+    grad_decoder_key = outer_sum(target_own, dk_self)
+    grad_decoder_value = outer_sum(target_own, dv_self)
+    grad_target = own_places(
+        d_third
+        + project_back(dq_self, decoder_query)
+        + project_back(dk_self, decoder_key)
+        + project_back(dv_self, decoder_value)
+    )
+    grad_target = jnp.swapaxes(grad_target, 0, 1)
+
+    def over_tables(*arrays):
+        return [a.astype(wide) for a in lax.psum([a.astype(low) for a in arrays], "dp")]
+
+    decoder_vectors = jnp.stack(
+        [
+            own_vector(v)
+            for v in (
+                grad_self_gain,
+                grad_self_shift,
+                grad_cross_gain,
+                grad_cross_shift,
+                grad_decoder_gain,
+                grad_decoder_shift,
+            )
+        ],
+        0,
+    )
+    (
+        grad_decoder_query,
+        grad_decoder_key,
+        grad_decoder_value,
+        grad_decoder_mix,
+        grad_cross_query,
+        grad_cross_mix,
+        grad_decoder_expand,
+        grad_decoder_contract,
+        decoder_vectors,
+    ) = over_tables(
+        grad_decoder_query,
+        grad_decoder_key,
+        grad_decoder_value,
+        grad_decoder_mix,
+        grad_cross_query,
+        grad_cross_mix,
+        grad_decoder_expand,
+        grad_decoder_contract,
+        decoder_vectors,
+    )
+    cross_pair, d_expand, d_contract, encoder_mix_part, decoder_vectors = lax.optimization_barrier(
+        (cross_pair, d_expand, d_contract, encoder_mix_part, decoder_vectors)
+    )
+    cross_pair, d_expand, d_contract, encoder_mix_part = over_tables(
+        cross_pair, d_expand, d_contract, encoder_mix_part
+    )
+    encoder_three, encoder_vectors, encoder_mix_part = lax.optimization_barrier(
+        (encoder_three, encoder_vectors, encoder_mix_part)
+    )
+    encoder_three, encoder_vectors = over_tables(encoder_three, encoder_vectors)
+    return (
+        unflat(encoded),
+        decoded,
+        grad_source,
+        grad_target,
+        encoder_three[0],
+        encoder_three[1],
+        encoder_three[2],
+        encoder_mix_part,
+        encoder_vectors[0],
+        encoder_vectors[1],
+        d_expand,
+        d_contract,
+        encoder_vectors[2],
+        encoder_vectors[3],
+        grad_decoder_query,
+        grad_decoder_key,
+        grad_decoder_value,
+        grad_decoder_mix,
+        decoder_vectors[0],
+        decoder_vectors[1],
+        grad_cross_query,
+        cross_pair[:, :width],
+        cross_pair[:, width:],
+        grad_cross_mix,
+        decoder_vectors[2],
+        decoder_vectors[3],
+        grad_decoder_expand,
+        grad_decoder_contract,
+        decoder_vectors[4],
+        decoder_vectors[5],
+    )
+
+
 def solution(mesh):
+    body = plane_body if fits_plane(mesh) else general_body
     in_specs = (
         P("seq", "dp", None),
         P("seq", "dp", None),

time: 2160 us -> 939 us (0.43)
  waiting for transfers between devices: 1190 us -> 279 us
  Pallas kernels: 0 us -> 386 us
  matrix products: 469 us -> 96.4 us
  local copies, waits for them, and re-layouts: 254 us -> 57.1 us
  other arithmetic: 118 us -> 64.9 us
  blocking collectives: 79.1 us -> 33 us
  loops' own time: 24.5 us -> 0 us
    reduce_scatter x13 -> x4, waiting for transfers between devices: 530 us -> 23.7 us  [the longest x1 23.7 us: plane_body(): lax.psum_scatter(d_contract, 'seq', scatter_dimension=0, tiled=False)]
    pallas_call x0 -> x16, Pallas kernels: none -> 386 us  [the longest x3 60.8 us: sum_small(): pl.pallas_call(sum_small_kernel, out_shape=jax.ShapeDtypeStruct(blocks, l...]
    dot_general x42 -> x2, matrix products: 279 us -> 6.56 us  [the longest x1 4.08 us: plane_body(): lax.dot_general(rows, dq_t, (((0,), (1,)), ((), ())), preferred_element_t...]
    all_gather x6 -> x3, waiting for transfers between devices: 272 us -> 6.82 us  [the longest x1 6.82 us: plane_body(): all_contract = lax.all_gather(encoder_contract, 'seq', axis=0)]
    unnamed x32 -> x9, waiting for transfers between devices: 192 us -> 2 us
    dynamic_slice x66 -> x6, local copies, waits for them, and re-layouts: 114 us -> 3.05 us  [the longest x3 1.6 us: own_vector(): return lax.dynamic_slice_in_dim(vector, me * slice_rows, slice_rows, 0)]
    psum x1 -> x2, waiting for transfers between devices: 192 us -> 247 us  [over_tables(): lax.psum([a.astype(low) for a in arrays], 'dp')]
    all_gather x4 -> x0, blocking collectives: 42.2 us -> none  [the longest x2 20 us: gather_rows(): return lax.all_gather(rows, 'seq', axis=0, tiled=True)]
  transfers between devices with their start and end apart: 26 -> 9, of which waited for: 23 -> 4; matrix products, arithmetic and copies ran while one was open for 22% -> 15% of each run, Pallas kernels for 0% -> 28%
where the time goes in v1:
time: 939 us; the launch traced here: 933 us
  Pallas kernels  386 us (41%)
  waiting for transfers between devices  279 us (30%)
  matrix products  96.4 us (10%)
  other arithmetic  64.9 us (7%)
  local copies, waits for them, and re-layouts  57.1 us (6%)
  blocking collectives  33 us (4%)
  between operations  15.5 us (2%)
    psum x2, waiting for transfers between devices, over_tables(): lax.psum([a.astype(low) for a in arrays], 'dp')  247 us
    pallas_call x3, Pallas kernels, sum_small(): pl.pallas_call(sum_small_kernel, out_shape=jax.ShapeDtypeStruct(blocks, l...  60.8 us
    pallas_call x1, Pallas kernels, flash_backward(): pl.pallas_call(functools.partial(flash_backward_kernel, chunk), out_shape...  58.5 us
    pallas_call x1, Pallas kernels, scatter_rows(): pl.pallas_call(scatter_rows_kernel, out_shape=(jax.ShapeDtypeStruct((2, r...  55.7 us
    pallas_call x1, Pallas kernels, flash_forward(): pl.pallas_call(flash_forward_kernel, out_shape=(jax.ShapeDtypeStruct((cou...  36.8 us
    pallas_call x1, Pallas kernels, gather_table(): pl.pallas_call(gather_table_kernel, out_shape=jax.ShapeDtypeStruct((8,) +...  34.6 us
    dot_general x14, matrix products, project(): return jnp.dot(rows, weight, preferred_element_type=jnp.float32)  34.5 us
    psum x2, blocking collectives, over_tables(): lax.psum([a.astype(low) for a in arrays], 'dp')  33 us
  transfers between devices with their start and end apart: 9, of which 4 were waited for; matrix products, arithmetic and copies ran while one was open for 15% of the time, Pallas kernels for 28%

profile of v1, /device:TPU:0, one launch (start us, length us, event | category | flops | bytes accessed | tf_op | source)
XLA Modules:
  0.0 933.1 jit_solution(9955552299540231283)
XLA Ops:
  15.9 34.6 %shard_map.535 = bf16[8,256,1024]{2,1,0:T(8,128)(2,1)} custom-call(bf16[2,256,1024]{2,1,0:T(8,128)(2,1)} %bitcast.218), custom_call_target="tpu_custom_call" | custom-call | tf_op jit(solution)/shard_map/pallas_call | solution.py:627
  50.5 3.5 convolution_convert_fusion.3.keys_t
  56.2 4.9 fusion.1.queries
  61.1 3.4 fusion.2.values
  64.4 36.8 %shard_map.536 = (bf16[2048,256]{1,0:T(8,128)(2,1)}, f32[2048,128]{1,0:T(8,128)}) custom-call(s32[1]{0:T(128)} %dynamic_slice.48.length, bf16[2048,256]{1,0:T(8,128)(2,1)} %fusion.1.queries, bf16[2048,256]{1,0:T(8,128)(2,1)} %copy.150.keys, bf16[2048,256]{1,0:T(8,128)(2,1)} %fusion.2.values), custom_call_target="tpu_custom_call" | custom-call | flops 17179869184 | bytes 4194304 | tf_op jit(solution)/shard_map/pallas_call | solution.py:911
  101.2 16.6 %shard_map.537 = bf16[2,256,1024]{2,1,0:T(8,128)(2,1)} custom-call(bf16[8,256,256]{2,1,0:T(8,128)(2,1)} %bitcast.223), custom_call_target="tpu_custom_call" | custom-call | tf_op jit(solution)/shard_map/pallas_call | solution.py:665
  117.9 3.3 fusion.71
  124.7 3.0 fusion.8.rows
  136.2 13.5 %shard_map.539 = (bf16[256,1024]{1,0:T(8,128)(2,1)}, f32[256,128]{1,0:T(8,128)}, f32[256,128]{1,0:T(8,128)}) custom-call(s32[2]{0:T(128)} %length.3, bf16[256,1024]{1,0:T(8,128)(2,1)} %convolution_convert_fusion.15.queries, bf16[256,1024]{1,0:T(8,128)(2,1)} %convolution_convert_fusion.14.keys, bf16[256,1024]{1,0:T(8,128)(2,1)} %convolution_convert_fusion.13.values), custom_call_target="tpu_custom_call" | custom-call | flops 536870912 | bytes 1572864 | tf_op jit(solution)/shard_map/pallas_call | solution.py:1068
  149.7 2.7 fusion.72
  155.8 6.8 all-gather.10.cloned.1.call-done
  162.6 17.8 %shard_map.538 = (f32[512,1024]{1,0:T(8,128)}, bf16[8,512,512]{2,1,0:T(8,128)(2,1)}, bf16[8,512,512]{2,1,0:T(8,128)(2,1)}) custom-call(bf16[512,1024]{1,0:T(8,128)(2,1)} %fusion.8.rows, bf16[8,1024,512]{2,1,0:T(8,128)(2,1)} %bitcast.261, bf16[8,512,1024]{2,1,0:T(8,128)(2,1)} %bitcast.263), custom_call_target="tpu_custom_call" | custom-call | flops 8589934592 | bytes 16777216 | tf_op jit(solution)/shard_map/pallas_call | solution.py:1187
  180.4 2.9 fusion.68
  190.2 6.0 shard_map.540
  197.9 23.7 %shard_map.541 = (bf16[8,32,1024]{2,1,0:T(8,128)(2,1)}, f32[8,32,128]{2,1,0:T(8,128)}) custom-call(bf16[8,32,1024]{2,1,0:T(8,128)(2,1)} %bitcast.246, f32[8,2,32,128]{3,2,1,0:T(8,128)} %pad_maximum_fusion.1.stats), custom_call_target="tpu_custom_call" | custom-call | tf_op jit(solution)/shard_map/pallas_call | solution.py:804
  221.7 2.7 fusion.73
  228.3 18.6 %shard_map.542 = bf16[8,32,1024]{2,1,0:T(8,128)(2,1)} custom-call(f32[8,32,1024]{2,1,0:T(8,128)} %bitcast.221), custom_call_target="tpu_custom_call" | custom-call | tf_op jit(solution)/shard_map/pallas_call | solution.py:744
  254.5 18.8 %shard_map.543 = bf16[8,32,1024]{2,1,0:T(8,128)(2,1)} custom-call(f32[8,32,1024]{2,1,0:T(8,128)} %bitcast.222), custom_call_target="tpu_custom_call" | custom-call | tf_op jit(solution)/shard_map/pallas_call | solution.py:744
  273.3 3.0 multiply_reduce_fusion.6
  279.5 11.9 %shard_map.544 = (f32[256,1024]{1,0:T(8,128)}, bf16[512,1024]{1,0:T(8,128)(2,1)}, bf16[512,1024]{1,0:T(8,128)(2,1)}) custom-call(s32[2]{0:T(128)} %broadcast_subtract_fusion.length, bf16[256,1024]{1,0:T(8,128)(2,1)} %convolution_convert_fusion.12.queries, bf16[512,1024]{1,0:T(8,128)(2,1)} %convolution_convert_fusion.9.keys, ...), custom_call_target="tpu_custom_call" | custom-call | flops 2684354560 | bytes 5242880 | tf_op jit(solution)/shard_map/pallas_call | solution.py:1135
  291.5 3.3 fusion.76
  301.0 25.7 %shard_map.545 = (f32[512,1024]{1,0:T(8,128)}, bf16[8,1024,512]{2,1,0:T(8,128)(2,1)}, bf16[8,512,1024]{2,1,0:T(8,128)(2,1)}) custom-call(bf16[1024,512]{1,0:T(8,128)(2,1)} %copy.156.rows_t, bf16[512,1024]{1,0:T(8,128)(2,1)} %add_convert_fusion.3.grads, bf16[8,512,512]{2,1,0:T(8,128)(2,1)} %get-tuple-element.75.acts, ...), custom_call_target="tpu_custom_call" | custom-call | flops 17179869184 | bytes 41943040 | tf_op jit(solution)/shard_map/pallas_call | solution.py:1232
  326.7 4.5 multiply_reduce_fusion.1
  333.3 2.7 convolution_convert_fusion.4
  336.0 6.2 convolution_convert_fusion
  342.9 2.6 copy.157
  350.1 23.4 %shard_map.549 = bf16[8,32,1024]{2,1,0:T(8,128)(2,1)} custom-call(f32[8,32,1024]{2,1,0:T(8,128)} %bitcast.239), custom_call_target="tpu_custom_call" | custom-call | tf_op jit(solution)/shard_map/pallas_call | solution.py:744
  375.2 4.0 multiply_reduce_fusion.7
  379.3 11.9 %psum.105 = bf16[6,128]{1,0:T(8,128)(2,1)S(1)} all-reduce(bf16[6,128]{1,0:T(8,128)(2,1)S(1)} %stack.52), channel_id=1, replica_groups=mesh['dp'=4,'seq'=8] {'dp'}, use_global_device_ids=true, to_apply=%region_37.38 | all-reduce | flops 768 | bytes 3072 | tf_op jit(solution)/shard_map/psum | solution.py:1463
  391.9 4.8 convolution_convert_fusion.7
  396.7 14.3 %shard_map.546 = bf16[8,256,256]{2,1,0:T(8,128)(2,1)} custom-call(bf16[2,256,1024]{2,1,0:T(8,128)(2,1)} %bitcast.244), custom_call_target="tpu_custom_call" | custom-call | tf_op jit(solution)/shard_map/pallas_call | solution.py:703
  411.0 3.1 convert_multiply_fusion
  414.1 2.9 copy.158
  419.4 58.5 %shard_map.547 = (bf16[256,2048]{1,0:T(8,128)(2,1)}, bf16[2048,256]{1,0:T(8,128)(2,1)}, bf16[2048,256]{1,0:T(8,128)(2,1)}) custom-call(s32[1]{0:T(128)} %dynamic_slice.48.length, bf16[2048,256]{1,0:T(8,128)(2,1)} %fusion.1.queries, bf16[2048,256]{1,0:T(8,128)(2,1)} %bitcast.224, f32[4,2048]{1,0:T(4,128)} %slice_bitcast_fusion.3.logsum, f32[4,2048]{1,0:T(4,128)} %bitcast.253, ...), custom_call_target="tpu_custom_call" | custom-call | flops 42949672960 | bytes 7340032 | tf_op jit(solution)/shard_map/pallas_call | solution.py:985
  477.9 4.1 fusion.9
  486.1 2.8 copy.160
  488.9 2.8 fusion.6.grads
  495.5 4.4 add_convert_fusion
  500.0 55.7 %shard_map.548 = (f32[2,256,1024]{2,1,0:T(8,128)}, bf16[8,144,768]{2,1,0:T(8,128)(2,1)}) custom-call(bf16[8,256,1024]{2,1,0:T(8,128)(2,1)} %bitcast.207, bf16[8,144,768]{2,1,0:T(8,128)(2,1)} %fusion.6.grads), custom_call_target="tpu_custom_call" | custom-call | tf_op jit(solution)/shard_map/pallas_call | solution.py:856
  560.0 10.4 %shard_map.550 = (f32[256,1024]{1,0:T(8,128)}, bf16[256,1024]{1,0:T(8,128)(2,1)}, bf16[256,1024]{1,0:T(8,128)(2,1)}) custom-call(s32[2]{0:T(128)} %length.3, bf16[256,1024]{1,0:T(8,128)(2,1)} %convolution_convert_fusion.15.queries, bf16[256,1024]{1,0:T(8,128)(2,1)} %convolution_convert_fusion.14.keys, bf16[256,1024]{1,0:T(8,128)(2,1)} %convolution_convert_fusion.13.values, ...), custom_call_target="tpu_custom_call" | custom-call | flops 1342177280 | bytes 2621440 | tf_op jit(solution)/shard_map/pallas_call | solution.py:1135
  584.5 23.7 %reduce-scatter.9.cloned.1.call-done = bf16[1,512,1024]{2,1,0:T(8,128)(2,1)} async-done(((bf16[8,512,1024]{2,1,0:T(8,128)(2,1)}), bf16[1,512,1024]{2,1,0:T(8,128)(2,1)}) %reduce-scatter.9.cloned.1.call-update) | async-done | bytes 1048592 | tf_op jit(solution)/shard_map/reduce_scatter | solution.py:1395
  618.1 27.8 %all-reduce.5.cloned.1.call-done = bf16[128,1024]{1,0:T(8,128)(2,1)} async-done(((bf16[128,1024]{1,0:T(8,128)(2,1)}), bf16[128,1024]{1,0:T(8,128)(2,1)}) %all-reduce.5.cloned.1.call-update) | async-done | bytes 262160 | tf_op jit(solution)/shard_map/psum | solution.py:1463
  647.7 3.4 copy.185
  652.7 2.5 convolution_add_fusion.2
  660.2 2.9 copy.184
  663.7 21.2 %psum.108 = bf16[4,128]{0,1:T(8,128)(2,1)S(1)} all-reduce(bf16[4,128]{0,1:T(8,128)(2,1)S(1)} %copy.175), channel_id=1, replica_groups=mesh['dp'=4,'seq'=8] {'dp'}, use_global_device_ids=true, to_apply=%region_40.41 | all-reduce | flops 512 | bytes 2048 | tf_op jit(solution)/shard_map/psum | solution.py:1463
  685.6 218.9 %all-reduce.7.cloned.1.call-done = (bf16[128,2048]{1,0:T(8,128)(2,1)}, bf16[3,128,1024]{1,2,0:T(8,128)(2,1)}, bf16[1024,512]{1,0:T(8,128)(2,1)}, bf16[512,1024]{...) async-done(((bf16[128,2048]{1,0:T(8,128)(2,1)}, ...) | async-done | bytes 7077904 | tf_op jit(solution)/shard_map/psum | solution.py:1463
  918.6 2.9 convert_element_type.299
  (359 shorter events, 131.9 us)
Async XLA Ops:
  7.2 43.3 %copy-start = (bf16[1024,1024]{1,0:T(8,128)(2,1)S(1)}, bf16[1024,1024]{1,0:T(8,128)(2,1)}, u32[]{:S(2)}) copy-start(bf16[1024,1024]{1,0:T(8,128)(2,1)} %param.37) | copy-start | bytes 6291460
  7.2 120.5 %all-gather.6.cloned.1.call-start = ((), (), s32[]{:S(2)}) async-start(), calls=%async_computation.4 | async-start | bytes 1179648 | tf_op jit(solution)/shard_map/all_gather | solution.py:1319
  9.1 4.0 copy-start.48
  9.2 146.6 %all-gather.8.cloned.1.call-start = ((), (), s32[]{:S(2)}) async-start(), calls=%async_computation.10 | async-start | bytes 9437184 | tf_op jit(solution)/shard_map/all_gather | solution.py:1324
  9.9 152.7 %all-gather.10.cloned.1.call-start = ((), (), s32[]{:S(2)}) async-start(), calls=%async_computation.11 | async-start | bytes 9437184 | tf_op jit(solution)/shard_map/all_gather | solution.py:1325
  10.6 573.9 %reduce-scatter.11.cloned.1.call-start = ((), (), s32[]{:S(2)}) async-start(), calls=%async_computation.8 | async-start | bytes 2359296 | tf_op jit(solution)/shard_map/reduce_scatter | solution.py:1399
  54.0 7.1 copy-start.59
  56.2 4.9 copy-start.22
  101.2 16.6 %copy-start.24 = (bf16[256,2,1024]{2,0,1:T(8,128)(2,1)S(1)}, bf16[256,2,1024]{2,0,1:T(8,128)(2,1)}, u32[]{:S(2)}) copy-start(bf16[256,2,1024]{2,0,1:T(8,128)(2,1)} %copy.188) | copy-start | bytes 3145732
  131.0 18.7 %copy-start.28 = (bf16[1,2,128,1024]{3,2,1,0:T(8,128)(2,1)}, bf16[1,2,128,1024]{3,2,1,0:T(8,128)(2,1)S(1)}, u32[]{:S(2)}) copy-start(bf16[1,2,128,1024]{3,2,1,0:T(8,128)(2,1)S(1)} %copy.152) | copy-start | bytes 1572868
  152.7 68.9 %copy-start.81 = (f32[256]{0:T(256)}, f32[256]{0:T(256)S(1)}, u32[]{:S(2)}) copy-start(f32[256]{0:T(256)S(1)} %fusion.52) | copy-start | bytes 3076
  224.4 52.0 %copy-start.75 = (f32[256]{0:T(256)}, f32[256]{0:T(256)S(1)}, u32[]{:S(2)}) copy-start(f32[256]{0:T(256)S(1)} %broadcast_multiply_fusion.3) | copy-start | bytes 3076
  224.7 51.7 %copy-start.77 = (f32[256]{0:T(256)}, f32[256]{0:T(256)S(1)}, u32[]{:S(2)}) copy-start(f32[256]{0:T(256)S(1)} %fusion.53) | copy-start | bytes 3076
  251.4 24.9 %copy-start.84 = (f32[256]{0:T(256)}, f32[256]{0:T(256)S(1)}, u32[]{:S(2)}) copy-start(f32[256]{0:T(256)S(1)} %negate_multiply_fusion.5) | copy-start | bytes 3076
  277.0 14.4 %copy-start.87 = (f32[256]{0:T(256)}, f32[256]{0:T(256)S(1)}, u32[]{:S(2)}) copy-start(f32[256]{0:T(256)S(1)} %negate_multiply_fusion.4) | copy-start | bytes 3076
  291.4 3.8 copy-start.30
  291.4 4.0 copy-start.52
  326.7 4.6 copy-start.2
  331.9 4.0 copy-start.96
  336.0 248.6 %reduce-scatter.5.cloned.1.call-start = ((), (), s32[]{:S(2)}) async-start(), calls=%async_computation.5 | async-start | bytes 4718592 | tf_op jit(solution)/shard_map/reduce_scatter | solution.py:1388
  342.2 242.3 %reduce-scatter.7.cloned.1.call-start = ((), (), s32[]{:S(2)}) async-start(), calls=%async_computation.6 | async-start | bytes 9437184 | tf_op jit(solution)/shard_map/reduce_scatter | solution.py:1394
  342.8 5.7 copy-start.68
  342.8 265.4 %reduce-scatter.9.cloned.1.call-start = ((), (), s32[]{:S(2)}) async-start(), calls=%async_computation.7 | async-start | bytes 9437184 | tf_op jit(solution)/shard_map/reduce_scatter | solution.py:1395
  373.6 272.3 %all-reduce.5.cloned.1.call-start = ((), (), s32[]{:S(2)}) async-start(), calls=%async_computation.9 | async-start | bytes 524288 | tf_op jit(solution)/shard_map/psum | solution.py:1463
  375.2 16.6 %copy-start.95 = (bf16[1024]{0:T(1024)(128)(2,1)S(1)}, bf16[1024]{0:T(1024)(128)(2,1)}, u32[]{:S(2)}) copy-start(bf16[1024]{0:T(1024)(128)(2,1)} %get-tuple-element.192) | copy-start | bytes 6148
  375.2 16.6 %copy-start.94 = (bf16[1024]{0:T(1024)(128)(2,1)S(1)}, bf16[1024]{0:T(1024)(128)(2,1)}, u32[]{:S(2)}) copy-start(bf16[1024]{0:T(1024)(128)(2,1)} %get-tuple-element.201) | copy-start | bytes 6148
  375.2 16.6 %copy-start.100 = (bf16[1024]{0:T(1024)(128)(2,1)S(1)}, bf16[1024]{0:T(1024)(128)(2,1)}, u32[]{:S(2)}) copy-start(bf16[1024]{0:T(1024)(128)(2,1)} %get-tuple-element.190) | copy-start | bytes 6148
  375.2 16.6 %copy-start.99 = (bf16[1024]{0:T(1024)(128)(2,1)S(1)}, bf16[1024]{0:T(1024)(128)(2,1)}, u32[]{:S(2)}) copy-start(bf16[1024]{0:T(1024)(128)(2,1)} %get-tuple-element.200) | copy-start | bytes 6148
  375.2 16.7 %copy-start.97 = (f32[512]{0:T(512)S(1)}, f32[512]{0:T(512)}, u32[]{:S(2)}) copy-start(f32[512]{0:T(512)} %copy-done.96) | copy-start | bytes 6148
  477.8 4.1 copy-start.23
  477.9 4.3 copy-start.44
  500.0 55.7 %copy-start.91 = (f32[256]{0:T(256)S(1)}, f32[256]{0:T(256)}, u32[]{:S(2)}) copy-start(f32[256]{0:T(256)} %copy-done.90) | copy-start | bytes 3076
  560.0 10.4 %copy-start.46 = (bf16[8,144,768]{2,1,0:T(8,128)(2,1)S(1)}, bf16[8,144,768]{2,1,0:T(8,128)(2,1)}, u32[]{:S(2)}) copy-start(bf16[8,144,768]{2,1,0:T(8,128)(2,1)} %get-tuple-element.89) | copy-start | bytes 5308420
  570.4 5.4 copy-start.33
  571.8 5.7 copy-start.26
  571.8 7.5 copy-start.13
  571.8 7.5 copy-start.89
  573.8 7.5 copy-start.11
  573.8 7.5 copy-start.85
  608.3 296.2 %all-reduce.7.cloned.1.call-start = ((), (), s32[]{:S(2)}) async-start(), calls=%async_computation.12 | async-start | bytes 14155776 | tf_op jit(solution)/shard_map/psum | solution.py:1463
  609.3 6.9 copy-start.15
  609.3 6.9 copy-start.93
  647.7 4.9 copy-start.27
  904.5 5.5 copy-start.67
  904.5 6.4 copy-start.66
  904.5 7.2 copy-start.65
  906.4 6.2 copy-start.43
  910.0 3.6 copy-start.63
  (69 other events, 150.3 us)
Sparse Core Ops, SparseCore 0:
  10.5 38.9 all-gather.5
  51.5 54.7 all-gather.7
  108.2 54.3 all-gather.9
  336.1 48.3 reduce-scatter.10
  388.1 51.3 reduce-scatter.4
  442.7 85.9 reduce-scatter.6
  532.6 75.5 reduce-scatter.8
  610.6 35.2 all-reduce.4
  651.4 253.0 all-reduce.6

commit v2 on v1

--- a/solution.py
+++ b/solution.py
@@ -554,6 +554,10 @@
     return mesh.shape["seq"] == 8
 
 
+def add_low(left, right):
+    return (left.astype(wide) + right.astype(wide)).astype(low)
+
+
 def nt(left, right):
     return lax.dot_general(left, right, (((1,), (1,)), ((), ())), preferred_element_type=wide)
 
@@ -578,12 +582,113 @@
     return pl.BlockSpec(memory_space=pl.ANY)
 
 
-def greet(masks):
+def greet(masks, size=0):
     me = lax.axis_index("seq")
     barrier = pltpu.get_barrier_semaphore()
     for mask in masks:
         pl.semaphore_signal(barrier, inc=1, device_id={"seq": me ^ mask}, device_id_type=MESH)
-    pl.semaphore_wait(barrier, len(masks))
+    if not size:
+        pl.semaphore_wait(barrier, len(masks))
+        return
+    place = lax.axis_index("dp")
+    inner = (place > 0) & (place < size - 1)
+
+    @pl.when(place > 0)
+    def _():
+        pl.semaphore_signal(barrier, inc=1, device_id={"dp": place - 1}, device_id_type=MESH)
+
+    @pl.when(place < size - 1)
+    def _():
+        pl.semaphore_signal(barrier, inc=1, device_id={"dp": place + 1}, device_id_type=MESH)
+
+    @pl.when(inner)
+    def _():
+        pl.semaphore_wait(barrier, len(masks) + 2)
+
+    @pl.when(jnp.logical_not(inner))
+    def _():
+        pl.semaphore_wait(barrier, len(masks) + 1)
+
+
+class Line:
+    lag = 2
+
+    def __init__(self, size, chunks, mine, came, sent, send, recv):
+        place = lax.axis_index("dp")
+        self.chunks, self.mine, self.came, self.sent, self.send, self.recv = chunks, mine, came, sent, send, recv
+        self.count = mine.shape[0] // chunks
+        self.has = (place > 0, place < size - 1)
+        self.neighbour = (place - 1, place + 1)
+        self.lower = place < size // 2
+        self.steps = chunks + self.lag
+
+    def copy(self, side, chunk, first=False):
+        part = pl.ds(chunk * self.count, self.count)
+        return pltpu.make_async_remote_copy(
+            src_ref=self.mine.at[part] if first else self.sent.at[side, part],
+            dst_ref=self.came.at[side, part],
+            send_sem=self.send.at[side, chunk],
+            recv_sem=self.recv.at[side, chunk],
+            device_id={"dp": self.neighbour[1 - side]},
+            device_id_type=MESH,
+        )
+
+    def begin(self):
+        for side in range(2):
+
+            @pl.when(jnp.logical_not(self.has[side]))
+            def _(side=side):
+                for chunk in range(self.chunks):
+                    self.copy(side, chunk, True).start()
+                self.came[side] = jnp.zeros(self.mine.shape, low)
+
+    def forward(self, side, chunk):
+        part = pl.ds(chunk * self.count, self.count)
+
+        @pl.when(self.has[side])
+        def _():
+            self.copy(side, chunk).wait_recv()
+
+            @pl.when(self.has[1 - side])
+            def _():
+                self.sent[side, part] = add_low(self.mine[part], self.came[side, part])
+                self.copy(side, chunk).start()
+
+    def step(self, number):
+        if number >= self.steps:
+            return
+        for near in range(2):
+
+            @pl.when(self.lower if near == 0 else jnp.logical_not(self.lower))
+            def _(near=near):
+                if number < self.chunks:
+                    self.forward(near, number)
+                if number >= self.lag:
+                    self.forward(1 - near, number - self.lag)
+
+    def rest(self, first):
+        for number in range(first, self.steps):
+            self.step(number)
+
+    def total(self, part=slice(None)):
+        return self.mine[part].astype(wide) + self.came[0, part].astype(wide) + self.came[1, part].astype(wide)
+
+    def end(self):
+        for side in range(2):
+
+            @pl.when(self.has[1 - side])
+            def _(side=side):
+                for chunk in range(self.chunks):
+                    self.copy(side, chunk).wait_send()
+
+
+def line_scratch(shape, chunks):
+    return [
+        pltpu.VMEM((2,) + shape, low),
+        pltpu.VMEM((2,) + shape, low),
+        pltpu.SemaphoreType.DMA((2, chunks)),
+        pltpu.SemaphoreType.DMA((2, chunks)),
+    ]
 
 
 def remote(src, dst, send, recv, to):
@@ -598,44 +703,134 @@
     )
 
 
-def gather_table_kernel(rows, out, send, recv, keep):
+def gather_table_kernel(rows, extra, out, out_extra, send, recv, keep):
     me = lax.axis_index("seq")
     mine = me // 4
     greet((1, 2, 4, 6))
-    local = pltpu.make_async_copy(rows.at[mine], out.at[me], keep)
-    local.start()
+    own = [
+        pltpu.make_async_copy(rows.at[mine], out.at[me], keep.at[0]),
+        pltpu.make_async_copy(extra, out_extra.at[me], keep.at[1]),
+    ]
+    for copy in own:
+        copy.start()
     started = []
+    both = ((0, lambda table: rows.at[table], out), (1, lambda table: extra, out_extra))
     for slot, mask, table in ((0, 6, 1 - mine), (1, 2, mine), (2, 4, 1 - mine), (3, 1, mine)):
-        copy = remote(rows.at[table], out.at[me], send.at[slot], recv.at[slot], me ^ mask)
+        for kind, source, place in both:
+            copy = remote(source(table), place.at[me], send.at[kind, slot], recv.at[kind, slot], me ^ mask)
+            copy.start()
+            started.append(copy)
+    for slot, mask in ((1, 2), (2, 4), (0, 6)):
+        owner = me ^ mask
+        for kind, source, place in both:
+            remote(source(0), place.at[owner], send.at[kind, slot], recv.at[kind, slot], me ^ 1).wait_recv()
+            copy = remote(
+                place.at[owner], place.at[owner], send.at[kind, 4 + slot], recv.at[kind, 4 + slot], me ^ 1
+            )
+            copy.start()
+            started.append(copy)
+    for kind, source, place in both:
+        remote(source(0), place.at[me ^ 1], send.at[kind, 3], recv.at[kind, 3], me ^ 1).wait_recv()
+        for slot, mask in ((1, 2), (2, 4), (0, 6)):
+            remote(
+                source(0), place.at[me ^ mask ^ 1], send.at[kind, 4 + slot], recv.at[kind, 4 + slot], me ^ 1
+            ).wait_recv()
+    for copy in started:
+        copy.wait_send()
+    for copy in own:
+        copy.wait()
+
+
+def gather_table(rows, extra):
+    return pl.pallas_call(
+        gather_table_kernel,
+        out_shape=(
+            jax.ShapeDtypeStruct((8,) + rows.shape[1:], rows.dtype),
+            jax.ShapeDtypeStruct((8,) + extra.shape, extra.dtype),
+        ),
+        in_specs=[any_spec()] * 2,
+        out_specs=(any_spec(), any_spec()),
+        scratch_shapes=[
+            pltpu.SemaphoreType.DMA((2, 7)),
+            pltpu.SemaphoreType.DMA((2, 7)),
+            pltpu.SemaphoreType.DMA((2,)),
+        ],
+        compiler_params=params(1),
+    )(rows, extra)
+
+
+def scatter_plane_kernel(terms, out, sib, pair, came, far, came_far, send, recv, send_pair, recv_pair, send_far, recv_far):
+    me = lax.axis_index("seq")
+    half = out.shape[0] // 2
+    greet((1, 2, 4))
+    halves = (pl.ds(0, half), pl.ds(half, half))
+    started = []
+    chips = (6, 2, 4, 0)
+    for slot, mask in enumerate(chips):
+        copy = remote(terms.at[me ^ 1 ^ mask], sib.at[slot], send.at[slot], recv.at[slot], me ^ 1)
         copy.start()
         started.append(copy)
-    for slot, mask in ((1, 2), (2, 4), (0, 6)):
-        owner = me ^ mask
-        remote(rows.at[0], out.at[owner], send.at[slot], recv.at[slot], me ^ 1).wait_recv()
-        copy = remote(out.at[owner], out.at[owner], send.at[4 + slot], recv.at[4 + slot], me ^ 1)
-        copy.start()
-        started.append(copy)
-    remote(rows.at[0], out.at[me ^ 1], send.at[3], recv.at[3], me ^ 1).wait_recv()
-    for slot, mask in ((1, 2), (2, 4), (0, 6)):
-        remote(rows.at[0], out.at[me ^ mask ^ 1], send.at[4 + slot], recv.at[4 + slot], me ^ 1).wait_recv()
+
+    def pair_copy(slot):
+        return remote(
+            pair.at[slot], came.at[slot], send_pair.at[slot], recv_pair.at[slot], me ^ (2, 4, 2, 4)[slot]
+        )
+
+    def far_copy(slot):
+        return remote(far.at[slot], came_far.at[slot], send_far.at[slot], recv_far.at[slot], me ^ (4, 2)[slot])
+
+    def both(mask, slot, rows):
+        return terms[me ^ mask, rows].astype(wide) + sib[slot, rows].astype(wide)
+
+    for slot, mask in enumerate(chips):
+        remote(terms.at[0], sib.at[slot], send.at[slot], recv.at[slot], me ^ 1).wait_recv()
+        if mask == 6:
+            for side in range(2):
+                pair[side] = both(6, 0, halves[side]).astype(low)
+                pair_copy(side).start()
+        if mask == 2:
+            pair[2] = both(2, 1, halves[0]).astype(low)
+            pair_copy(2).start()
+        if mask == 4:
+            pair[3] = both(4, 2, halves[1]).astype(low)
+            pair_copy(3).start()
+    for side in range(2):
+        pair_copy(side).wait_recv()
+        mask, slot = ((4, 2), (2, 1))[side]
+        far[side] = (both(mask, slot, halves[side]) + came[side].astype(wide)).astype(low)
+        far_copy(side).start()
+    for side in range(2):
+        pair_copy(2 + side).wait_recv()
+        out[halves[side]] = both(0, 3, halves[side]) + came[2 + side].astype(wide)
+    for side in range(2):
+        far_copy(side).wait_recv()
+        out[halves[side]] += came_far[side].astype(wide)
     for copy in started:
         copy.wait_send()
-    local.wait()
-
-
-def gather_table(rows):
+    for slot in range(4):
+        pair_copy(slot).wait_send()
+    for side in range(2):
+        far_copy(side).wait_send()
+
+
+def scatter_plane(terms):
+    _, rows, width = terms.shape
     return pl.pallas_call(
-        gather_table_kernel,
-        out_shape=jax.ShapeDtypeStruct((8,) + rows.shape[1:], rows.dtype),
-        in_specs=[any_spec()],
-        out_specs=any_spec(),
+        scatter_plane_kernel,
+        out_shape=jax.ShapeDtypeStruct((rows, width), wide),
+        in_specs=[vmem_spec()],
+        out_specs=vmem_spec(),
         scratch_shapes=[
-            pltpu.SemaphoreType.DMA((7,)),
-            pltpu.SemaphoreType.DMA((7,)),
-            pltpu.SemaphoreType.DMA,
-        ],
-        compiler_params=params(1),
-    )(rows)
+            pltpu.VMEM((4, rows, width), low),
+            pltpu.VMEM((4, rows // 2, width), low),
+            pltpu.VMEM((4, rows // 2, width), low),
+            pltpu.VMEM((2, rows // 2, width), low),
+            pltpu.VMEM((2, rows // 2, width), low),
+        ]
+        + [pltpu.SemaphoreType.DMA((4,))] * 4
+        + [pltpu.SemaphoreType.DMA((2,))] * 2,
+        compiler_params=params(9),
+    )(terms)
 
 
 def heads_to_rows_kernel(blocks, out, send, recv, keep):
@@ -714,7 +909,7 @@
     )(rows)
 
 
-def sum_small_kernel(terms, out, mine, came, send, recv, send_back, recv_back):
+def sum_small_kernel(terms, earlier, out, mine, came, send, recv, send_back, recv_back):
     me = lax.axis_index("seq")
     greet(PEERS)
     mine[...] = terms[...].astype(low)
@@ -738,18 +933,19 @@
         copy.wait_send()
 
 
-def sum_small(terms):
+def sum_small(terms, collective_id, earlier=None):
     count, width = terms.shape
+    earlier = terms if earlier is None else earlier
     blocks = (8, count // 8, width)
     return pl.pallas_call(
         sum_small_kernel,
         out_shape=jax.ShapeDtypeStruct(blocks, low),
-        in_specs=[vmem_spec()],
+        in_specs=[vmem_spec(), any_spec()],
         out_specs=vmem_spec(),
         scratch_shapes=[pltpu.VMEM(blocks, low), pltpu.VMEM(blocks, low)]
         + [pltpu.SemaphoreType.DMA((8,))] * 4,
-        compiler_params=params(4),
-    )(terms.reshape(blocks)).reshape(count, width)
+        compiler_params=params(collective_id),
+    )(terms.reshape(blocks), earlier).reshape(count, width)
 
 
 def merge_parts_kernel(terms, stats, out, logsum, came, came_stats, send, recv, send_st, recv_st, back, recv_back, back_st, recv_back_st):
@@ -816,65 +1012,135 @@
     return out.reshape(count, width), logsum.reshape(count, 128)
 
 
-def scatter_rows_kernel(terms, grads, out, out_grads, sib, pair, came, send, recv, send_pair, recv_pair, send_grad, recv_grad, keep):
+def finish_kernel(
+    size, rows, grads, weights, vectors, joined, out, out_line, out_joined,
+    terms, sib, pair, came, blocks, came_blocks, line,
+    send, recv, send_pair, recv_pair, send_block, recv_block,
+    line_came, line_sent, send_line, recv_line, join_came, join_sent, send_join, recv_join,
+):
     me = lax.axis_index("seq")
     mine = me // 4
-    core = me % 2
-    greet(PEERS)
-    local = pltpu.make_async_copy(grads.at[me], out_grads.at[me], keep)
-    local.start()
-    started = []
+    count = out.shape[1]
+    width = grads.shape[1]
+    cut = blocks.shape[1] - 16
+    quarter = width // 3
+    greet(PEERS, size)
+    other = Line(size, 4, joined, join_came, join_sent, send_join, recv_join)
+    other.begin()
+    own = Line(size, 7, line, line_came, line_sent, send_line, recv_line)
+
+    d = grads[...]
+
+    def block_copy(mask):
+        return remote(
+            blocks.at[me ^ mask], came_blocks.at[mask], send_block.at[mask], recv_block.at[mask], me ^ mask
+        )
+
+    for mask in PEERS + (0,):
+        owner = me ^ mask
+        columns = pl.ds(pl.multiple_of(owner * cut, cut), cut)
+        blocks[owner, :cut] = tn(rows[:, columns], d).astype(low)
+        blocks[owner, cut:] = vectors[owner]
+        if mask:
+            block_copy(mask).start()
+    for number in range(3):
+        other.step(number)
     chips = (6, 2, 4, 0)
+
+    def term(owner):
+        return nt(grads[pl.ds(pl.multiple_of(owner * count, count), count)], weights[...])
+
+    def sib_copy(slot):
+        return remote(terms.at[slot], sib.at[slot], send.at[slot], recv.at[slot], me ^ 1)
+
+    def pair_copy(slot):
+        return remote(pair.at[slot], came.at[slot], send_pair.at[slot], recv_pair.at[slot], me ^ chips[slot])
+
     for slot, mask in enumerate(chips):
-        copy = remote(terms.at[me ^ 1 ^ mask], sib.at[slot], send.at[slot], recv.at[slot], me ^ 1)
-        copy.start()
-        started.append(copy)
+        terms[slot] = term(me ^ 1 ^ mask).astype(low)
+        sib_copy(slot).start()
+    other.rest(3)
     for slot, mask in enumerate(chips):
-        remote(terms.at[0], sib.at[slot], send.at[slot], recv.at[slot], me ^ 1).wait_recv()
+        here = term(me ^ mask)
+        sib_copy(slot).wait_recv()
+        here = here + sib[slot].astype(wide)
         if mask:
-            pair[slot] = (terms[me ^ mask].astype(wide) + sib[slot].astype(wide)).astype(low)
-            copy = remote(pair.at[slot], came.at[slot], send_pair.at[slot], recv_pair.at[slot], me ^ mask)
-            copy.start()
-            started.append(copy)
+            pair[slot] = here.astype(low)
+            pair_copy(slot).start()
+        else:
+            out[mine] = here
+
     for mask in PEERS:
-        copy = remote(grads.at[me ^ mask], out_grads.at[me], send_grad.at[mask], recv_grad.at[mask], me ^ mask)
-        copy.start()
-        started.append(copy)
-    for slot, mask in enumerate(chips[:3]):
-        remote(pair.at[0], came.at[slot], send_pair.at[slot], recv_pair.at[slot], me ^ mask).wait_recv()
-    out[mine] = terms[me].astype(wide) + sib[3].astype(wide) + came[1].astype(wide)
+        block_copy(mask).wait_recv()
+    came_blocks[0] = blocks[me]
+
+    def came_from(owner, part):
+        return came_blocks[owner ^ me, part].astype(wide)
+
+    total = jnp.zeros((16, width), wide)
+    for source in range(4):
+        both = came_from(source, pl.ds(0, cut)) + came_from(source + 4, pl.ds(0, cut))
+        for kind in range(3):
+            line[kind * cut : (kind + 1) * cut, source * quarter : (source + 1) * quarter] = both[
+                :, kind * quarter : (kind + 1) * quarter
+            ].astype(low)
+        total = total + came_from(source, pl.ds(cut, 16)) + came_from(source + 4, pl.ds(cut, 16))
+    line[3 * cut :] = jnp.zeros_like(line[3 * cut :])
+    line[3 * cut : 3 * cut + 16, :width] = total.astype(low)
+
+    own.begin()
+    own.rest(0)
+    for slot in (1, 2, 0):
+        pair_copy(slot).wait_recv()
+    out[mine] += came[1].astype(wide)
     out[1 - mine] = came[2].astype(wide) + came[0].astype(wide)
+
+    out_line[...] = own.total()
+    out_joined[...] = other.total()
     for mask in PEERS:
-        remote(grads.at[0], out_grads.at[me ^ mask], send_grad.at[mask], recv_grad.at[mask], me ^ mask).wait_recv()
-    for copy in started:
-        copy.wait_send()
-    local.wait()
-
-
-def scatter_rows(terms, grads):
-    _, rows, width = terms.shape
+        block_copy(mask).wait_send()
+    for slot in range(4):
+        sib_copy(slot).wait_send()
+    for slot in range(3):
+        pair_copy(slot).wait_send()
+    own.end()
+    other.end()
+
+
+def finish(rows, grads, weights, vectors, joined):
+    width = rows.shape[1]
+    count = rows.shape[0] // 8
+    cut = width // 8
+    line = (3 * cut + 64, width)
+    blocks = (8, cut + 16, grads.shape[1])
+    four, three = pltpu.SemaphoreType.DMA((4,)), pltpu.SemaphoreType.DMA((3,))
     return pl.pallas_call(
-        scatter_rows_kernel,
+        functools.partial(finish_kernel, lax.axis_size("dp")),
         out_shape=(
-            jax.ShapeDtypeStruct((2, rows, width), wide),
-            jax.ShapeDtypeStruct(grads.shape, low),
+            jax.ShapeDtypeStruct((2, count, width), wide),
+            jax.ShapeDtypeStruct(line, wide),
+            jax.ShapeDtypeStruct(joined.shape, wide),
         ),
-        in_specs=[vmem_spec(), any_spec()],
-        out_specs=(vmem_spec(), any_spec()),
+        in_specs=[vmem_spec()] * 5,
+        out_specs=(vmem_spec(),) * 3,
         scratch_shapes=[
-            pltpu.VMEM((4, rows, width), low),
-            pltpu.VMEM((3, rows, width), low),
-            pltpu.VMEM((3, rows, width), low),
-            pltpu.SemaphoreType.DMA((4,)),
-            pltpu.SemaphoreType.DMA((4,)),
-            pltpu.SemaphoreType.DMA((3,)),
-            pltpu.SemaphoreType.DMA((3,)),
-            pltpu.SemaphoreType.DMA((8,)),
-            pltpu.SemaphoreType.DMA((8,)),
-            pltpu.SemaphoreType.DMA,
-        ],
+            pltpu.VMEM((4, count, width), low),
+            pltpu.VMEM((4, count, width), low),
+            pltpu.VMEM((3, count, width), low),
+            pltpu.VMEM((3, count, width), low),
+            pltpu.VMEM(blocks, low),
+            pltpu.VMEM(blocks, low),
+            pltpu.VMEM(line, low),
+            four,
+            four,
+            three,
+            three,
+        ]
+        + [pltpu.SemaphoreType.DMA((8,))] * 2
+        + line_scratch(line, 7)
+        + line_scratch(joined.shape, 4),
         compiler_params=params(6),
-    )(terms, grads)
+    )(rows, grads, weights, vectors, joined)
 
 
 def plain(**more):
@@ -906,8 +1172,8 @@
     logsum[...] = logs
 
 
-def flash_forward(length, queries, keys, values, block):
-    count, width = queries.shape
+def flash_forward(length, three, block):
+    count, width = three.shape[0], three.shape[1] // 3
     return pl.pallas_call(
         flash_forward_kernel,
         out_shape=(
@@ -919,8 +1185,8 @@
             grid=(count // block,),
             in_specs=[
                 pl.BlockSpec((block, width), lambda i, n: (i, 0)),
-                pl.BlockSpec((count, width), lambda i, n: (0, 0)),
-                pl.BlockSpec((count, width), lambda i, n: (0, 0)),
+                pl.BlockSpec((count, width), lambda i, n: (0, 1)),
+                pl.BlockSpec((count, width), lambda i, n: (0, 2)),
             ],
             out_specs=[
                 pl.BlockSpec((block, width), lambda i, n: (i, 0)),
@@ -928,13 +1194,10 @@
             ],
         ),
         compiler_params=plain(),
-        cost_estimate=pl.CostEstimate(
-            flops=16 * count * count * width, bytes_accessed=8 * count * width, transcendentals=0
-        ),
-    )(length, queries, keys, values)
-
-
-def flash_backward_kernel(chunk, length, queries, grads, logsum, delta, keys, keys_t, values, dq_t, dk, dv, q_stack, g_stack, p_stack, s_stack, k_sum, v_sum):
+    )(length, three, three, three)
+
+
+def flash_backward_kernel(chunk, length, queries, grads, logsum, delta, keys, keys_t, values, out, q_stack, g_stack, p_stack, s_stack, k_sum, v_sum):
     step = pl.program_id(0)
     rows, width = queries.shape
     count = keys.shape[0]
@@ -970,25 +1233,21 @@
             dq_sums[head] = dq_sums[head] + nn(keys_t[head * 64 : head * 64 + 64, part], d_scores)
         v_sum[part] += nn(p_stack[...], g_stack[...])
         k_sum[part] += nn(s_stack[...], q_stack[...])
-    for head in range(heads):
-        dq_t[head * 64 : head * 64 + 64, :] = (dq_sums[head] * 0.125).astype(low)
+    dq = jnp.concatenate(dq_sums, 0) * 0.125
+    out[pl.ds(pl.multiple_of(step * rows, rows), rows), 0:width] = dq.T.astype(low)
 
     @pl.when(step == pl.num_programs(0) - 1)
     def _():
-        dk[...] = k_sum[...].astype(low)
-        dv[...] = v_sum[...].astype(low)
-
-
-def flash_backward(length, queries, grads, logsum, delta, keys, values, block, chunk):
-    count, width = queries.shape
+        out[:, width : 2 * width] = k_sum[...].astype(low)
+        out[:, 2 * width : 3 * width] = v_sum[...].astype(low)
+
+
+def flash_backward(length, three, grads, logsum, delta, block, chunk):
+    count, width = grads.shape
     heads = width // 64
     return pl.pallas_call(
         functools.partial(flash_backward_kernel, chunk),
-        out_shape=(
-            jax.ShapeDtypeStruct((width, count), low),
-            jax.ShapeDtypeStruct((count, width), low),
-            jax.ShapeDtypeStruct((count, width), low),
-        ),
+        out_shape=jax.ShapeDtypeStruct((count, 3 * width), low),
         grid_spec=pltpu.PrefetchScalarGridSpec(
             num_scalar_prefetch=1,
             grid=(count // block,),
@@ -997,15 +1256,11 @@
                 pl.BlockSpec((block, width), lambda i, n: (i, 0)),
                 pl.BlockSpec((heads, block), lambda i, n: (0, i)),
                 pl.BlockSpec((heads, block), lambda i, n: (0, i)),
-                pl.BlockSpec((count, width), lambda i, n: (0, 0)),
+                pl.BlockSpec((count, width), lambda i, n: (0, 1)),
                 pl.BlockSpec((width, count), lambda i, n: (0, 0)),
-                pl.BlockSpec((count, width), lambda i, n: (0, 0)),
+                pl.BlockSpec((count, width), lambda i, n: (0, 2)),
             ],
-            out_specs=[
-                pl.BlockSpec((width, block), lambda i, n: (0, i)),
-                pl.BlockSpec((count, width), lambda i, n: (0, 0)),
-                pl.BlockSpec((count, width), lambda i, n: (0, 0)),
-            ],
+            out_specs=pl.BlockSpec((count, 3 * width), lambda i, n: (0, 0)),
             scratch_shapes=[
                 pltpu.VMEM((heads * block, width), low),
                 pltpu.VMEM((heads * block, width), low),
@@ -1016,10 +1271,7 @@
             ],
         ),
         compiler_params=plain(),
-        cost_estimate=pl.CostEstimate(
-            flops=40 * count * count * width, bytes_accessed=14 * count * width, transcendentals=0
-        ),
-    )(length, queries, grads, logsum, delta, keys, keys.T, values)
+    )(length, three, grads, logsum, delta, three, three[:, width : 2 * width].T, three)
 
 
 def small_forward_kernel(causal, length, queries, keys, values, context, tops, sums):
@@ -1079,13 +1331,10 @@
             out_specs=[block(rows, width), block(rows, 128), block(rows, 128)],
         ),
         compiler_params=plain(),
-        cost_estimate=pl.CostEstimate(
-            flops=16 * tables * rows * count * width, bytes_accessed=6 * tables * count * width, transcendentals=0
-        ),
     )(length, queries, keys, values)
 
 
-def small_backward_kernel(causal, length, queries, keys, values, grads, context, logsum, dq, dk, dv):
+def small_backward_kernel(causal, length, queries, keys, values, grads, context, logsum, earlier, dq, dk, dv):
     table = pl.program_id(0)
     rows, width = queries.shape
     count = keys.shape[0]
@@ -1124,7 +1373,7 @@
         dv[:, place] = dv_here.astype(low)
 
 
-def small_backward(length, queries, keys, values, grads, context, logsum, causal):
+def small_backward(length, queries, keys, values, grads, context, logsum, causal, earlier):
     tables = length.shape[0]
     rows, width = queries.shape[0] // tables, queries.shape[1]
     count = keys.shape[0] // tables
@@ -1149,14 +1398,12 @@
                 block(rows, width),
                 block(rows, width),
                 block(rows, 128),
+                any_spec(),
             ],
             out_specs=[block(rows, width), block(count, width), block(count, width)],
         ),
         compiler_params=plain(),
-        cost_estimate=pl.CostEstimate(
-            flops=40 * tables * rows * count * width, bytes_accessed=10 * tables * count * width, transcendentals=0
-        ),
-    )(length, queries, keys, values, grads, context, logsum)
+    )(length, queries, keys, values, grads, context, logsum, earlier)
 
 
 def gelu_parts(values):
@@ -1165,11 +1412,9 @@
     return values * bell, slope
 
 
-def feed_forward_kernel(rows, expand, contract, out, acts, slopes):
-    act, slope = gelu_parts(nn(rows[...], expand[0]))
-    act = act.astype(low)
-    acts[0] = act
-    slopes[0] = slope.astype(low)
+def feed_forward_kernel(rows, expand, contract, out):
+    hidden = nn(rows[...], expand[0])
+    act = (hidden * (0.5 * (1.0 + lax.erf(hidden * 0.7071067811865476)))).astype(low)
     term = nn(act, contract[0])
 
     @pl.when(pl.program_id(0) == 0)
@@ -1186,75 +1431,220 @@
     parts, _, hidden = expand.shape
     return pl.pallas_call(
         feed_forward_kernel,
-        out_shape=(
-            jax.ShapeDtypeStruct((count, width), wide),
-            jax.ShapeDtypeStruct((parts, count, hidden), low),
-            jax.ShapeDtypeStruct((parts, count, hidden), low),
-        ),
+        out_shape=jax.ShapeDtypeStruct((count, width), wide),
         grid=(parts,),
         in_specs=[
             pl.BlockSpec((count, width), lambda j: (0, 0)),
             pl.BlockSpec((1, width, hidden), lambda j: (j, 0, 0)),
             pl.BlockSpec((1, hidden, width), lambda j: (j, 0, 0)),
         ],
-        out_specs=[
-            pl.BlockSpec((count, width), lambda j: (0, 0)),
-            pl.BlockSpec((1, count, hidden), lambda j: (j, 0, 0)),
-            pl.BlockSpec((1, count, hidden), lambda j: (j, 0, 0)),
-        ],
+        out_specs=pl.BlockSpec((count, width), lambda j: (0, 0)),
         compiler_params=plain(),
-        cost_estimate=pl.CostEstimate(
-            flops=4 * count * width * hidden * parts, bytes_accessed=4 * width * hidden * parts, transcendentals=0
+    )(rows, expand, contract)
+
+
+def outer_kernel(order, earlier, rows, *refs):
+    *grads, away, kept = refs
+    step = pl.program_id(0)
+    half = pl.num_programs(0) // 2
+    size = rows.shape[1]
+    for place, grad in enumerate(grads):
+        term = tn(rows[...], grad[...]).astype(low)
+
+        @pl.when(step < half)
+        def _(place=place, term=term):
+            away[0, place * size : (place + 1) * size] = term
+
+        @pl.when(step >= half)
+        def _(place=place, term=term):
+            kept[0, place * size : (place + 1) * size] = term
+
+
+def outer_by_owner(order, earlier, rows, *grads):
+    count, width = rows.shape
+    parts = order.shape[0]
+    half, size = parts // 2, width // parts
+    shape = jax.ShapeDtypeStruct((half, len(grads) * size, width), low)
+    return pl.pallas_call(
+        outer_kernel,
+        out_shape=(shape, shape),
+        grid_spec=pltpu.PrefetchScalarGridSpec(
+            num_scalar_prefetch=1,
+            grid=(parts,),
+            in_specs=[any_spec(), pl.BlockSpec((count, size), lambda j, o: (0, o[j]))]
+            + [pl.BlockSpec((count, width), lambda j, o: (0, 0))] * len(grads),
+            out_specs=[
+                pl.BlockSpec((1,) + shape.shape[1:], lambda j, o: (jnp.minimum(j, half - 1), 0, 0)),
+                pl.BlockSpec((1,) + shape.shape[1:], lambda j, o: (jnp.maximum(j - half, 0), 0, 0)),
+            ],
         ),
-    )(rows, expand, contract)
-
-
-def feed_backward_kernel(rows_t, grads, acts, slopes, expand, contract, out, d_expand, d_contract):
-    g = grads[...]
-    act = acts[0]
-    d_hidden = (nt(g, contract[0]) * slopes[0].astype(wide)).astype(low)
-    d_contract[0] = tn(act, g).astype(low)
-    d_expand[0] = nn(rows_t[...], d_hidden).astype(low)
-    term = nt(d_hidden, expand[0])
-
-    @pl.when(pl.program_id(0) == 0)
+        compiler_params=plain(),
+    )(order, earlier, rows, *grads)
+
+
+def widen_kernel(feed, later, earlier, *outs):
+    half = outs[1].shape[0]
+    outs[0][...] = feed[:half].astype(wide).T
+    outs[1][...] = feed[half:].astype(wide)
+    start = 0
+    for out in outs[2:]:
+        out[...] = later[start : start + out.shape[0]].astype(wide)
+        start += out.shape[0]
+
+
+def widen_after(feed, later, heights, earlier):
+    width = feed.shape[1]
+    half = feed.shape[0] // 2
+    shapes = [jax.ShapeDtypeStruct((width, half), wide), jax.ShapeDtypeStruct((half, width), wide)]
+    shapes += [jax.ShapeDtypeStruct((height, width), wide) for height in heights]
+    return pl.pallas_call(
+        widen_kernel,
+        out_shape=tuple(shapes),
+        in_specs=[vmem_spec()] * 2 + [any_spec()],
+        out_specs=tuple(vmem_spec() for _ in shapes),
+        compiler_params=plain(),
+    )(feed, later, earlier)
+
+
+def feed_backward_kernel(rows, grads, expand, contract, earlier, out, d_both, expand_sum, contract_sum):
+    step = pl.program_id(0)
+    x = rows[0]
+    g = grads[0]
+    act, slope = gelu_parts(nn(x, expand[...]))
+    d_hidden = (nt(g, contract[...]) * slope).astype(low)
+    out[0] = nt(d_hidden, expand[...]).astype(low)
+    one = tn(d_hidden, x)
+    two = tn(act.astype(low), g)
+
+    @pl.when(step == 0)
     def _():
-        out[...] = term
-
-    @pl.when(pl.program_id(0) > 0)
+        expand_sum[...] = one
+        contract_sum[...] = two
+
+    @pl.when(step > 0)
     def _():
-        out[...] += term
-
-
-def feed_backward(rows, grads, acts, slopes, expand, contract):
-    count, width = rows.shape
-    parts, _, hidden = expand.shape
+        expand_sum[...] += one
+        contract_sum[...] += two
+
+    @pl.when(step == pl.num_programs(0) - 1)
+    def _():
+        d_both[: expand_sum.shape[0]] = expand_sum[...].astype(low)
+        d_both[expand_sum.shape[0] :] = contract_sum[...].astype(low)
+
+
+def feed_backward(rows, grads, expand, contract, earlier):
+    parts, count, width = rows.shape
+    hidden = contract.shape[0]
     return pl.pallas_call(
         feed_backward_kernel,
-        out_shape=(
-            jax.ShapeDtypeStruct((count, width), wide),
-            jax.ShapeDtypeStruct((parts, width, hidden), low),
-            jax.ShapeDtypeStruct((parts, hidden, width), low),
-        ),
+        out_shape=(jax.ShapeDtypeStruct(rows.shape, low), jax.ShapeDtypeStruct((2 * hidden, width), low)),
         grid=(parts,),
         in_specs=[
-            pl.BlockSpec((width, count), lambda j: (0, 0)),
-            pl.BlockSpec((count, width), lambda j: (0, 0)),
-            pl.BlockSpec((1, count, hidden), lambda j: (j, 0, 0)),
-            pl.BlockSpec((1, count, hidden), lambda j: (j, 0, 0)),
-            pl.BlockSpec((1, width, hidden), lambda j: (j, 0, 0)),
-            pl.BlockSpec((1, hidden, width), lambda j: (j, 0, 0)),
+            pl.BlockSpec((1, count, width), lambda j: (j, 0, 0)),
+            pl.BlockSpec((1, count, width), lambda j: (j, 0, 0)),
+            pl.BlockSpec((width, hidden), lambda j: (0, 0)),
+            pl.BlockSpec((hidden, width), lambda j: (0, 0)),
+            any_spec(),
         ],
         out_specs=[
-            pl.BlockSpec((count, width), lambda j: (0, 0)),
-            pl.BlockSpec((1, width, hidden), lambda j: (j, 0, 0)),
-            pl.BlockSpec((1, hidden, width), lambda j: (j, 0, 0)),
+            pl.BlockSpec((1, count, width), lambda j: (j, 0, 0)),
+            pl.BlockSpec((2 * hidden, width), lambda j: (0, 0)),
         ],
+        scratch_shapes=[pltpu.VMEM((hidden, width), wide)] * 2,
         compiler_params=plain(),
-        cost_estimate=pl.CostEstimate(
-            flops=8 * count * width * hidden * parts, bytes_accessed=10 * width * hidden * parts, transcendentals=0
-        ),
-    )(rows.T, grads, acts, slopes, expand, contract)
+    )(rows, grads, expand, contract, earlier)
+
+
+def feed_weights_kernel(rows, grads, expand, contract, earlier, d_expand, d_contract, expand_sum, contract_sum):
+    step = pl.program_id(0)
+    x = rows[...].reshape(-1, rows.shape[3])
+    g = grads[...].reshape(-1, rows.shape[3])
+    act, slope = gelu_parts(nn(x, expand[...]))
+    d_hidden = (nt(g, contract[...]) * slope).astype(low)
+    one = tn(d_hidden, x)
+    two = tn(act.astype(low), g)
+
+    @pl.when(step == 0)
+    def _():
+        expand_sum[...] = one
+        contract_sum[...] = two
+
+    @pl.when(step > 0)
+    def _():
+        expand_sum[...] += one
+        contract_sum[...] += two
+
+    @pl.when(step == pl.num_programs(0) - 1)
+    def _():
+        d_expand[...] = expand_sum[...].T
+        d_contract[...] = contract_sum[...]
+
+
+def feed_weights(both, expand, contract, earlier):
+    parts, _, count, width = both.shape
+    hidden = contract.shape[0]
+    block = (parts // 2, 1, count, width)
+    return pl.pallas_call(
+        feed_weights_kernel,
+        out_shape=(jax.ShapeDtypeStruct((width, hidden), wide), jax.ShapeDtypeStruct((hidden, width), wide)),
+        grid=(2,),
+        in_specs=[
+            pl.BlockSpec(block, lambda j: (j, 0, 0, 0)),
+            pl.BlockSpec(block, lambda j: (j, 1, 0, 0)),
+            pl.BlockSpec((width, hidden), lambda j: (0, 0)),
+            pl.BlockSpec((hidden, width), lambda j: (0, 0)),
+            any_spec(),
+        ],
+        out_specs=[
+            pl.BlockSpec((width, hidden), lambda j: (0, 0)),
+            pl.BlockSpec((hidden, width), lambda j: (0, 0)),
+        ],
+        scratch_shapes=[pltpu.VMEM((hidden, width), wide)] * 2,
+        compiler_params=plain(),
+    )(both, both, expand, contract, earlier)
+
+
+OWNERS = (3, 5, 7, 1, 2, 4, 6, 0)
+
+
+def swap(array, mask):
+    return lax.ppermute(array, "seq", [(i, i ^ mask) for i in range(8)])
+
+
+def add_kernel(left, right, earlier, out):
+    out[...] = add_low(left[...], right[...])
+
+
+def add_after(left, right, earlier):
+    return pl.pallas_call(
+        add_kernel,
+        out_shape=jax.ShapeDtypeStruct(left.shape, low),
+        in_specs=[vmem_spec()] * 2 + [any_spec()],
+        out_specs=vmem_spec(),
+        compiler_params=plain(),
+    )(left, right, earlier)
+
+
+def scatter_cores(away, kept, earlier):
+    return add_after(kept, swap(away, 1), earlier)
+
+
+def scatter_first(both):
+    half = both.shape[1] // 2
+    one, two = both[:, :half], both[:, half:]
+    one_came = swap(jnp.stack([one[0], one[2]]), 2)
+    two_came = swap(jnp.stack([two[1], two[2]]), 4)
+    return (
+        add_low(one[3], one_came[0]),
+        add_low(one[1], one_came[1]),
+        add_low(two[3], two_came[0]),
+        add_low(two[0], two_came[1]),
+    )
+
+
+def scatter_second(parts):
+    one, one_far, two, two_far = parts
+    return add_low(one, swap(one_far, 4)), add_low(two, swap(two_far, 2))
 
 
 def plane_body(
@@ -1316,28 +1706,24 @@
         return lax.dynamic_slice_in_dim(vector, me * slice_rows, slice_rows, 0)
 
     source_flat = flat(source_tokens)
-    target_all = lax.all_gather(
-        jnp.stack([jnp.swapaxes(target_tokens, 0, 1), jnp.swapaxes(target_cotangent, 0, 1)], 0), "seq", axis=2, tiled=True
-    )
-    target_flat = target_all[0].reshape(-1, width)
-    target_grad = target_all[1].reshape(-1, width)
     all_expand = lax.all_gather(encoder_expand, "seq", axis=0)
     all_contract = lax.all_gather(encoder_contract, "seq", axis=0)
-
-    rows = gather_table(source_flat.reshape(tables, slots, width))
+    target_pair = jnp.stack([jnp.swapaxes(target_tokens, 0, 1), jnp.swapaxes(target_cotangent, 0, 1)], 0)
+    rows, target_all = gather_table(source_flat.reshape(tables, slots, width), target_pair.reshape(-1, width))
     rows = rows.reshape(-1, width)
-    w_query, w_key, w_value = columns(encoder_query), columns(encoder_key), columns(encoder_value)
+    target_all = jnp.moveaxis(target_all.reshape(8, 2, tables, places, width), 0, 2).reshape(2, -1, width)
+    target_flat, target_grad = target_all[0], target_all[1]
+    w_three = jnp.concatenate([columns(encoder_query), columns(encoder_key), columns(encoder_value)], 1)
     length = lax.dynamic_slice_in_dim(source_lengths, me // 4, 1, 0)
-    queries = project(rows, w_query).astype(low)
-    keys = project(rows, w_key).astype(low)
-    values = project(rows, w_value).astype(low)
-    context, logsum = flash_forward(length, queries, keys, values, 256)
+    three = project(rows, w_three).astype(low)
+    context, logsum = flash_forward(length, three, 256)
     encoder_context = heads_to_rows(context.reshape(8, slots, quarter)).reshape(-1, width)
     first, first_back = jax.vjp(
         layer_norm, source_flat.astype(wide) + project(encoder_context, encoder_mix), attend_gain, attend_shift
     )
     first_low = first.astype(low)
-    widened, acts, slopes = feed_forward(first_low, all_expand, all_contract)
+    widened = feed_forward(first_low, all_expand, all_contract)
+    first_all = lax.all_gather(first_low, "seq", axis=0)
     second, second_back = jax.vjp(layer_norm, first + widened, encoder_gain, encoder_shift)
     encoded = second.astype(low)
 
@@ -1366,72 +1752,42 @@
     hidden = project(fourth_low, decoder_expand)
     decoder_acts, gelu_back = jax.vjp(gelu_exact, hidden)
     decoder_acts = decoder_acts.astype(low)
-    narrowed = sum_small(project(decoder_acts, decoder_contract)).astype(wide)
+    narrowed = sum_small(project(decoder_acts, decoder_contract), 4, first_all).astype(wide)
     fifth, fifth_back = jax.vjp(layer_norm, fourth + narrowed, decoder_gain, decoder_shift)
     decoded = jnp.swapaxes(own_places(fifth.astype(low)), 0, 1)
 
     d_fifth, grad_decoder_gain, grad_decoder_shift = fifth_back(target_grad.astype(wide))
     fifth_low = d_fifth.astype(low)
     d_hidden = gelu_back(project_back(fifth_low, decoder_contract))[0].astype(low)
-    grad_decoder_expand = outer_sum(fourth_low, d_hidden)
-    grad_decoder_contract = outer_sum(decoder_acts, fifth_low)
-    d_rows = sum_small(project_back(d_hidden, decoder_expand)).astype(wide)
+    eighth = fourth_low.shape[0] // 8
+    decoder_pair = jnp.stack(
+        [lax.dynamic_slice_in_dim(array, me * eighth, eighth, 0) for array in (fourth_low, fifth_low)], 0
+    )
+    decoder_pair = lax.all_gather(decoder_pair, ("dp", "seq"), axis=0)
+    def over_tables(terms):
+        part = lax.psum_scatter(terms, "dp", scatter_dimension=0, tiled=True)
+        return lax.all_gather(part, "dp", axis=0, tiled=True)
+
+    def join(arrays):
+        return jnp.concatenate([a.astype(low) for a in arrays], 0)
+
+    d_rows = sum_small(project_back(d_hidden, decoder_expand), 10).astype(wide)
     d_fourth, grad_cross_gain, grad_cross_shift = fourth_back(d_fifth + d_rows)
     cross_low = d_fourth.astype(low)
     grad_cross_mix = outer_sum(own(cross_context), cross_low)
     d_cross = project_back(cross_low, cross_mix).astype(low)
     dq_part, dk_cross, dv_cross = small_backward(
-        here, cross_queries, cross_keys, cross_values, d_cross, cross_context, cross_logs, False
+        here, cross_queries, cross_keys, cross_values, d_cross, cross_context, cross_logs, False, cross_logs
     )
     d_encoded = project_back(dk_cross, cross_key) + project_back(dv_cross, cross_value)
-    cross_pair = outer_sum(encoded, jnp.concatenate([dk_cross, dv_cross], 1)).astype(low)
-    cross_pair = lax.psum_scatter(cross_pair, "seq", scatter_dimension=0, tiled=True)
+    order = me ^ jnp.array(OWNERS, jnp.int32)
+
 
     d_second, grad_encoder_gain, grad_encoder_shift = second_back(flat(source_cotangent).astype(wide) + d_encoded)
-    d_rows, d_expand, d_contract = feed_backward(
-        first_low, d_second.astype(low), acts, slopes, all_expand, all_contract
-    )
-    d_expand = lax.psum_scatter(d_expand, "seq", scatter_dimension=0, tiled=False)
-    d_contract = lax.psum_scatter(d_contract, "seq", scatter_dimension=0, tiled=False)
-    d_first, grad_attend_gain, grad_attend_shift = first_back(d_second + d_rows)
-    encoder_low = d_first.astype(low)
-    encoder_mix_part = outer_sum(encoder_context, encoder_low).astype(low)
-    encoder_mix_part = lax.psum_scatter(encoder_mix_part, "seq", scatter_dimension=0, tiled=True)
-    d_context = rows_to_heads(project_back(encoder_low, encoder_mix).astype(low).reshape(tables, slots, width))
-    d_context = d_context.reshape(-1, quarter)
-    delta = jnp.sum(
-        (d_context.astype(wide) * context.astype(wide)).reshape(-1, quarter // 64, 64), -1
-    )
-    dq_t, dk, dv = flash_backward(
-        length, queries, d_context, logsum[:, : quarter // 64].T, delta.T, keys, values, 256, 512
-    )
-    term = (
-        lax.dot_general(dq_t, w_query, (((0,), (1,)), ((), ())), preferred_element_type=wide)
-        + project_back(dk, w_key)
-        + project_back(dv, w_value)
-    ).astype(low)
-    weight_terms = jnp.concatenate(
-        [
-            lax.dot_general(rows, dq_t, (((0,), (1,)), ((), ())), preferred_element_type=wide).astype(low),
-            outer_sum(rows, dk).astype(low),
-            outer_sum(rows, dv).astype(low),
-        ],
-        1,
-    )
-    vectors = jnp.stack(
-        [grad_attend_gain, grad_attend_shift, grad_encoder_gain, grad_encoder_shift], 0
-    ).astype(low)
-    vectors = jnp.swapaxes(vectors.reshape(4, 8, slice_rows), 0, 1)
-    vectors = jnp.pad(vectors, ((0, 0), (0, 12), (0, 3 * quarter - slice_rows)))
-    grads = jnp.concatenate([weight_terms.reshape(8, slice_rows, 3 * quarter), vectors], 1)
-    d_source, came = scatter_rows(term.reshape(8, slots, width), grads)
-    came = jnp.sum(came.reshape(2, 4, slice_rows + 16, 3 * quarter).astype(wide), 0)
-    grad_source = unflat(d_first + d_source.reshape(-1, width))
-    encoder_three = jnp.moveaxis(came[:, :slice_rows].reshape(4, slice_rows, 3, quarter), (2, 1), (0, 1))
-    encoder_three = encoder_three.reshape(3, slice_rows, width)
-    encoder_vectors = jnp.sum(came[:, slice_rows : slice_rows + 4, :slice_rows], 0)
-
-    dq_cross = sum_small(dq_part)
+    d_second_low = d_second.astype(low)
+    d_all = lax.all_gather(d_second_low, "seq", axis=0)
+    dq_cross = sum_small(dq_part, 11, d_second_low)
+    cross_away, cross_kept = outer_by_owner(order, decoder_pair, encoded, dk_cross, dv_cross)
     grad_cross_query = outer_sum(own(third_low), dq_cross)
     d_third, grad_self_gain, grad_self_shift = third_back(d_fourth + project_back(dq_cross, cross_query))
     self_low = d_third.astype(low)
@@ -1445,6 +1801,7 @@
         decoder_context,
         self_logs,
         True,
+        cross_away,
     )
     dq_self = dq_self.astype(low)
     target_own = own(target_flat)
@@ -1458,9 +1815,6 @@
         + project_back(dv_self, decoder_value)
     )
     grad_target = jnp.swapaxes(grad_target, 0, 1)
-
-    def over_tables(*arrays):
-        return [a.astype(wide) for a in lax.psum([a.astype(low) for a in arrays], "dp")]
 
     decoder_vectors = jnp.stack(
         [
@@ -1476,37 +1830,49 @@
         ],
         0,
     )
-    (
+    decoder_vectors = jnp.pad(decoder_vectors.reshape(1, -1), ((0, 15), (0, width - 6 * slice_rows)))
+    middle = [
         grad_decoder_query,
         grad_decoder_key,
         grad_decoder_value,
         grad_decoder_mix,
         grad_cross_query,
         grad_cross_mix,
-        grad_decoder_expand,
-        grad_decoder_contract,
         decoder_vectors,
-    ) = over_tables(
-        grad_decoder_query,
-        grad_decoder_key,
-        grad_decoder_value,
-        grad_decoder_mix,
-        grad_cross_query,
-        grad_cross_mix,
-        grad_decoder_expand,
-        grad_decoder_contract,
-        decoder_vectors,
-    )
-    cross_pair, d_expand, d_contract, encoder_mix_part, decoder_vectors = lax.optimization_barrier(
-        (cross_pair, d_expand, d_contract, encoder_mix_part, decoder_vectors)
-    )
-    cross_pair, d_expand, d_contract, encoder_mix_part = over_tables(
-        cross_pair, d_expand, d_contract, encoder_mix_part
-    )
-    encoder_three, encoder_vectors, encoder_mix_part = lax.optimization_barrier(
-        (encoder_three, encoder_vectors, encoder_mix_part)
-    )
-    encoder_three, encoder_vectors = over_tables(encoder_three, encoder_vectors)
+    ]
+    middle_join = join(middle + [jnp.zeros((48, width), low)])
+    middle_sum = over_tables(middle_join)
+    d_terms, feed_join = feed_backward(first_all, d_all, encoder_expand, encoder_contract, dq_self)
+    feed_sum = over_tables(feed_join)
+    cross_both = scatter_cores(cross_away, cross_kept, feed_join)
+    d_rows = scatter_plane(d_terms)
+    d_first, grad_attend_gain, grad_attend_shift = first_back(d_second + d_rows)
+    encoder_low = d_first.astype(low)
+    mix_away, mix_kept = outer_by_owner(order, encoder_low, encoder_context, encoder_low)
+    d_context = rows_to_heads(project_back(encoder_low, encoder_mix).astype(low).reshape(tables, slots, width))
+    mix_both = scatter_cores(mix_away, mix_kept, d_context)
+    d_context = d_context.reshape(-1, quarter)
+    delta = jnp.sum(
+        (d_context.astype(wide) * context.astype(wide)).reshape(-1, quarter // 64, 64), -1
+    )
+    d_three = flash_backward(length, three, d_context, logsum[:, : quarter // 64].T, delta.T, 256, 512)
+    vectors = jnp.stack(
+        [grad_attend_gain, grad_attend_shift, grad_encoder_gain, grad_encoder_shift], 0
+    ).astype(low)
+    vectors = jnp.swapaxes(vectors.reshape(4, 8, slice_rows), 0, 1)
+    vectors = jnp.pad(vectors, ((0, 0), (0, 12), (0, 3 * quarter - slice_rows)))
+    parts = scatter_second(scatter_first(mix_both)) + scatter_second(scatter_first(cross_both))
+    d_source, line, plane_sum = finish(rows, d_three, w_three, vectors, join(parts))
+    grad_decoder_expand, grad_decoder_contract = feed_weights(
+        decoder_pair, decoder_expand, decoder_contract, d_three
+    )
+    grad_source = unflat(d_first + d_source.reshape(-1, width))
+    encoder_three = line[: 3 * slice_rows].reshape(3, slice_rows, width)
+    encoder_vectors = line[3 * slice_rows : 3 * slice_rows + 4, :slice_rows]
+    plane_three = plane_sum.reshape(3, slice_rows, width)
+    sums = widen_after(feed_sum, middle_sum, [part.shape[0] for part in middle], line)
+    grad_encoder_expand, grad_encoder_contract, *six, decoder_vectors = sums
+    decoder_vectors = decoder_vectors[0, : 6 * slice_rows].reshape(6, slice_rows)
     return (
         unflat(encoded),
         decoded,
@@ -1515,23 +1881,23 @@
         encoder_three[0],
         encoder_three[1],
         encoder_three[2],
-        encoder_mix_part,
+        plane_three[0],
         encoder_vectors[0],
         encoder_vectors[1],
-        d_expand,
-        d_contract,
+        grad_encoder_expand,
+        grad_encoder_contract,
         encoder_vectors[2],
         encoder_vectors[3],
-        grad_decoder_query,
-        grad_decoder_key,
-        grad_decoder_value,
-        grad_decoder_mix,
+        six[0],
+        six[1],
+        six[2],
+        six[3],
         decoder_vectors[0],
         decoder_vectors[1],
-        grad_cross_query,
-        cross_pair[:, :width],
-        cross_pair[:, width:],
-        grad_cross_mix,
+        six[4],
+        plane_three[1],
+        plane_three[2],
+        six[5],
         decoder_vectors[2],
         decoder_vectors[3],
         grad_decoder_expand,

time: 939 us -> 720 us (0.77)
  waiting for transfers between devices: 279 us -> 9.37 us
  Pallas kernels: 386 us -> 515 us
  blocking collectives: 33 us -> 0 us
  matrix products: 96.4 us -> 65.1 us
  other arithmetic: 64.9 us -> 47 us
    psum x2 -> x0, waiting for transfers between devices: 247 us -> none  [over_tables(): lax.psum([a.astype(low) for a in arrays], 'dp')]
    pallas_call x4 -> x11, Pallas kernels: 134 us -> 257 us  [the longest x1 76.3 us: finish(): pl.pallas_call(functools.partial(finish_kernel, lax.axis_size('dp')), out...]
    psum x2 -> x0, blocking collectives: 33 us -> none  [over_tables(): lax.psum([a.astype(low) for a in arrays], 'dp')]
    reduce_scatter x4 -> x2, waiting for transfers between devices: 23.7 us -> 0.02 us  [over_tables(): part = lax.psum_scatter(terms, 'dp', scatter_dimension=0, tiled=True)]
    dot_general x12 -> x6, matrix products: 25.8 us -> 11.1 us  [outer_sum(): jnp.einsum('rd,re->de', rows, grads, preferred_element_type=jnp.float32)]
    convert_element_type x15 -> x9, other arithmetic: 19.3 us -> 9.59 us  [the longest x4 5.5 us: add_low(): return (left.astype(wide) + right.astype(wide)).astype(low)]
    dot_general x13 -> x10, matrix products: 29.5 us -> 23 us  [project_back(): jnp.einsum('re,de->rd', grads, weight, preferred_element_type=jnp.float32)]
    unnamed x222 -> x153, local copies, waits for them, and re-layouts: 21.5 us -> 15.8 us
  transfers between devices with their start and end apart: 9 -> 19, of which waited for: 4 -> 5; matrix products, arithmetic and copies ran while one was open for 15% -> 20% of each run, Pallas kernels for 28% -> 69%
where the time goes in v2:
time: 720 us; the launch traced here: 710 us
  Pallas kernels  515 us (72%)
  matrix products  65.1 us (9%)
  local copies, waits for them, and re-layouts  48.9 us (7%)
  other arithmetic  47 us (7%)
  between operations  15.2 us (2%)
  starting transfers between devices  9.77 us (1%)
  waiting for transfers between devices  9.37 us (1%)
    pallas_call x1, Pallas kernels, finish(): pl.pallas_call(functools.partial(finish_kernel, lax.axis_size('dp')), out...  76.3 us
    pallas_call x1, Pallas kernels, flash_backward(): pl.pallas_call(functools.partial(flash_backward_kernel, chunk), out_shape...  58.7 us
    pallas_call x3, Pallas kernels, sum_small(): pl.pallas_call(sum_small_kernel, out_shape=jax.ShapeDtypeStruct(blocks, l...  55.9 us
    pallas_call x1, Pallas kernels, gather_table(): pl.pallas_call(gather_table_kernel, out_shape=(jax.ShapeDtypeStruct((8,)...  48 us
    pallas_call x1, Pallas kernels, scatter_plane(): pl.pallas_call(scatter_plane_kernel, out_shape=jax.ShapeDtypeStruct((rows...  44.7 us
    pallas_call x1, Pallas kernels, flash_forward(): pl.pallas_call(flash_forward_kernel, out_shape=(jax.ShapeDtypeStruct((cou...  36.8 us
    pallas_call x1, Pallas kernels, feed_backward(): pl.pallas_call(feed_backward_kernel, out_shape=(jax.ShapeDtypeStruct(rows...  31.1 us
    dot_general x12, matrix products, project(): return jnp.dot(rows, weight, preferred_element_type=jnp.float32)  31 us
  transfers between devices with their start and end apart: 19, of which 5 were waited for; matrix products, arithmetic and copies ran while one was open for 20% of the time, Pallas kernels for 69%

profile of v2, /device:TPU:0, one launch (start us, length us, event | category | flops | bytes accessed | tf_op | source)
XLA Modules:
  0.0 709.9 jit_solution(4149781352499813275)
XLA Ops:
  11.6 48.0 %shard_map.544 = (bf16[8,256,1024]{2,1,0:T(8,128)(2,1)}, bf16[8,64,1024]{2,1,0:T(8,128)(2,1)}) custom-call(bf16[2,256,1024]{2,1,0:T(8,128)(2,1)} %bitcast.237, bf16[64,1024]{1,0:T(8,128)(2,1)} %bitcast.262), custom_call_target="tpu_custom_call" | custom-call | tf_op jit(solution)/shard_map/pallas_call | solution.py:745
  63.3 7.4 %convolution_convert_fusion.queries.keys.values = bf16[2048,768]{1,0:T(8,128)(2,1)} fusion(bf16[2048,1024]{1,0:T(8,128)(2,1)} %bitcast.233, bf16[1024,256]{1,0:T(8,128)(2,1)S(1)} %get-tuple-element.176, bf16[1024,256]{1,0:T(8,128)(2,1)S(1)} %get-tuple-element.177, bf16[1024,256]{1,0:T(8,128)(2,1)S(1)} %constant_dynamic-slice_fusion.4), kind=kOutput, calls=%fused_computation | convolution fusion | flops 3227516928 | bytes 8912896 | tf_op jit(solution)/shard_map/dot_general | solution.py:29
  70.6 36.8 %shard_map.545 = (bf16[2048,256]{1,0:T(8,128)(2,1)}, f32[2048,128]{1,0:T(8,128)}) custom-call(s32[1]{0:T(128)} %dynamic_slice.54.length, bf16[2048,768]{1,0:T(8,128)(2,1)} %convolution_convert_fusion.queries.keys.values, bf16[2048,768]{1,0:T(8,128)(2,1)} %convolution_convert_fusion.queries.keys.values, ...), custom_call_target="tpu_custom_call" | custom-call | tf_op jit(solution)/shard_map/pallas_call | solution.py:1177
  107.5 19.9 %shard_map.546 = bf16[2,256,1024]{2,1,0:T(8,128)(2,1)} custom-call(bf16[8,256,256]{2,1,0:T(8,128)(2,1)} %bitcast.240), custom_call_target="tpu_custom_call" | custom-call | tf_op jit(solution)/shard_map/pallas_call | solution.py:860
  127.4 3.3 fusion.72
  134.8 3.3 convolution_convert_fusion.7.values
  141.3 13.0 %shard_map.548 = (bf16[256,1024]{1,0:T(8,128)(2,1)}, f32[256,128]{1,0:T(8,128)}, f32[256,128]{1,0:T(8,128)}) custom-call(s32[2]{0:T(128)} %length.3, bf16[256,1024]{1,0:T(8,128)(2,1)} %convolution_convert_fusion.9.queries, bf16[256,1024]{1,0:T(8,128)(2,1)} %convolution_convert_fusion.8.keys, bf16[256,1024]{1,0:T(8,128)(2,1)} %convolution_convert_fusion.7.values), custom_call_target="tpu_custom_call" | custom-call | tf_op jit(solution)/shard_map/pallas_call | solution.py:1320
  154.3 2.6 fusion.73
  160.3 15.3 %shard_map.547 = f32[512,1024]{1,0:T(8,128)} custom-call(bf16[512,1024]{1,0:T(8,128)(2,1)} %fusion.1.rows, bf16[8,1024,512]{2,1,0:T(8,128)(2,1)} %bitcast.228, bf16[8,512,1024]{2,1,0:T(8,128)(2,1)} %bitcast.229), custom_call_target="tpu_custom_call" | custom-call | tf_op jit(solution)/shard_map/pallas_call | solution.py:1432
  175.6 2.9 fusion.66
  179.8 2.2 convolution_convert_fusion.2.values
  182.0 2.2 convolution_convert_fusion.3.keys
  184.3 6.1 shard_map.549
  192.0 29.4 %shard_map.550 = (bf16[8,32,1024]{2,1,0:T(8,128)(2,1)}, f32[8,32,128]{2,1,0:T(8,128)}) custom-call(bf16[8,32,1024]{2,1,0:T(8,128)(2,1)} %bitcast.263, f32[8,2,32,128]{3,2,1,0:T(8,128)} %pad_maximum_fusion.3.stats), custom_call_target="tpu_custom_call" | custom-call | tf_op jit(solution)/shard_map/pallas_call | solution.py:1000
  221.4 2.6 fusion.74
  226.9 2.4 fusion.19
  229.3 18.7 %shard_map.551 = bf16[8,32,1024]{2,1,0:T(8,128)(2,1)} custom-call(f32[8,32,1024]{2,1,0:T(8,128)} %bitcast.252, bf16[8,512,1024]{2,1,0:T(8,128)(2,1)} %bitcast.223), custom_call_target="tpu_custom_call" | custom-call | tf_op jit(solution)/shard_map/pallas_call | solution.py:940
  254.5 1.9 convert_bitcast_fusion
  256.4 2.0 copy.95
  258.4 4.7 fusion.20.earlier
  263.1 18.7 %shard_map.552 = bf16[8,32,1024]{2,1,0:T(8,128)(2,1)} custom-call(f32[8,32,1024]{2,1,0:T(8,128)} %bitcast.239, f32[256,1024]{1,0:T(8,128)} %fusion.20.earlier), custom_call_target="tpu_custom_call" | custom-call | tf_op jit(solution)/shard_map/pallas_call | solution.py:940
  281.9 2.4 multiply_reduce_fusion.6
  287.4 11.9 %shard_map.553 = (f32[256,1024]{1,0:T(8,128)}, bf16[512,1024]{1,0:T(8,128)(2,1)}, bf16[512,1024]{1,0:T(8,128)(2,1)}) custom-call(s32[2]{0:T(128)} %broadcast_subtract_fusion.length, bf16[256,1024]{1,0:T(8,128)(2,1)} %convolution_convert_fusion.6.queries, bf16[512,1024]{1,0:T(8,128)(2,1)} %convolution_convert_fusion.3.keys, ...), custom_call_target="tpu_custom_call" | custom-call | tf_op jit(solution)/shard_map/pallas_call | solution.py:1384
  299.4 3.3 fusion.78
  309.5 18.6 %shard_map.554 = bf16[8,32,1024]{2,1,0:T(8,128)(2,1)} custom-call(f32[8,32,1024]{2,1,0:T(8,128)} %bitcast.254, bf16[512,1024]{1,0:T(8,128)(2,1)} %add_convert_fusion.2.earlier), custom_call_target="tpu_custom_call" | custom-call | tf_op jit(solution)/shard_map/pallas_call | solution.py:940
  328.4 3.7 multiply_reduce_fusion.7
  335.8 10.4 %shard_map.555 = (bf16[4,256,1024]{2,1,0:T(8,128)(2,1)}, bf16[4,256,1024]{2,1,0:T(8,128)(2,1)}) custom-call(s32[8]{0:T(128)} %broadcast_xor_fusion.order, bf16[32,2,32,1024]{3,2,1,0:T(8,128)(2,1)} %bitcast.220, bf16[512,1024]{1,0:T(8,128)(2,1)} %copy-done.18, bf16[512,1024]{1,0:T(8,128)(2,1)} %get-tuple-element.77.refs_0_, ...), custom_call_target="tpu_custom_call" | custom-call | tf_op jit(solution)/shard_map/pallas_call | solution.py:1468
  346.2 10.1 %shard_map.556 = (f32[256,1024]{1,0:T(8,128)}, bf16[256,1024]{1,0:T(8,128)(2,1)}, bf16[256,1024]{1,0:T(8,128)(2,1)}) custom-call(s32[2]{0:T(128)} %length.3, bf16[256,1024]{1,0:T(8,128)(2,1)} %convolution_convert_fusion.9.queries, bf16[256,1024]{1,0:T(8,128)(2,1)} %convolution_convert_fusion.8.keys, bf16[256,1024]{1,0:T(8,128)(2,1)} %convolution_convert_fusion.7.values, ...), custom_call_target="tpu_custom_call" | custom-call | tf_op jit(solution)/shard_map/pallas_call | solution.py:1384
  357.8 2.0 fusion.7
  371.9 31.1 %shard_map.557 = (bf16[8,512,1024]{2,1,0:T(8,128)(2,1)}, bf16[1024,1024]{1,0:T(8,128)(2,1)}) custom-call(bf16[8,512,1024]{2,1,0:T(8,128)(2,1)} %bitcast.224, bf16[8,512,1024]{2,1,0:T(8,128)(2,1)} %bitcast.227, bf16[1024,512]{1,0:T(8,128)(2,1)} %expand.2, bf16[512,1024]{1,0:T(8,128)(2,1)} %contract.2, bf16[256,1024]{1,0:T(8,128)(2,1)} %copy-done.20), custom_call_target="tpu_custom_call" | custom-call | tf_op jit(solution)/shard_map/pallas_call | solution.py:1538
  405.8 2.5 copy.97
  408.4 2.7 pad_maximum_fusion.weights
  412.5 2.0 copy.117
  421.6 44.7 %shard_map.558 = f32[512,1024]{1,0:T(8,128)} custom-call(bf16[8,512,1024]{2,1,0:T(8,128)(2,1)} %get-tuple-element.84.terms), custom_call_target="tpu_custom_call" | custom-call | tf_op jit(solution)/shard_map/pallas_call | solution.py:818
  466.4 3.2 multiply_reduce_fusion.1
  472.8 8.0 %shard_map.561 = (bf16[4,128,1024]{2,1,0:T(8,128)(2,1)}, bf16[4,128,1024]{2,1,0:T(8,128)(2,1)}) custom-call(s32[8]{0:T(128)} %broadcast_xor_fusion.order, bf16[512,1024]{1,0:T(8,128)(2,1)} %add_convert_fusion.1.earlier.refs_0_, bf16[512,1024]{1,0:T(8,128)(2,1)} %bitcast.236, bf16[512,1024]{1,0:T(8,128)(2,1)} %add_convert_fusion.1.earlier.refs_0_), custom_call_target="tpu_custom_call" | custom-call | tf_op jit(solution)/shard_map/pallas_call | solution.py:1468
  480.8 3.9 convolution_convert_fusion.1
  484.7 15.6 %shard_map.559.earlier = bf16[8,256,256]{2,1,0:T(8,128)(2,1)} custom-call(bf16[2,256,1024]{2,1,0:T(8,128)(2,1)} %bitcast.255), custom_call_target="tpu_custom_call" | custom-call | tf_op jit(solution)/shard_map/pallas_call | solution.py:898
  500.4 4.2 shard_map.563
  514.8 2.4 bitcast_reduce_fusion
  518.2 2.9 shard_map.562
  525.4 2.4 collective-permute-done.6
  528.6 1.9 fusion.22
  532.6 58.7 %shard_map.560.grads.earlier = bf16[2048,768]{1,0:T(8,128)(2,1)} custom-call(s32[1]{0:T(128)} %dynamic_slice.54.length, bf16[2048,768]{1,0:T(8,128)(2,1)} %convolution_convert_fusion.queries.keys.values, bf16[2048,256]{1,0:T(8,128)(2,1)} %bitcast.225, f32[4,2048]{1,0:T(4,128)} %slice_bitcast_fusion.1.logsum, f32[4,2048]{1,0:T(4,128)} %bitcast.264, ...), custom_call_target="tpu_custom_call" | custom-call | tf_op jit(solution)/shard_map/pallas_call | solution.py:1248
  591.2 10.8 %shard_map.566 = (f32[1024,512]{1,0:T(8,128)}, f32[512,1024]{1,0:T(8,128)}) custom-call(bf16[32,2,32,1024]{3,2,1,0:T(8,128)(2,1)} %bitcast.221, bf16[32,2,32,1024]{3,2,1,0:T(8,128)(2,1)} %bitcast.222, bf16[1024,512]{1,0:T(8,128)(2,1)} %expand.3, bf16[512,1024]{1,0:T(8,128)(2,1)} %contract.3, bf16[2048,768]{1,0:T(8,128)(2,1)} %shard_map.560.grads.earlier), custom_call_target="tpu_custom_call" | custom-call | tf_op jit(solution)/shard_map/pallas_call | solution.py:1587
  612.4 76.3 %shard_map.564 = (f32[2,256,1024]{2,1,0:T(8,128)}, f32[448,1024]{1,0:T(8,128)}, f32[384,1024]{1,0:T(8,128)}) custom-call(bf16[2048,1024]{1,0:T(8,128)(2,1)} %bitcast.234, bf16[2048,768]{1,0:T(8,128)(2,1)} %shard_map.560.grads.earlier, bf16[1024,768]{1,0:T(8,128)(2,1)} %pad_maximum_fusion.weights, bf16[8,16,768]{2,1,0:T(8,128)(2,1)} %pad.9.vectors, ...), custom_call_target="tpu_custom_call" | custom-call | tf_op jit(solution)/shard_map/pallas_call | solution.py:1117
  690.5 2.9 copy.116
  696.4 5.5 shard_map.565
  (306 shorter events, 107.2 us)
Async XLA Ops:
  7.2 172.6 %copy-start = (bf16[1024,1024]{1,0:T(8,128)(2,1)S(1)}, bf16[1024,1024]{1,0:T(8,128)(2,1)}, u32[]{:S(2)}) copy-start(bf16[1024,1024]{1,0:T(8,128)(2,1)} %param.55) | copy-start | bytes 6291460
  7.3 153.0 %all-gather.17.cloned.1.call-start = ((), (), s32[]{:S(2)}) async-start(), calls=%async_computation.6 | async-start | bytes 9437184 | tf_op jit(solution)/shard_map/all_gather | solution.py:1709
  8.0 152.3 %all-gather.19.cloned.1.call-start = ((), (), s32[]{:S(2)}) async-start(), calls=%async_computation.7 | async-start | bytes 9437184 | tf_op jit(solution)/shard_map/all_gather | solution.py:1710
  8.7 220.6 %all-gather.21.cloned.1.call-start = ((), (), s32[]{:S(2)}) async-start(), calls=%async_computation.8 | async-start | bytes 9437184 | tf_op jit(solution)/shard_map/all_gather | solution.py:1726
  107.5 19.9 %copy-start.28 = (bf16[256,2,1024]{2,0,1:T(8,128)(2,1)S(1)}, bf16[256,2,1024]{2,0,1:T(8,128)(2,1)}, u32[]{:S(2)}) copy-start(bf16[256,2,1024]{2,0,1:T(8,128)(2,1)} %copy.121) | copy-start | bytes 3145732
  133.3 202.4 %all-gather.25.cloned.1.call-start = ((), (), s32[]{:S(2)}) async-start(), calls=%async_computation.10 | async-start | bytes 4325376 | tf_op jit(solution)/shard_map/all_gather | solution.py:1766
  134.8 4.9 copy-start.33
  134.8 3.3 copy-start.42
  154.2 3.5 copy-start.63
  154.3 3.5 copy-start.68
  254.4 117.5 %all-gather.23.cloned.1.call-start = ((), (), s32[]{:S(2)}) async-start(), calls=%async_computation.9 | async-start | bytes 9437184 | tf_op jit(solution)/shard_map/all_gather | solution.py:1788
  299.3 3.4 copy-start.3
  299.3 3.4 copy-start.22
  299.4 3.4 copy-start.31
  305.4 3.5 copy-start.56
  305.4 3.5 copy-start.57
  307.0 113.4 %reduce-scatter.5.cloned.1.call-start = ((), (), s32[]{:S(2)}) async-start(), calls=%async_computation.4 | async-start | bytes 2129920 | tf_op jit(solution)/shard_map/reduce_scatter | solution.py:1768
  307.0 21.3 %copy-start.15 = (f32[256,1024]{1,0:T(8,128)S(1)}, f32[256,1024]{1,0:T(8,128)}, u32[]{:S(2)}) copy-start(f32[256,1024]{1,0:T(8,128)} %copy-done.14) | copy-start | bytes 3145732
  356.4 3.4 copy-start.40
  356.4 5.2 copy-start.39
  357.8 9.3 %copy-start.20 = (bf16[256,1024]{1,0:T(8,128)(2,1)}, bf16[256,1024]{1,0:T(8,128)(2,1)S(1)}, u32[]{:S(2)}) copy-start(bf16[256,1024]{1,0:T(8,128)(2,1)S(1)} %convert_element_type.323.earlier) | copy-start | bytes 1572868
  357.8 7.4 %copy-start.26 = (bf16[8,32,1024]{2,1,0:T(8,128)(2,1)S(1)}, bf16[8,32,1024]{2,1,0:T(8,128)(2,1)}, u32[]{:S(2)}) copy-start(bf16[8,32,1024]{2,1,0:T(8,128)(2,1)} %shard_map.554) | copy-start | bytes 1572868
  370.2 136.0 %reduce-scatter.3.cloned.1.call-start = ((), (), s32[]{:S(2)}) async-start(), calls=%async_computation.2 | async-start | bytes 2621440 | tf_op jit(solution)/shard_map/reduce_scatter | solution.py:1768
  403.0 293.4 %all-gather.15.cloned.1.call-start = ((), (), s32[]{:S(2)}) async-start(), calls=%async_computation.5 | async-start | bytes 2129920 | tf_op jit(solution)/shard_map/all_gather | solution.py:1769
  404.4 4.0 copy-start.46
  408.3 4.2 copy-start.19
  408.3 8.1 %copy-start.21 = (bf16[256,1024]{1,0:T(8,128)(2,1)S(1)}, bf16[256,1024]{1,0:T(8,128)(2,1)}, u32[]{:S(2)}) copy-start(bf16[256,1024]{1,0:T(8,128)(2,1)} %copy-done.20) | copy-start | bytes 1572868
  408.4 8.1 %copy-start.38 = (bf16[1024,1024]{1,0:T(8,128)(2,1)S(1)}, bf16[1024,1024]{1,0:T(8,128)(2,1)}, u32[]{:S(2)}) copy-start(bf16[1024,1024]{1,0:T(8,128)(2,1)} %param.47) | copy-start | bytes 6291460
  416.1 84.3 %collective-permute-start.5 = (bf16[4,256,1024]{2,1,0:T(8,128)(2,1)}, bf16[4,256,1024]{2,1,0:T(8,128)(2,1)}, u32[]{:S(2)}, u32[]{:S(2)}) collective-permute-start(bf16[4,256,1024]{2,1,0:T(8,128)(2,1)} %get-tuple-element.82.earlier), channel_id=1, source_target_pairs={{0,1},{1,0},{2,3},{3,2},{4,5},{5,4},{6,7},{7,6},{8,9},{9,8},{10,11... | collective-permute-start | bytes 6291464 | tf_op jit(solution)/shard_map/ppermute | solution.py:1611
  420.4 276.0 %all-gather.13.cloned.1.call-start = ((), (), s32[]{:S(2)}) async-start(), calls=%async_computation.3 | async-start | bytes 2621440 | tf_op jit(solution)/shard_map/all_gather | solution.py:1769
  421.6 44.7 %copy-start.5 = (f32[512,1024]{1,0:T(8,128)S(1)}, f32[512,1024]{1,0:T(8,128)}, u32[]{:S(2)}) copy-start(f32[512,1024]{1,0:T(8,128)} %copy-done.4) | copy-start | bytes 6291460
  472.8 8.0 %copy-start.17 = (bf16[512,1024]{1,0:T(8,128)(2,1)S(1)}, bf16[512,1024]{1,0:T(8,128)(2,1)}, u32[]{:S(2)}) copy-start(bf16[512,1024]{1,0:T(8,128)(2,1)} %add_convert_fusion.1.earlier.refs_0_) | copy-start | bytes 3145732
  500.2 17.0 %collective-permute-start = (bf16[4,128,1024]{2,1,0:T(8,128)(2,1)}, bf16[4,128,1024]{2,1,0:T(8,128)(2,1)S(1)}, u32[]{:S(2)}, u32[]{:S(2)}) collective-permute-start(bf16[4,128,1024]{2,1,0:T(8,128)(2,1)} %get-tuple-element.87), channel_id=1, source_target_pairs={{0,1},{1,0},{2,3},{3,2},{4,5},{5,4},{6,7},{7,6},{8,9},{9,8},{10,11... | collective-permute-start | bytes 3145736 | tf_op jit(solution)/shard_map/ppermute | solution.py:1611
  500.4 4.2 copy-start.11
  500.4 4.2 copy-start.29
  506.2 3.8 copy-start.23
  512.9 14.9 %collective-permute-start.6 = (bf16[2,128,1024]{2,1,0:T(8,128)(2,1)S(1)}, bf16[2,128,1024]{2,1,0:T(8,128)(2,1)}, u32[]{:S(2)}, u32[]{:S(2)}) collective-permute-start(bf16[2,128,1024]{2,1,0:T(8,128)(2,1)S(1)} %pad_maximum_fusion.2), channel_id=1, source_target_pairs={{0,2},{1,3},{2,0},{3,1},{4,6},{5,7},{6,4},{7,5},{8,10},{9,11},{10,... | collective-permute-start | bytes 1572872 | tf_op jit(solution)/shard_map/ppermute | solution.py:1611
  513.5 15.1 %collective-permute-start.8 = (bf16[2,128,1024]{2,1,0:T(8,128)(2,1)}, bf16[2,128,1024]{2,1,0:T(8,128)(2,1)}, u32[]{:S(2)}, u32[]{:S(2)}) collective-permute-start(bf16[2,128,1024]{2,1,0:T(8,128)(2,1)} %stack.82), channel_id=1, source_target_pairs={{0,4},{1,5},{2,6},{3,7},{4,0},{5,1},{6,2},{7,3},{8,12},{9,13},{10,... | collective-permute-start | bytes 1572872 | tf_op jit(solution)/shard_map/ppermute | solution.py:1611
  518.2 10.4 %copy-start.24 = (bf16[4,256,1024]{2,1,0:T(8,128)(2,1)S(1)}, bf16[4,256,1024]{2,1,0:T(8,128)(2,1)}, u32[]{:S(2)}) copy-start(bf16[4,256,1024]{2,1,0:T(8,128)(2,1)} %shard_map.563) | copy-start | bytes 6291460
  523.1 79.6 %collective-permute-start.1 = (bf16[2,64,1024]{2,1,0:T(8,128)(2,1)S(1)}, bf16[2,64,1024]{2,1,0:T(8,128)(2,1)}, u32[]{:S(2)}, u32[]{:S(2)}) collective-permute-start(bf16[2,64,1024]{2,1,0:T(8,128)(2,1)S(1)} %pad_maximum_fusion.4), channel_id=1, source_target_pairs={{0,2},{1,3},{2,0},{3,1},{4,6},{5,7},{6,4},{7,5},{8,10},{9,11},{10,... | collective-permute-start | bytes 786440 | tf_op jit(solution)/shard_map/ppermute | solution.py:1611
  523.9 78.9 %collective-permute-start.3 = (bf16[2,64,1024]{2,1,0:T(8,128)(2,1)S(1)}, bf16[2,64,1024]{2,1,0:T(8,128)(2,1)}, u32[]{:S(2)}, u32[]{:S(2)}) collective-permute-start(bf16[2,64,1024]{2,1,0:T(8,128)(2,1)S(1)} %stack.81), channel_id=1, source_target_pairs={{0,4},{1,5},{2,6},{3,7},{4,0},{5,1},{6,2},{7,3},{8,12},{9,13},{10,... | collective-permute-start | bytes 786440 | tf_op jit(solution)/shard_map/ppermute | solution.py:1611
  530.6 75.4 %collective-permute-start.7 = (bf16[128,1024]{1,0:T(8,128)(2,1)}, bf16[128,1024]{1,0:T(8,128)(2,1)}, u32[]{:S(2)}, u32[]{:S(2)}) collective-permute-start(bf16[128,1024]{1,0:T(8,128)(2,1)} %get-tuple-element.137), channel_id=1, source_target_pairs={{0,4},{1,5},{2,6},{3,7},{4,0},{5,1},{6,2},{7,3},{8,12},{9,13},{10,... | collective-permute-start | bytes 786440 | tf_op jit(solution)/shard_map/ppermute | solution.py:1611
  531.9 74.1 %collective-permute-start.9 = (bf16[128,1024]{1,0:T(8,128)(2,1)S(1)}, bf16[128,1024]{1,0:T(8,128)(2,1)}, u32[]{:S(2)}, u32[]{:S(2)}) collective-permute-start(bf16[128,1024]{1,0:T(8,128)(2,1)S(1)} %get-tuple-element.138), channel_id=1, source_target_pairs={{0,2},{1,3},{2,0},{3,1},{4,6},{5,7},{6,4},{7,5},{8,10},{9,11},{10,... | collective-permute-start | bytes 786440 | tf_op jit(solution)/shard_map/ppermute | solution.py:1611
  591.2 11.5 %copy-start.30 = (bf16[4,128,1024]{2,1,0:T(8,128)(2,1)S(1)}, bf16[4,128,1024]{2,1,0:T(8,128)(2,1)}, u32[]{:S(2)}) copy-start(bf16[4,128,1024]{2,1,0:T(8,128)(2,1)} %shard_map.562) | copy-start | bytes 3145732
  603.8 5.0 collective-permute-start.2
  605.4 5.0 collective-permute-start.4
  612.4 76.3 %copy-start.9 = (f32[512,1024]{1,0:T(8,128)S(1)}, f32[512,1024]{1,0:T(8,128)}, u32[]{:S(2)}) copy-start(f32[512,1024]{1,0:T(8,128)} %copy-done.8) | copy-start | bytes 6291460
  695.2 7.9 %copy-start.1 = (bf16[1024,1024]{1,0:T(8,128)(2,1)S(1)}, bf16[1024,1024]{1,0:T(8,128)(2,1)}, u32[]{:S(2)}) copy-start(bf16[1024,1024]{1,0:T(8,128)(2,1)} %param.55) | copy-start | bytes 6291460
  (45 other events, 76.8 us)
Sparse Core Ops, SparseCore 0:
  10.0 76.6 all-gather.16
  88.6 58.9 all-gather.18
  150.0 62.6 all-gather.20
  254.6 61.9 all-gather.24
  318.9 53.0 all-gather.22
  374.1 37.3 reduce-scatter.4
  414.4 42.9 reduce-scatter.2
  459.0 38.4 all-gather.14
  506.4 45.9 all-gather.12

commit v3 on v2

--- a/solution.py
+++ b/solution.py
@@ -558,6 +558,9 @@
     return (left.astype(wide) + right.astype(wide)).astype(low)
 
 
+OWNERS = (3, 5, 7, 1, 2, 4, 6, 0)
+
+
 def nt(left, right):
     return lax.dot_general(left, right, (((1,), (1,)), ((), ())), preferred_element_type=wide)
 
@@ -759,7 +762,7 @@
     )(rows, extra)
 
 
-def scatter_plane_kernel(terms, out, sib, pair, came, far, came_far, send, recv, send_pair, recv_pair, send_far, recv_far):
+def scatter_plane_kernel(terms, pairs, expand, contract, out, d_expand, d_contract, sib, pair, came, far, came_far, send, recv, send_pair, recv_pair, send_far, recv_far):
     me = lax.axis_index("seq")
     half = out.shape[0] // 2
     greet((1, 2, 4))
@@ -794,6 +797,12 @@
         if mask == 4:
             pair[3] = both(4, 2, halves[1]).astype(low)
             pair_copy(3).start()
+    x = pairs[:, 0].reshape(-1, pairs.shape[3])
+    g = pairs[:, 1].reshape(-1, pairs.shape[3])
+    act, slope = gelu_parts(nn(x, expand[...]))
+    d_hidden = (nt(g, contract[...]) * slope).astype(low)
+    d_expand[...] = tn(x, d_hidden)
+    d_contract[...] = tn(act.astype(low), g)
     for side in range(2):
         pair_copy(side).wait_recv()
         mask, slot = ((4, 2), (2, 1))[side]
@@ -813,13 +822,17 @@
         far_copy(side).wait_send()
 
 
-def scatter_plane(terms):
+def scatter_plane(terms, pairs, expand, contract):
     _, rows, width = terms.shape
     return pl.pallas_call(
         scatter_plane_kernel,
-        out_shape=jax.ShapeDtypeStruct((rows, width), wide),
-        in_specs=[vmem_spec()],
-        out_specs=vmem_spec(),
+        out_shape=(
+            jax.ShapeDtypeStruct((rows, width), wide),
+            jax.ShapeDtypeStruct(expand.shape, wide),
+            jax.ShapeDtypeStruct(contract.shape, wide),
+        ),
+        in_specs=[vmem_spec()] * 4,
+        out_specs=(vmem_spec(),) * 3,
         scratch_shapes=[
             pltpu.VMEM((4, rows, width), low),
             pltpu.VMEM((4, rows // 2, width), low),
@@ -830,7 +843,7 @@
         + [pltpu.SemaphoreType.DMA((4,))] * 4
         + [pltpu.SemaphoreType.DMA((2,))] * 2,
         compiler_params=params(9),
-    )(terms)
+    )(terms, pairs, expand, contract)
 
 
 def heads_to_rows_kernel(blocks, out, send, recv, keep):
@@ -871,7 +884,7 @@
     )(blocks)
 
 
-def rows_to_heads_kernel(rows, out, send, recv, keep):
+def rows_to_heads_kernel(rows, left, right, out, away, kept, send, recv, keep):
     me = lax.axis_index("seq")
     width = out.shape[2]
     greet(PEERS)
@@ -886,6 +899,10 @@
         copy = remote(part(me ^ mask), out.at[me], send.at[mask], recv.at[mask], me ^ mask)
         copy.start()
         started.append(copy)
+    size = left.shape[1] // 8
+    for place, mask in enumerate(OWNERS):
+        columns = pl.ds(pl.multiple_of((me ^ mask) * size, size), size)
+        (away, kept)[place // 4][place % 4] = tn(left[:, columns], right[...]).astype(low)
     for mask in PEERS:
         remote(part(me), out.at[me ^ mask], send.at[mask], recv.at[mask], me ^ mask).wait_recv()
     for copy in started:
@@ -893,20 +910,21 @@
     local.wait()
 
 
-def rows_to_heads(rows):
+def rows_to_heads(rows, left, right):
     _, count, width = rows.shape
+    half = jax.ShapeDtypeStruct((4, width // 8, width), low)
     return pl.pallas_call(
         rows_to_heads_kernel,
-        out_shape=jax.ShapeDtypeStruct((8, count, width // 4), rows.dtype),
-        in_specs=[any_spec()],
-        out_specs=any_spec(),
+        out_shape=(jax.ShapeDtypeStruct((8, count, width // 4), rows.dtype), half, half),
+        in_specs=[any_spec(), vmem_spec(), vmem_spec()],
+        out_specs=(any_spec(), vmem_spec(), vmem_spec()),
         scratch_shapes=[
             pltpu.SemaphoreType.DMA((8,)),
             pltpu.SemaphoreType.DMA((8,)),
             pltpu.SemaphoreType.DMA,
         ],
         compiler_params=params(3),
-    )(rows)
+    )(rows, left, right)
 
 
 def sum_small_kernel(terms, earlier, out, mine, came, send, recv, send_back, recv_back):
@@ -1013,7 +1031,7 @@
 
 
 def finish_kernel(
-    size, rows, grads, weights, vectors, joined, out, out_line, out_joined,
+    size, rows, grads, weights, vectors, joined, feed, middle, out, out_line, out_joined, out_turned, out_straight, out_middle,
     terms, sib, pair, came, blocks, came_blocks, line,
     send, recv, send_pair, recv_pair, send_block, recv_block,
     line_came, line_sent, send_line, recv_line, join_came, join_sent, send_join, recv_join,
@@ -1036,15 +1054,16 @@
             blocks.at[me ^ mask], came_blocks.at[mask], send_block.at[mask], recv_block.at[mask], me ^ mask
         )
 
-    for mask in PEERS + (0,):
-        owner = me ^ mask
-        columns = pl.ds(pl.multiple_of(owner * cut, cut), cut)
-        blocks[owner, :cut] = tn(rows[:, columns], d).astype(low)
-        blocks[owner, cut:] = vectors[owner]
+    for mask in (6, 2, 4, 0):
+        first = ((me ^ mask) // 2) * 2
+        columns = pl.ds(pl.multiple_of(first * cut, 2 * cut), 2 * cut)
+        both = tn(rows[:, columns], d).astype(low)
+        for place in range(2):
+            blocks[first + place, :cut] = both[place * cut : (place + 1) * cut]
+            blocks[first + place, cut:] = vectors[first + place]
         if mask:
             block_copy(mask).start()
-    for number in range(3):
-        other.step(number)
+        block_copy(mask + 1).start()
     chips = (6, 2, 4, 0)
 
     def term(owner):
@@ -1059,7 +1078,6 @@
     for slot, mask in enumerate(chips):
         terms[slot] = term(me ^ 1 ^ mask).astype(low)
         sib_copy(slot).start()
-    other.rest(3)
     for slot, mask in enumerate(chips):
         here = term(me ^ mask)
         sib_copy(slot).wait_recv()
@@ -1069,6 +1087,13 @@
             pair_copy(slot).start()
         else:
             out[mine] = here
+
+    other.rest(0)
+
+    half = out_straight.shape[0]
+    out_turned[...] = feed[:half].astype(wide).T
+    out_straight[...] = feed[half:].astype(wide)
+    out_middle[...] = middle[...].astype(wide)
 
     for mask in PEERS:
         block_copy(mask).wait_recv()
@@ -1107,7 +1132,7 @@
     other.end()
 
 
-def finish(rows, grads, weights, vectors, joined):
+def finish(rows, grads, weights, vectors, joined, feed, middle):
     width = rows.shape[1]
     count = rows.shape[0] // 8
     cut = width // 8
@@ -1120,9 +1145,12 @@
             jax.ShapeDtypeStruct((2, count, width), wide),
             jax.ShapeDtypeStruct(line, wide),
             jax.ShapeDtypeStruct(joined.shape, wide),
+            jax.ShapeDtypeStruct((width, feed.shape[0] // 2), wide),
+            jax.ShapeDtypeStruct((feed.shape[0] // 2, width), wide),
+            jax.ShapeDtypeStruct(middle.shape, wide),
         ),
-        in_specs=[vmem_spec()] * 5,
-        out_specs=(vmem_spec(),) * 3,
+        in_specs=[vmem_spec()] * 7,
+        out_specs=(vmem_spec(),) * 6,
         scratch_shapes=[
             pltpu.VMEM((4, count, width), low),
             pltpu.VMEM((4, count, width), low),
@@ -1140,17 +1168,18 @@
         + line_scratch(line, 7)
         + line_scratch(joined.shape, 4),
         compiler_params=params(6),
-    )(rows, grads, weights, vectors, joined)
+    )(rows, grads, weights, vectors, joined, feed, middle)
 
 
 def plain(**more):
     return pltpu.CompilerParams(vmem_limit_bytes=VMEM_BYTES, **more)
 
 
-def flash_forward_kernel(length, queries, keys, values, context, logsum):
+def flash_forward_kernel(length, queries, keys, values, context, logsum, scores, probs):
     rows, width = queries.shape
     count = keys.shape[0]
     heads = width // 64
+    strip = 16
     of_head = lane_head((1, width), 64)
     q = queries[...] * jnp.asarray(0.125, low)
     k = keys[...]
@@ -1160,13 +1189,18 @@
     lanes = lax.broadcasted_iota(jnp.int32, (1, 128), 1)
     fill = jnp.where(lax.broadcasted_iota(jnp.int32, (1, count), 1) < length[0], 0.0, masked_fill)
     for head in range(heads):
-        scores = nt(jnp.where(of_head == head, q, jnp.zeros_like(q)), k) + fill
-        top = jnp.max(scores, -1, keepdims=True)
-        weights = jnp.exp(scores - top)
-        summed = jnp.sum(weights, -1, keepdims=True)
-        probs = (weights * (1.0 / summed)).astype(low)
-        part = nn(probs, v)
-        total = jnp.where(of_head == head, part, total)
+        slot = head % 2
+        scores[slot] = nt(jnp.where(of_head == head, q, jnp.zeros_like(q)), k)
+        tops, sums = [], []
+        for start in range(0, rows, strip):
+            part = scores[slot, start : start + strip] + fill
+            top = jnp.max(part, -1, keepdims=True)
+            weights = jnp.exp(part - top)
+            tops.append(top)
+            sums.append(jnp.sum(weights, -1, keepdims=True))
+            probs[slot, start : start + strip] = weights.astype(low)
+        top, summed = jnp.concatenate(tops, 0), jnp.concatenate(sums, 0)
+        total = jnp.where(of_head == head, nn(probs[slot], v) * (1.0 / summed), total)
         logs = jnp.where(lanes == head, top + jnp.log(summed), logs)
     context[...] = total.astype(low)
     logsum[...] = logs
@@ -1192,6 +1226,7 @@
                 pl.BlockSpec((block, width), lambda i, n: (i, 0)),
                 pl.BlockSpec((block, 128), lambda i, n: (i, 0)),
             ],
+            scratch_shapes=[pltpu.VMEM((2, block, count), wide), pltpu.VMEM((2, block, count), low)],
         ),
         compiler_params=plain(),
     )(length, three, three, three)
@@ -1482,30 +1517,6 @@
     )(order, earlier, rows, *grads)
 
 
-def widen_kernel(feed, later, earlier, *outs):
-    half = outs[1].shape[0]
-    outs[0][...] = feed[:half].astype(wide).T
-    outs[1][...] = feed[half:].astype(wide)
-    start = 0
-    for out in outs[2:]:
-        out[...] = later[start : start + out.shape[0]].astype(wide)
-        start += out.shape[0]
-
-
-def widen_after(feed, later, heights, earlier):
-    width = feed.shape[1]
-    half = feed.shape[0] // 2
-    shapes = [jax.ShapeDtypeStruct((width, half), wide), jax.ShapeDtypeStruct((half, width), wide)]
-    shapes += [jax.ShapeDtypeStruct((height, width), wide) for height in heights]
-    return pl.pallas_call(
-        widen_kernel,
-        out_shape=tuple(shapes),
-        in_specs=[vmem_spec()] * 2 + [any_spec()],
-        out_specs=tuple(vmem_spec() for _ in shapes),
-        compiler_params=plain(),
-    )(feed, later, earlier)
-
-
 def feed_backward_kernel(rows, grads, expand, contract, earlier, out, d_both, expand_sum, contract_sum):
     step = pl.program_id(0)
     x = rows[0]
@@ -1553,58 +1564,6 @@
         scratch_shapes=[pltpu.VMEM((hidden, width), wide)] * 2,
         compiler_params=plain(),
     )(rows, grads, expand, contract, earlier)
-
-
-def feed_weights_kernel(rows, grads, expand, contract, earlier, d_expand, d_contract, expand_sum, contract_sum):
-    step = pl.program_id(0)
-    x = rows[...].reshape(-1, rows.shape[3])
-    g = grads[...].reshape(-1, rows.shape[3])
-    act, slope = gelu_parts(nn(x, expand[...]))
-    d_hidden = (nt(g, contract[...]) * slope).astype(low)
-    one = tn(d_hidden, x)
-    two = tn(act.astype(low), g)
-
-    @pl.when(step == 0)
-    def _():
-        expand_sum[...] = one
-        contract_sum[...] = two
-
-    @pl.when(step > 0)
-    def _():
-        expand_sum[...] += one
-        contract_sum[...] += two
-
-    @pl.when(step == pl.num_programs(0) - 1)
-    def _():
-        d_expand[...] = expand_sum[...].T
-        d_contract[...] = contract_sum[...]
-
-
-def feed_weights(both, expand, contract, earlier):
-    parts, _, count, width = both.shape
-    hidden = contract.shape[0]
-    block = (parts // 2, 1, count, width)
-    return pl.pallas_call(
-        feed_weights_kernel,
-        out_shape=(jax.ShapeDtypeStruct((width, hidden), wide), jax.ShapeDtypeStruct((hidden, width), wide)),
-        grid=(2,),
-        in_specs=[
-            pl.BlockSpec(block, lambda j: (j, 0, 0, 0)),
-            pl.BlockSpec(block, lambda j: (j, 1, 0, 0)),
-            pl.BlockSpec((width, hidden), lambda j: (0, 0)),
-            pl.BlockSpec((hidden, width), lambda j: (0, 0)),
-            any_spec(),
-        ],
-        out_specs=[
-            pl.BlockSpec((width, hidden), lambda j: (0, 0)),
-            pl.BlockSpec((hidden, width), lambda j: (0, 0)),
-        ],
-        scratch_shapes=[pltpu.VMEM((hidden, width), wide)] * 2,
-        compiler_params=plain(),
-    )(both, both, expand, contract, earlier)
-
-
-OWNERS = (3, 5, 7, 1, 2, 4, 6, 0)
 
 
 def swap(array, mask):
@@ -1716,7 +1675,7 @@
     w_three = jnp.concatenate([columns(encoder_query), columns(encoder_key), columns(encoder_value)], 1)
     length = lax.dynamic_slice_in_dim(source_lengths, me // 4, 1, 0)
     three = project(rows, w_three).astype(low)
-    context, logsum = flash_forward(length, three, 256)
+    context, logsum = flash_forward(length, three, 512)
     encoder_context = heads_to_rows(context.reshape(8, slots, quarter)).reshape(-1, width)
     first, first_back = jax.vjp(
         layer_norm, source_flat.astype(wide) + project(encoder_context, encoder_mix), attend_gain, attend_shift
@@ -1845,33 +1804,35 @@
     d_terms, feed_join = feed_backward(first_all, d_all, encoder_expand, encoder_contract, dq_self)
     feed_sum = over_tables(feed_join)
     cross_both = scatter_cores(cross_away, cross_kept, feed_join)
-    d_rows = scatter_plane(d_terms)
+    d_rows, grad_decoder_expand, grad_decoder_contract = scatter_plane(
+        d_terms, decoder_pair, decoder_expand, decoder_contract
+    )
     d_first, grad_attend_gain, grad_attend_shift = first_back(d_second + d_rows)
     encoder_low = d_first.astype(low)
-    mix_away, mix_kept = outer_by_owner(order, encoder_low, encoder_context, encoder_low)
-    d_context = rows_to_heads(project_back(encoder_low, encoder_mix).astype(low).reshape(tables, slots, width))
+    d_context, mix_away, mix_kept = rows_to_heads(
+        project_back(encoder_low, encoder_mix).astype(low).reshape(tables, slots, width), encoder_context, encoder_low
+    )
     mix_both = scatter_cores(mix_away, mix_kept, d_context)
     d_context = d_context.reshape(-1, quarter)
     delta = jnp.sum(
         (d_context.astype(wide) * context.astype(wide)).reshape(-1, quarter // 64, 64), -1
     )
-    d_three = flash_backward(length, three, d_context, logsum[:, : quarter // 64].T, delta.T, 256, 512)
+    d_three = flash_backward(length, three, d_context, logsum[:, : quarter // 64].T, delta.T, 512, 1024)
     vectors = jnp.stack(
         [grad_attend_gain, grad_attend_shift, grad_encoder_gain, grad_encoder_shift], 0
     ).astype(low)
     vectors = jnp.swapaxes(vectors.reshape(4, 8, slice_rows), 0, 1)
     vectors = jnp.pad(vectors, ((0, 0), (0, 12), (0, 3 * quarter - slice_rows)))
     parts = scatter_second(scatter_first(mix_both)) + scatter_second(scatter_first(cross_both))
-    d_source, line, plane_sum = finish(rows, d_three, w_three, vectors, join(parts))
-    grad_decoder_expand, grad_decoder_contract = feed_weights(
-        decoder_pair, decoder_expand, decoder_contract, d_three
+    d_source, line, plane_sum, grad_encoder_expand, grad_encoder_contract, middle_wide = finish(
+        rows, d_three, w_three, vectors, join(parts), feed_sum, middle_sum
     )
     grad_source = unflat(d_first + d_source.reshape(-1, width))
     encoder_three = line[: 3 * slice_rows].reshape(3, slice_rows, width)
     encoder_vectors = line[3 * slice_rows : 3 * slice_rows + 4, :slice_rows]
     plane_three = plane_sum.reshape(3, slice_rows, width)
-    sums = widen_after(feed_sum, middle_sum, [part.shape[0] for part in middle], line)
-    grad_encoder_expand, grad_encoder_contract, *six, decoder_vectors = sums
+    six = middle_wide[: 6 * slice_rows].reshape(6, slice_rows, width)
+    decoder_vectors = middle_wide[6 * slice_rows : 6 * slice_rows + 1]
     decoder_vectors = decoder_vectors[0, : 6 * slice_rows].reshape(6, slice_rows)
     return (
         unflat(encoded),

time: 720 us -> 707 us (0.982)
  Pallas kernels: 515 us -> 496 us
  local copies, waits for them, and re-layouts: 48.9 us -> 61.9 us
    pallas_call x4 -> x2, Pallas kernels: 76.6 us -> 66 us  [the longest x1 48.1 us: scatter_plane(): pl.pallas_call(scatter_plane_kernel, out_shape=(jax.ShapeDtypeStruct((row...]
    pallas_call x1, Pallas kernels: 58.7 us -> 49.1 us  [flash_backward(): pl.pallas_call(functools.partial(flash_backward_kernel, chunk), out_shape...]
    pallas_call x1, Pallas kernels: 29.4 us -> 37.7 us  [merge_parts(): pl.pallas_call(merge_parts_kernel, out_shape=(jax.ShapeDtypeStruct((8, ro...]
    unnamed x153 -> x165, local copies, waits for them, and re-layouts: 15.8 us -> 23.9 us
    pallas_call x2 -> x1, Pallas kernels: 18.5 us -> 10.5 us  [outer_by_owner(): pl.pallas_call(outer_kernel, out_shape=(shape, shape), grid_spec=pltpu.Pr...]
  transfers between devices with their start and end apart: 19 -> 19, of which waited for: 5 -> 5; matrix products, arithmetic and copies ran while one was open for 20% -> 19% of each run, Pallas kernels for 69% -> 57%
where the time goes in v3:
time: 707 us; the launch traced here: 701 us
  Pallas kernels  496 us (70%)
  matrix products  65.4 us (9%)
  local copies, waits for them, and re-layouts  61.9 us (9%)
  other arithmetic  45.3 us (6%)
  between operations  15.2 us (2%)
  starting transfers between devices  8.88 us (1%)
  waiting for transfers between devices  8.2 us (1%)
    pallas_call x1, Pallas kernels, finish(): pl.pallas_call(functools.partial(finish_kernel, lax.axis_size('dp')), out...  79.8 us
    pallas_call x3, Pallas kernels, sum_small(): pl.pallas_call(sum_small_kernel, out_shape=jax.ShapeDtypeStruct(blocks, l...  58.5 us
    pallas_call x1, Pallas kernels, flash_backward(): pl.pallas_call(functools.partial(flash_backward_kernel, chunk), out_shape...  49.1 us
    pallas_call x1, Pallas kernels, scatter_plane(): pl.pallas_call(scatter_plane_kernel, out_shape=(jax.ShapeDtypeStruct((row...  48.1 us
    pallas_call x1, Pallas kernels, gather_table(): pl.pallas_call(gather_table_kernel, out_shape=(jax.ShapeDtypeStruct((8,)...  48 us
    pallas_call x1, Pallas kernels, merge_parts(): pl.pallas_call(merge_parts_kernel, out_shape=(jax.ShapeDtypeStruct((8, ro...  37.7 us
    pallas_call x1, Pallas kernels, feed_backward(): pl.pallas_call(feed_backward_kernel, out_shape=(jax.ShapeDtypeStruct(rows...  31.1 us
    dot_general x12, matrix products, project(): return jnp.dot(rows, weight, preferred_element_type=jnp.float32)  31 us
  transfers between devices with their start and end apart: 19, of which 5 were waited for; matrix products, arithmetic and copies ran while one was open for 19% of the time, Pallas kernels for 57%

profile of v3, /device:TPU:0, one launch (start us, length us, event | category | flops | bytes accessed | tf_op | source)
XLA Modules:
  0.0 700.8 jit_solution(9383800541566438229)
XLA Ops:
  11.0 48.0 %shard_map.544 = (bf16[8,256,1024]{2,1,0:T(8,128)(2,1)}, bf16[8,64,1024]{2,1,0:T(8,128)(2,1)}) custom-call(bf16[2,256,1024]{2,1,0:T(8,128)(2,1)} %bitcast.236, bf16[64,1024]{1,0:T(8,128)(2,1)} %bitcast.261), custom_call_target="tpu_custom_call" | custom-call | tf_op jit(solution)/shard_map/pallas_call | solution.py:748
  63.3 7.3 %convolution_convert_fusion.queries.keys.values = bf16[2048,768]{1,0:T(8,128)(2,1)} fusion(bf16[2048,1024]{1,0:T(8,128)(2,1)} %bitcast.234, bf16[1024,256]{1,0:T(8,128)(2,1)S(1)} %get-tuple-element.174, bf16[1024,256]{1,0:T(8,128)(2,1)S(1)} %get-tuple-element.175, bf16[1024,256]{1,0:T(8,128)(2,1)S(1)} %constant_dynamic-slice_fusion.4), kind=kOutput, calls=%fused_computation | convolution fusion | flops 3227516928 | bytes 8912896 | tf_op jit(solution)/shard_map/dot_general | solution.py:29
  70.6 31.0 %shard_map.545 = (bf16[2048,256]{1,0:T(8,128)(2,1)}, f32[2048,128]{1,0:T(8,128)}) custom-call(s32[1]{0:T(128)} %dynamic_slice.54.length, bf16[2048,768]{1,0:T(8,128)(2,1)} %convolution_convert_fusion.queries.keys.values, bf16[2048,768]{1,0:T(8,128)(2,1)} %convolution_convert_fusion.queries.keys.values, ...), custom_call_target="tpu_custom_call" | custom-call | tf_op jit(solution)/shard_map/pallas_call | solution.py:1211
  101.6 20.1 %shard_map.546 = bf16[2,256,1024]{2,1,0:T(8,128)(2,1)} custom-call(bf16[8,256,256]{2,1,0:T(8,128)(2,1)} %bitcast.239), custom_call_target="tpu_custom_call" | custom-call | tf_op jit(solution)/shard_map/pallas_call | solution.py:873
  121.7 3.3 fusion.73
  129.3 3.2 convolution_convert_fusion.7.values
  135.7 13.2 %shard_map.548 = (bf16[256,1024]{1,0:T(8,128)(2,1)}, f32[256,128]{1,0:T(8,128)}, f32[256,128]{1,0:T(8,128)}) custom-call(s32[2]{0:T(128)} %length.3, bf16[256,1024]{1,0:T(8,128)(2,1)} %convolution_convert_fusion.9.queries, bf16[256,1024]{1,0:T(8,128)(2,1)} %convolution_convert_fusion.8.keys, bf16[256,1024]{1,0:T(8,128)(2,1)} %convolution_convert_fusion.7.values), custom_call_target="tpu_custom_call" | custom-call | tf_op jit(solution)/shard_map/pallas_call | solution.py:1355
  148.9 2.7 fusion.74
  155.0 15.7 %shard_map.547 = f32[512,1024]{1,0:T(8,128)} custom-call(bf16[512,1024]{1,0:T(8,128)(2,1)} %fusion.1.rows, bf16[8,1024,512]{2,1,0:T(8,128)(2,1)} %bitcast.227, bf16[8,512,1024]{2,1,0:T(8,128)(2,1)} %bitcast.228), custom_call_target="tpu_custom_call" | custom-call | tf_op jit(solution)/shard_map/pallas_call | solution.py:1467
  170.7 2.9 fusion.66
  174.9 2.2 convolution_convert_fusion.2.values
  177.1 2.2 convolution_convert_fusion.3.keys
  179.4 6.2 shard_map.549
  187.3 37.7 %shard_map.550 = (bf16[8,32,1024]{2,1,0:T(8,128)(2,1)}, f32[8,32,128]{2,1,0:T(8,128)}) custom-call(bf16[8,32,1024]{2,1,0:T(8,128)(2,1)} %bitcast.262, f32[8,2,32,128]{3,2,1,0:T(8,128)} %pad_maximum_fusion.3.stats), custom_call_target="tpu_custom_call" | custom-call | tf_op jit(solution)/shard_map/pallas_call | solution.py:1018
  225.1 2.6 fusion.75
  230.9 2.4 fusion.19
  233.3 18.6 %shard_map.551 = bf16[8,32,1024]{2,1,0:T(8,128)(2,1)} custom-call(f32[8,32,1024]{2,1,0:T(8,128)} %bitcast.252, bf16[8,512,1024]{2,1,0:T(8,128)(2,1)} %bitcast.220), custom_call_target="tpu_custom_call" | custom-call | tf_op jit(solution)/shard_map/pallas_call | solution.py:958
  258.5 1.9 convert_bitcast_fusion
  260.5 2.0 copy.95
  262.4 4.7 fusion.20.earlier
  267.2 19.1 %shard_map.552 = bf16[8,32,1024]{2,1,0:T(8,128)(2,1)} custom-call(f32[8,32,1024]{2,1,0:T(8,128)} %bitcast.238, f32[256,1024]{1,0:T(8,128)} %fusion.20.earlier), custom_call_target="tpu_custom_call" | custom-call | tf_op jit(solution)/shard_map/pallas_call | solution.py:958
  286.2 2.4 multiply_reduce_fusion.6
  291.8 11.7 %shard_map.553 = (f32[256,1024]{1,0:T(8,128)}, bf16[512,1024]{1,0:T(8,128)(2,1)}, bf16[512,1024]{1,0:T(8,128)(2,1)}) custom-call(s32[2]{0:T(128)} %broadcast_subtract_fusion.length, bf16[256,1024]{1,0:T(8,128)(2,1)} %convolution_convert_fusion.6.queries, bf16[512,1024]{1,0:T(8,128)(2,1)} %convolution_convert_fusion.3.keys, ...), custom_call_target="tpu_custom_call" | custom-call | tf_op jit(solution)/shard_map/pallas_call | solution.py:1419
  303.5 3.3 fusion.79
  313.7 20.8 %shard_map.554 = bf16[8,32,1024]{2,1,0:T(8,128)(2,1)} custom-call(f32[8,32,1024]{2,1,0:T(8,128)} %bitcast.254, bf16[512,1024]{1,0:T(8,128)(2,1)} %add_convert_fusion.2.earlier), custom_call_target="tpu_custom_call" | custom-call | tf_op jit(solution)/shard_map/pallas_call | solution.py:958
  334.5 3.7 multiply_reduce_fusion.7
  342.1 10.5 %shard_map.555 = (bf16[4,256,1024]{2,1,0:T(8,128)(2,1)}, bf16[4,256,1024]{2,1,0:T(8,128)(2,1)}) custom-call(s32[8]{0:T(128)} %broadcast_xor_fusion.order, bf16[32,2,32,1024]{3,2,1,0:T(8,128)(2,1)} %bitcast.222, bf16[512,1024]{1,0:T(8,128)(2,1)} %copy-done.16, bf16[512,1024]{1,0:T(8,128)(2,1)} %get-tuple-element.73.refs_0_, ...), custom_call_target="tpu_custom_call" | custom-call | tf_op jit(solution)/shard_map/pallas_call | solution.py:1503
  352.6 10.2 %shard_map.556 = (f32[256,1024]{1,0:T(8,128)}, bf16[256,1024]{1,0:T(8,128)(2,1)}, bf16[256,1024]{1,0:T(8,128)(2,1)}) custom-call(s32[2]{0:T(128)} %length.3, bf16[256,1024]{1,0:T(8,128)(2,1)} %convolution_convert_fusion.9.queries, bf16[256,1024]{1,0:T(8,128)(2,1)} %convolution_convert_fusion.8.keys, bf16[256,1024]{1,0:T(8,128)(2,1)} %convolution_convert_fusion.7.values, ...), custom_call_target="tpu_custom_call" | custom-call | tf_op jit(solution)/shard_map/pallas_call | solution.py:1419
  364.2 2.0 fusion.7
  376.6 31.1 %shard_map.557 = (bf16[8,512,1024]{2,1,0:T(8,128)(2,1)}, bf16[1024,1024]{1,0:T(8,128)(2,1)}) custom-call(bf16[8,512,1024]{2,1,0:T(8,128)(2,1)} %bitcast.221, bf16[8,512,1024]{2,1,0:T(8,128)(2,1)} %bitcast.226, bf16[1024,512]{1,0:T(8,128)(2,1)} %expand.2, bf16[512,1024]{1,0:T(8,128)(2,1)} %contract.2, bf16[256,1024]{1,0:T(8,128)(2,1)} %copy-done.18), custom_call_target="tpu_custom_call" | custom-call | tf_op jit(solution)/shard_map/pallas_call | solution.py:1549
  410.1 2.3 slice_bitcast_fusion
  412.3 3.4 reduce-scatter.5.cloned.1.call-done
  415.8 2.5 pad_maximum_fusion.weights
  418.3 2.7 copy.99.keys_t
  422.8 2.0 copy.117
  429.8 48.1 %shard_map.558 = (f32[512,1024]{1,0:T(8,128)}, f32[1024,512]{1,0:T(8,128)}, f32[512,1024]{1,0:T(8,128)}) custom-call(bf16[8,512,1024]{2,1,0:T(8,128)(2,1)} %get-tuple-element.80.terms, bf16[32,2,32,1024]{3,2,1,0:T(8,128)(2,1)} %bitcast.223, bf16[1024,512]{1,0:T(8,128)(2,1)} %expand.3, bf16[512,1024]{1,0:T(8,128)(2,1)} %contract.3), custom_call_target="tpu_custom_call" | custom-call | tf_op jit(solution)/shard_map/pallas_call | solution.py:827
  477.9 3.2 multiply_reduce_fusion.1
  481.1 1.9 fusion.60
  484.8 4.2 convolution_convert_fusion.1
  489.1 18.0 %shard_map.559 = (bf16[8,256,256]{2,1,0:T(8,128)(2,1)}, bf16[4,128,1024]{2,1,0:T(8,128)(2,1)}, bf16[4,128,1024]{2,1,0:T(8,128)(2,1)}) custom-call(bf16[2,256,1024]{2,1,0:T(8,128)(2,1)} %bitcast.251, bf16[512,1024]{1,0:T(8,128)(2,1)} %bitcast.233, bf16[512,1024]{1,0:T(8,128)(2,1)} %copy-done.26), custom_call_target="tpu_custom_call" | custom-call | tf_op jit(solution)/shard_map/pallas_call | solution.py:916
  507.3 4.2 shard_map.562
  511.5 2.0 stack.82
  522.7 2.9 shard_map.561
  530.2 1.9 fusion.22
  535.0 49.1 %shard_map.560.grads = bf16[2048,768]{1,0:T(8,128)(2,1)} custom-call(s32[1]{0:T(128)} %dynamic_slice.54.length, bf16[2048,768]{1,0:T(8,128)(2,1)} %convolution_convert_fusion.queries.keys.values, bf16[2048,256]{1,0:T(8,128)(2,1)} %bitcast.224, f32[4,2048]{1,0:T(4,128)} %slice_bitcast_fusion.1.logsum, f32[4,2048]{1,0:T(4,128)} %bitcast.263, ...), custom_call_target="tpu_custom_call" | custom-call | tf_op jit(solution)/shard_map/pallas_call | solution.py:1283
  593.6 79.8 %shard_map.563 = (f32[2,256,1024]{2,1,0:T(8,128)}, f32[448,1024]{1,0:T(8,128)}, f32[384,1024]{1,0:T(8,128)}, f32[1024,512]{1,0:T(8,128)}, f32[512,1024]{1,0:T(8,128)}, /*index=5*/f32[832,1024]{1,0:T(8,128)}) custom-call(bf16[2048,1024]{1,0:T(8,128)(2,1)} %bitcast.235, bf16[2048,768]{1,0:T(8,128)(2,1)} %shard_map.560.grads, ...), custom_call_target="tpu_custom_call" | custom-call | tf_op jit(solution)/shard_map/pallas_call | solution.py:1142
  673.5 3.7 fusion.68
  680.6 2.9 copy.116
  (316 shorter events, 107.8 us)
Async XLA Ops:
  7.2 167.7 %copy-start = (bf16[1024,1024]{1,0:T(8,128)(2,1)S(1)}, bf16[1024,1024]{1,0:T(8,128)(2,1)}, u32[]{:S(2)}) copy-start(bf16[1024,1024]{1,0:T(8,128)(2,1)} %param.55) | copy-start | bytes 6291460
  7.3 147.7 %all-gather.17.cloned.1.call-start = ((), (), s32[]{:S(2)}) async-start(), calls=%async_computation.6 | async-start | bytes 9437184 | tf_op jit(solution)/shard_map/all_gather | solution.py:1668
  8.0 147.0 %all-gather.19.cloned.1.call-start = ((), (), s32[]{:S(2)}) async-start(), calls=%async_computation.7 | async-start | bytes 9437184 | tf_op jit(solution)/shard_map/all_gather | solution.py:1669
  8.7 50.2 %copy-start.76 = (s32[2]{0:T(128)S(1)}, s32[2]{0:T(128)}, u32[]{:S(2)}) copy-start(s32[2]{0:T(128)} %param.35) | copy-start | bytes 28
  8.7 224.6 %all-gather.21.cloned.1.call-start = ((), (), s32[]{:S(2)}) async-start(), calls=%async_computation.8 | async-start | bytes 9437184 | tf_op jit(solution)/shard_map/all_gather | solution.py:1685
  101.6 20.1 %copy-start.25 = (bf16[256,2,1024]{2,0,1:T(8,128)(2,1)S(1)}, bf16[256,2,1024]{2,0,1:T(8,128)(2,1)}, u32[]{:S(2)}) copy-start(bf16[256,2,1024]{2,0,1:T(8,128)(2,1)} %copy.121) | copy-start | bytes 3145732
  127.7 214.5 %all-gather.25.cloned.1.call-start = ((), (), s32[]{:S(2)}) async-start(), calls=%async_computation.10 | async-start | bytes 4325376 | tf_op jit(solution)/shard_map/all_gather | solution.py:1725
  128.2 5.9 copy-start.30
  148.9 3.5 copy-start.67
  148.9 3.5 copy-start.72
  258.5 118.2 %all-gather.23.cloned.1.call-start = ((), (), s32[]{:S(2)}) async-start(), calls=%async_computation.9 | async-start | bytes 9437184 | tf_op jit(solution)/shard_map/all_gather | solution.py:1747
  303.5 3.4 copy-start.3
  303.5 3.4 copy-start.20
  303.5 3.4 copy-start.29
  309.5 3.5 copy-start.60
  309.6 3.5 copy-start.61
  311.2 104.5 %reduce-scatter.5.cloned.1.call-start = ((), (), s32[]{:S(2)}) async-start(), calls=%async_computation.4 | async-start | bytes 2129920 | tf_op jit(solution)/shard_map/reduce_scatter | solution.py:1727
  311.2 23.3 %copy-start.13 = (f32[256,1024]{1,0:T(8,128)S(1)}, f32[256,1024]{1,0:T(8,128)}, u32[]{:S(2)}) copy-start(f32[256,1024]{1,0:T(8,128)} %copy-done.12) | copy-start | bytes 3145732
  362.7 3.4 copy-start.38
  362.8 5.2 copy-start.37
  364.1 9.3 %copy-start.18 = (bf16[256,1024]{1,0:T(8,128)(2,1)}, bf16[256,1024]{1,0:T(8,128)(2,1)S(1)}, u32[]{:S(2)}) copy-start(bf16[256,1024]{1,0:T(8,128)(2,1)S(1)} %convert_element_type.323.earlier) | copy-start | bytes 1572868
  364.2 7.4 %copy-start.22 = (bf16[8,32,1024]{2,1,0:T(8,128)(2,1)S(1)}, bf16[8,32,1024]{2,1,0:T(8,128)(2,1)}, u32[]{:S(2)}) copy-start(bf16[8,32,1024]{2,1,0:T(8,128)(2,1)} %shard_map.554) | copy-start | bytes 1572868
  376.5 106.5 %reduce-scatter.3.cloned.1.call-start = ((), (), s32[]{:S(2)}) async-start(), calls=%async_computation.2 | async-start | bytes 2621440 | tf_op jit(solution)/shard_map/reduce_scatter | solution.py:1727
  407.8 185.8 %all-gather.15.cloned.1.call-start = ((), (), s32[]{:S(2)}) async-start(), calls=%async_computation.5 | async-start | bytes 2129920 | tf_op jit(solution)/shard_map/all_gather | solution.py:1728
  407.8 8.0 %copy-start.49 = (bf16[1024,256]{1,0:T(8,128)(2,1)S(1)}, bf16[1024,256]{1,0:T(8,128)(2,1)}, u32[]{:S(2)}) copy-start(bf16[1024,256]{1,0:T(8,128)(2,1)} %copy-done.48) | copy-start | bytes 1572868
  415.7 7.1 %copy-start.17 = (bf16[512,1024]{1,0:T(8,128)(2,1)S(1)}, bf16[512,1024]{1,0:T(8,128)(2,1)}, u32[]{:S(2)}) copy-start(bf16[512,1024]{1,0:T(8,128)(2,1)} %copy-done.16) | copy-start | bytes 3145732
  415.7 177.8 %all-gather.13.cloned.1.call-start = ((), (), s32[]{:S(2)}) async-start(), calls=%async_computation.3 | async-start | bytes 2621440 | tf_op jit(solution)/shard_map/all_gather | solution.py:1728
  418.3 6.5 copy-start.19
  421.1 3.8 copy-start.36
  424.9 82.5 %collective-permute-start.5 = (bf16[4,256,1024]{2,1,0:T(8,128)(2,1)}, bf16[4,256,1024]{2,1,0:T(8,128)(2,1)}, u32[]{:S(2)}, u32[]{:S(2)}) collective-permute-start(bf16[4,256,1024]{2,1,0:T(8,128)(2,1)} %get-tuple-element.78.earlier), channel_id=1, source_target_pairs={{0,1},{1,0},{2,3},{3,2},{4,5},{5,4},{6,7},{7,6},{8,9},{9,8},{10,11... | collective-permute-start | bytes 6291464 | tf_op jit(solution)/shard_map/ppermute | solution.py:1570
  429.8 48.1 %copy-start.5 = (f32[512,1024]{1,0:T(8,128)S(1)}, f32[512,1024]{1,0:T(8,128)}, u32[]{:S(2)}) copy-start(f32[512,1024]{1,0:T(8,128)} %copy-done.4) | copy-start | bytes 6291460
  484.8 4.2 copy-start.26
  507.0 14.7 %collective-permute-start = (bf16[4,128,1024]{2,1,0:T(8,128)(2,1)}, bf16[4,128,1024]{2,1,0:T(8,128)(2,1)S(1)}, u32[]{:S(2)}, u32[]{:S(2)}) collective-permute-start(bf16[4,128,1024]{2,1,0:T(8,128)(2,1)} %get-tuple-element.85), channel_id=1, source_target_pairs={{0,1},{1,0},{2,3},{3,2},{4,5},{5,4},{6,7},{7,6},{8,9},{9,8},{10,11... | collective-permute-start | bytes 3145736 | tf_op jit(solution)/shard_map/ppermute | solution.py:1570
  511.5 5.9 copy-start.14
  511.5 5.9 copy-start.27
  515.4 14.5 %collective-permute-start.6 = (bf16[2,128,1024]{2,1,0:T(8,128)(2,1)}, bf16[2,128,1024]{2,1,0:T(8,128)(2,1)}, u32[]{:S(2)}, u32[]{:S(2)}) collective-permute-start(bf16[2,128,1024]{2,1,0:T(8,128)(2,1)} %pad_maximum_fusion.2), channel_id=1, source_target_pairs={{0,2},{1,3},{2,0},{3,1},{4,6},{5,7},{6,4},{7,5},{8,10},{9,11},{10,... | collective-permute-start | bytes 1572872 | tf_op jit(solution)/shard_map/ppermute | solution.py:1570
  516.2 14.0 %collective-permute-start.8 = (bf16[2,128,1024]{2,1,0:T(8,128)(2,1)}, bf16[2,128,1024]{2,1,0:T(8,128)(2,1)}, u32[]{:S(2)}, u32[]{:S(2)}) collective-permute-start(bf16[2,128,1024]{2,1,0:T(8,128)(2,1)} %stack.82), channel_id=1, source_target_pairs={{0,4},{1,5},{2,6},{3,7},{4,0},{5,1},{6,2},{7,3},{8,12},{9,13},{10,... | collective-permute-start | bytes 1572872 | tf_op jit(solution)/shard_map/ppermute | solution.py:1570
  522.7 7.5 %copy-start.21 = (bf16[4,256,1024]{2,1,0:T(8,128)(2,1)S(1)}, bf16[4,256,1024]{2,1,0:T(8,128)(2,1)}, u32[]{:S(2)}) copy-start(bf16[4,256,1024]{2,1,0:T(8,128)(2,1)} %shard_map.562) | copy-start | bytes 6291460
  527.6 56.4 %collective-permute-start.1 = (bf16[2,64,1024]{2,1,0:T(8,128)(2,1)S(1)}, bf16[2,64,1024]{2,1,0:T(8,128)(2,1)}, u32[]{:S(2)}, u32[]{:S(2)}) collective-permute-start(bf16[2,64,1024]{2,1,0:T(8,128)(2,1)S(1)} %pad_maximum_fusion.4), channel_id=1, source_target_pairs={{0,2},{1,3},{2,0},{3,1},{4,6},{5,7},{6,4},{7,5},{8,10},{9,11},{10,... | collective-permute-start | bytes 786440 | tf_op jit(solution)/shard_map/ppermute | solution.py:1570
  528.6 55.5 %collective-permute-start.3 = (bf16[2,64,1024]{2,1,0:T(8,128)(2,1)S(1)}, bf16[2,64,1024]{2,1,0:T(8,128)(2,1)}, u32[]{:S(2)}, u32[]{:S(2)}) collective-permute-start(bf16[2,64,1024]{2,1,0:T(8,128)(2,1)S(1)} %stack.81), channel_id=1, source_target_pairs={{0,4},{1,5},{2,6},{3,7},{4,0},{5,1},{6,2},{7,3},{8,12},{9,13},{10,... | collective-permute-start | bytes 786440 | tf_op jit(solution)/shard_map/ppermute | solution.py:1570
  532.2 55.1 %collective-permute-start.7 = (bf16[128,1024]{1,0:T(8,128)(2,1)}, bf16[128,1024]{1,0:T(8,128)(2,1)}, u32[]{:S(2)}, u32[]{:S(2)}) collective-permute-start(bf16[128,1024]{1,0:T(8,128)(2,1)} %get-tuple-element.141), channel_id=1, source_target_pairs={{0,4},{1,5},{2,6},{3,7},{4,0},{5,1},{6,2},{7,3},{8,12},{9,13},{10,... | collective-permute-start | bytes 786440 | tf_op jit(solution)/shard_map/ppermute | solution.py:1570
  533.4 53.8 %collective-permute-start.9 = (bf16[128,1024]{1,0:T(8,128)(2,1)S(1)}, bf16[128,1024]{1,0:T(8,128)(2,1)}, u32[]{:S(2)}, u32[]{:S(2)}) collective-permute-start(bf16[128,1024]{1,0:T(8,128)(2,1)S(1)} %get-tuple-element.142), channel_id=1, source_target_pairs={{0,2},{1,3},{2,0},{3,1},{4,6},{5,7},{6,4},{7,5},{8,10},{9,11},{10,... | collective-permute-start | bytes 786440 | tf_op jit(solution)/shard_map/ppermute | solution.py:1570
  534.9 49.1 %copy-start.28 = (bf16[4,128,1024]{2,1,0:T(8,128)(2,1)S(1)}, bf16[4,128,1024]{2,1,0:T(8,128)(2,1)}, u32[]{:S(2)}) copy-start(bf16[4,128,1024]{2,1,0:T(8,128)(2,1)} %shard_map.561) | copy-start | bytes 3145732
  585.1 5.0 collective-permute-start.2
  586.6 5.0 collective-permute-start.4
  673.4 5.1 copy-start.53
  673.4 6.8 copy-start.47
  690.4 3.7 copy-start.1
  (49 other events, 89.1 us)
Sparse Core Ops, SparseCore 0:
  10.0 76.0 all-gather.16
  88.0 65.2 all-gather.18
  155.7 69.8 all-gather.20
  258.6 62.3 all-gather.24
  323.2 52.9 all-gather.22
  378.4 37.2 reduce-scatter.4
  418.6 42.9 reduce-scatter.2
  463.2 38.5 all-gather.14
  503.4 44.7 all-gather.12

commit v4 on v3

--- a/solution.py
+++ b/solution.py
@@ -966,6 +966,60 @@
     )(terms.reshape(blocks), earlier).reshape(count, width)
 
 
+def sum_small_outer_kernel(
+    terms, earlier, left, one, two, out, away, kept, mine, came, send, recv, send_back, recv_back
+):
+    me = lax.axis_index("seq")
+    greet(PEERS)
+    mine[...] = terms[...].astype(low)
+    started = []
+    for mask in PEERS:
+        copy = remote(mine.at[me ^ mask], came.at[mask], send.at[mask], recv.at[mask], me ^ mask)
+        copy.start()
+        started.append(copy)
+    size = left.shape[1] // 8
+
+    def outer(place):
+        columns = pl.ds(pl.multiple_of((me ^ OWNERS[place]) * size, size), size)
+        target = (away, kept)[place // 4]
+        for row, grads in enumerate((one, two)):
+            target[place % 4, row * size : (row + 1) * size] = tn(left[:, columns], grads[...]).astype(low)
+
+    for place in range(4):
+        outer(place)
+    total = terms[me].astype(wide)
+    for mask in PEERS:
+        remote(mine.at[0], came.at[mask], send.at[mask], recv.at[mask], me ^ mask).wait_recv()
+        total = total + came[mask].astype(wide)
+    out[me] = total.astype(low)
+    for mask in PEERS:
+        copy = remote(out.at[me], out.at[me], send_back.at[mask], recv_back.at[mask], me ^ mask)
+        copy.start()
+        started.append(copy)
+    for place in range(4, 8):
+        outer(place)
+    for mask in PEERS:
+        remote(mine.at[0], out.at[me ^ mask], send_back.at[mask], recv_back.at[mask], me ^ mask).wait_recv()
+    for copy in started:
+        copy.wait_send()
+
+
+def sum_small_outer(terms, earlier, left, one, two):
+    count, width = terms.shape
+    blocks = (8, count // 8, width)
+    half = jax.ShapeDtypeStruct((4, left.shape[1] // 4, width), low)
+    total, away, kept = pl.pallas_call(
+        sum_small_outer_kernel,
+        out_shape=(jax.ShapeDtypeStruct(blocks, low), half, half),
+        in_specs=[vmem_spec(), any_spec()] + [vmem_spec()] * 3,
+        out_specs=(vmem_spec(),) * 3,
+        scratch_shapes=[pltpu.VMEM(blocks, low), pltpu.VMEM(blocks, low)]
+        + [pltpu.SemaphoreType.DMA((8,))] * 4,
+        compiler_params=params(11),
+    )(terms.reshape(blocks), earlier, left, one, two)
+    return total.reshape(count, width), away, kept
+
+
 def merge_parts_kernel(terms, stats, out, logsum, came, came_stats, send, recv, send_st, recv_st, back, recv_back, back_st, recv_back_st):
     me = lax.axis_index("seq")
     width = out.shape[2]
@@ -1745,8 +1799,7 @@
     d_second, grad_encoder_gain, grad_encoder_shift = second_back(flat(source_cotangent).astype(wide) + d_encoded)
     d_second_low = d_second.astype(low)
     d_all = lax.all_gather(d_second_low, "seq", axis=0)
-    dq_cross = sum_small(dq_part, 11, d_second_low)
-    cross_away, cross_kept = outer_by_owner(order, decoder_pair, encoded, dk_cross, dv_cross)
+    dq_cross, cross_away, cross_kept = sum_small_outer(dq_part, d_second_low, encoded, dk_cross, dv_cross)
     grad_cross_query = outer_sum(own(third_low), dq_cross)
     d_third, grad_self_gain, grad_self_shift = third_back(d_fourth + project_back(dq_cross, cross_query))
     self_low = d_third.astype(low)
@@ -1760,7 +1813,7 @@
         decoder_context,
         self_logs,
         True,
-        cross_away,
+        decoder_pair,
     )
     dq_self = dq_self.astype(low)
     target_own = own(target_flat)

time: 707 us -> 708 us (level)
  waiting for transfers between devices: 8.2 us -> 16.9 us
    pallas_call x3 -> x2, Pallas kernels: 58.5 us -> 37.7 us  [sum_small(): pl.pallas_call(sum_small_kernel, out_shape=jax.ShapeDtypeStruct(blocks, l...]
    pallas_call x1, Pallas kernels: 10.5 us -> 23.6 us  [sum_small_outer(): pl.pallas_call(sum_small_outer_kernel, out_shape=(jax.ShapeDtypeStruct(bl...]
    all_gather x1, waiting for transfers between devices: 0.02 us -> 7.63 us  [plane_body(): d_all = lax.all_gather(d_second_low, 'seq', axis=0)]
    unnamed x165 -> x163, local copies, waits for them, and re-layouts: 23.9 us -> 23.9 us
  transfers between devices with their start and end apart: 19 -> 19, of which waited for: 5 -> 6; matrix products, arithmetic and copies ran while one was open for 19% -> 19% of each run, Pallas kernels for 57% -> 56%
where the time goes in v4:
time: 708 us; the launch traced here: 702 us
  Pallas kernels  489 us (69%)
  matrix products  65.4 us (9%)
  local copies, waits for them, and re-layouts  61.8 us (9%)
  other arithmetic  44.7 us (6%)
  waiting for transfers between devices  16.9 us (2%)
  between operations  15.2 us (2%)
  starting transfers between devices  8.96 us (1%)
    pallas_call x1, Pallas kernels, finish(): pl.pallas_call(functools.partial(finish_kernel, lax.axis_size('dp')), out...  80.3 us
    pallas_call x1, Pallas kernels, flash_backward(): pl.pallas_call(functools.partial(flash_backward_kernel, chunk), out_shape...  49.2 us
    pallas_call x1, Pallas kernels, scatter_plane(): pl.pallas_call(scatter_plane_kernel, out_shape=(jax.ShapeDtypeStruct((row...  48.8 us
    pallas_call x1, Pallas kernels, gather_table(): pl.pallas_call(gather_table_kernel, out_shape=(jax.ShapeDtypeStruct((8,)...  48 us
    pallas_call x1, Pallas kernels, merge_parts(): pl.pallas_call(merge_parts_kernel, out_shape=(jax.ShapeDtypeStruct((8, ro...  37.8 us
    pallas_call x2, Pallas kernels, sum_small(): pl.pallas_call(sum_small_kernel, out_shape=jax.ShapeDtypeStruct(blocks, l...  37.7 us
    pallas_call x1, Pallas kernels, feed_backward(): pl.pallas_call(feed_backward_kernel, out_shape=(jax.ShapeDtypeStruct(rows...  31.1 us
    dot_general x12, matrix products, project(): return jnp.dot(rows, weight, preferred_element_type=jnp.float32)  31 us
  transfers between devices with their start and end apart: 19, of which 6 were waited for; matrix products, arithmetic and copies ran while one was open for 19% of the time, Pallas kernels for 56%

profile of v4, /device:TPU:0, one launch (start us, length us, event | category | flops | bytes accessed | tf_op | source)
XLA Modules:
  0.0 701.9 jit_solution(1192302987516453411)
XLA Ops:
  11.0 48.0 %shard_map.535 = (bf16[8,256,1024]{2,1,0:T(8,128)(2,1)}, bf16[8,64,1024]{2,1,0:T(8,128)(2,1)}) custom-call(bf16[2,256,1024]{2,1,0:T(8,128)(2,1)} %bitcast.234, bf16[64,1024]{1,0:T(8,128)(2,1)} %bitcast.261), custom_call_target="tpu_custom_call" | custom-call | tf_op jit(solution)/shard_map/pallas_call | solution.py:748
  63.3 7.4 %convolution_convert_fusion.queries.keys.values = bf16[2048,768]{1,0:T(8,128)(2,1)} fusion(bf16[2048,1024]{1,0:T(8,128)(2,1)} %bitcast.232, bf16[1024,256]{1,0:T(8,128)(2,1)S(1)} %get-tuple-element.176, bf16[1024,256]{1,0:T(8,128)(2,1)S(1)} %get-tuple-element.177, bf16[1024,256]{1,0:T(8,128)(2,1)S(1)} %constant_dynamic-slice_fusion.4), kind=kOutput, calls=%fused_computation | convolution fusion | flops 3227516928 | bytes 8912896 | tf_op jit(solution)/shard_map/dot_general | solution.py:29
  70.6 30.9 %shard_map.536 = (bf16[2048,256]{1,0:T(8,128)(2,1)}, f32[2048,128]{1,0:T(8,128)}) custom-call(s32[1]{0:T(128)} %dynamic_slice.54.length, bf16[2048,768]{1,0:T(8,128)(2,1)} %convolution_convert_fusion.queries.keys.values, bf16[2048,768]{1,0:T(8,128)(2,1)} %convolution_convert_fusion.queries.keys.values, ...), custom_call_target="tpu_custom_call" | custom-call | tf_op jit(solution)/shard_map/pallas_call | solution.py:1265
  101.5 20.1 %shard_map.537 = bf16[2,256,1024]{2,1,0:T(8,128)(2,1)} custom-call(bf16[8,256,256]{2,1,0:T(8,128)(2,1)} %bitcast.237), custom_call_target="tpu_custom_call" | custom-call | tf_op jit(solution)/shard_map/pallas_call | solution.py:873
  121.7 3.3 fusion.73
  129.3 3.2 convolution_convert_fusion.7.values
  135.7 13.2 %shard_map.539 = (bf16[256,1024]{1,0:T(8,128)(2,1)}, f32[256,128]{1,0:T(8,128)}, f32[256,128]{1,0:T(8,128)}) custom-call(s32[2]{0:T(128)} %length.3, bf16[256,1024]{1,0:T(8,128)(2,1)} %convolution_convert_fusion.9.queries, bf16[256,1024]{1,0:T(8,128)(2,1)} %convolution_convert_fusion.8.keys, bf16[256,1024]{1,0:T(8,128)(2,1)} %convolution_convert_fusion.7.values), custom_call_target="tpu_custom_call" | custom-call | tf_op jit(solution)/shard_map/pallas_call | solution.py:1409
  148.9 2.7 fusion.74
  154.9 15.7 %shard_map.538 = f32[512,1024]{1,0:T(8,128)} custom-call(bf16[512,1024]{1,0:T(8,128)(2,1)} %fusion.1.rows, bf16[8,1024,512]{2,1,0:T(8,128)(2,1)} %bitcast.227, bf16[8,512,1024]{2,1,0:T(8,128)(2,1)} %bitcast.228), custom_call_target="tpu_custom_call" | custom-call | tf_op jit(solution)/shard_map/pallas_call | solution.py:1521
  170.7 2.9 fusion.66
  174.9 2.2 convolution_convert_fusion.2.values
  177.1 2.2 convolution_convert_fusion.3.keys
  179.3 6.3 shard_map.540
  187.3 37.8 %shard_map.541 = (bf16[8,32,1024]{2,1,0:T(8,128)(2,1)}, f32[8,32,128]{2,1,0:T(8,128)}) custom-call(bf16[8,32,1024]{2,1,0:T(8,128)(2,1)} %bitcast.262, f32[8,2,32,128]{3,2,1,0:T(8,128)} %pad_maximum_fusion.3.stats), custom_call_target="tpu_custom_call" | custom-call | tf_op jit(solution)/shard_map/pallas_call | solution.py:1072
  225.1 2.6 fusion.75
  230.9 2.4 fusion.19
  233.3 18.6 %shard_map.542 = bf16[8,32,1024]{2,1,0:T(8,128)(2,1)} custom-call(f32[8,32,1024]{2,1,0:T(8,128)} %bitcast.253, bf16[8,512,1024]{2,1,0:T(8,128)(2,1)} %bitcast.220), custom_call_target="tpu_custom_call" | custom-call | tf_op jit(solution)/shard_map/pallas_call | solution.py:958
  258.5 1.9 convert_bitcast_fusion
  260.4 2.0 copy.94
  262.4 4.7 fusion.20.earlier
  267.1 19.1 %shard_map.543 = bf16[8,32,1024]{2,1,0:T(8,128)(2,1)} custom-call(f32[8,32,1024]{2,1,0:T(8,128)} %bitcast.236, f32[256,1024]{1,0:T(8,128)} %fusion.20.earlier), custom_call_target="tpu_custom_call" | custom-call | tf_op jit(solution)/shard_map/pallas_call | solution.py:958
  286.2 2.4 multiply_reduce_fusion.6
  291.8 11.7 %shard_map.544 = (f32[256,1024]{1,0:T(8,128)}, bf16[512,1024]{1,0:T(8,128)(2,1)}, bf16[512,1024]{1,0:T(8,128)(2,1)}) custom-call(s32[2]{0:T(128)} %broadcast_subtract_fusion.length, bf16[256,1024]{1,0:T(8,128)(2,1)} %convolution_convert_fusion.6.queries, bf16[512,1024]{1,0:T(8,128)(2,1)} %convolution_convert_fusion.3.keys, ...), custom_call_target="tpu_custom_call" | custom-call | tf_op jit(solution)/shard_map/pallas_call | solution.py:1473
  303.5 3.3 fusion.79
  313.1 23.6 %shard_map.545 = (bf16[8,32,1024]{2,1,0:T(8,128)(2,1)}, bf16[4,256,1024]{2,1,0:T(8,128)(2,1)}, bf16[4,256,1024]{2,1,0:T(8,128)(2,1)}) custom-call(f32[8,32,1024]{2,1,0:T(8,128)} %bitcast.251, bf16[512,1024]{1,0:T(8,128)(2,1)} %add_convert_fusion.2.earlier, bf16[512,1024]{1,0:T(8,128)(2,1)} %copy-done.12, bf16[512,1024]{1,0:T(8,128)(2,1)} %get-tuple-element.74.one, ...), custom_call_target="tpu_custom_call" | custom-call | tf_op jit(solution)/shard_map/pallas_call | solution.py:1011
  336.6 3.7 multiply_reduce_fusion.7
  344.3 10.4 %shard_map.546 = (f32[256,1024]{1,0:T(8,128)}, bf16[256,1024]{1,0:T(8,128)(2,1)}, bf16[256,1024]{1,0:T(8,128)(2,1)}) custom-call(s32[2]{0:T(128)} %length.3, bf16[256,1024]{1,0:T(8,128)(2,1)} %convolution_convert_fusion.9.queries, bf16[256,1024]{1,0:T(8,128)(2,1)} %convolution_convert_fusion.8.keys, bf16[256,1024]{1,0:T(8,128)(2,1)} %convolution_convert_fusion.7.values, ...), custom_call_target="tpu_custom_call" | custom-call | tf_op jit(solution)/shard_map/pallas_call | solution.py:1473
  356.1 2.0 fusion.7
  368.5 7.6 %all-gather.23.cloned.1.call-done = bf16[4096,1024]{1,0:T(8,128)(2,1)} async-done(((bf16[512,1024]{1,0:T(8,128)(2,1)}), bf16[4096,1024]{1,0:T(8,128)(2,1)}) %all-gather.23.cloned.1.call-update) | async-done | bytes 8388624 | tf_op jit(solution)/shard_map/all_gather | solution.py:1801
  376.1 31.1 %shard_map.547 = (bf16[8,512,1024]{2,1,0:T(8,128)(2,1)}, bf16[1024,1024]{1,0:T(8,128)(2,1)}) custom-call(bf16[8,512,1024]{2,1,0:T(8,128)(2,1)} %bitcast.221, bf16[8,512,1024]{2,1,0:T(8,128)(2,1)} %bitcast.226, bf16[1024,512]{1,0:T(8,128)(2,1)} %expand.2, bf16[512,1024]{1,0:T(8,128)(2,1)} %contract.2, bf16[256,1024]{1,0:T(8,128)(2,1)} %copy-done.18), custom_call_target="tpu_custom_call" | custom-call | tf_op jit(solution)/shard_map/pallas_call | solution.py:1603
  409.6 2.3 slice_bitcast_fusion
  411.8 4.4 reduce-scatter.5.cloned.1.call-done
  416.3 2.5 pad_maximum_fusion.weights
  418.9 2.7 copy.98.keys_t
  423.4 2.0 copy.116
  430.4 48.8 %shard_map.548 = (f32[512,1024]{1,0:T(8,128)}, f32[1024,512]{1,0:T(8,128)}, f32[512,1024]{1,0:T(8,128)}) custom-call(bf16[8,512,1024]{2,1,0:T(8,128)(2,1)} %get-tuple-element.81.terms, bf16[32,2,32,1024]{3,2,1,0:T(8,128)(2,1)} %bitcast.223, bf16[1024,512]{1,0:T(8,128)(2,1)} %expand.3, bf16[512,1024]{1,0:T(8,128)(2,1)} %contract.3), custom_call_target="tpu_custom_call" | custom-call | tf_op jit(solution)/shard_map/pallas_call | solution.py:827
  479.2 3.2 multiply_reduce_fusion.1
  482.4 1.9 fusion.60
  486.2 4.2 convolution_convert_fusion.1
  490.4 17.1 %shard_map.549 = (bf16[8,256,256]{2,1,0:T(8,128)(2,1)}, bf16[4,128,1024]{2,1,0:T(8,128)(2,1)}, bf16[4,128,1024]{2,1,0:T(8,128)(2,1)}) custom-call(bf16[2,256,1024]{2,1,0:T(8,128)(2,1)} %bitcast.252, bf16[512,1024]{1,0:T(8,128)(2,1)} %bitcast.231, bf16[512,1024]{1,0:T(8,128)(2,1)} %copy-done.26), custom_call_target="tpu_custom_call" | custom-call | tf_op jit(solution)/shard_map/pallas_call | solution.py:916
  507.9 4.2 shard_map.552
  512.2 2.0 stack.82
  523.3 2.9 shard_map.551
  532.0 1.9 fusion.22
  536.6 49.2 %shard_map.550.grads = bf16[2048,768]{1,0:T(8,128)(2,1)} custom-call(s32[1]{0:T(128)} %dynamic_slice.54.length, bf16[2048,768]{1,0:T(8,128)(2,1)} %convolution_convert_fusion.queries.keys.values, bf16[2048,256]{1,0:T(8,128)(2,1)} %bitcast.225, f32[4,2048]{1,0:T(4,128)} %slice_bitcast_fusion.1.logsum, f32[4,2048]{1,0:T(4,128)} %bitcast.263, ...), custom_call_target="tpu_custom_call" | custom-call | tf_op jit(solution)/shard_map/pallas_call | solution.py:1337
  594.2 80.3 %shard_map.553 = (f32[2,256,1024]{2,1,0:T(8,128)}, f32[448,1024]{1,0:T(8,128)}, f32[384,1024]{1,0:T(8,128)}, f32[1024,512]{1,0:T(8,128)}, f32[512,1024]{1,0:T(8,128)}, /*index=5*/f32[832,1024]{1,0:T(8,128)}) custom-call(bf16[2048,1024]{1,0:T(8,128)(2,1)} %bitcast.233, bf16[2048,768]{1,0:T(8,128)(2,1)} %shard_map.550.grads, ...), custom_call_target="tpu_custom_call" | custom-call | tf_op jit(solution)/shard_map/pallas_call | solution.py:1196
  674.5 3.7 fusion.68
  681.6 2.9 copy.115
  (312 shorter events, 107.3 us)
Async XLA Ops:
  7.2 167.7 %copy-start = (bf16[1024,1024]{1,0:T(8,128)(2,1)S(1)}, bf16[1024,1024]{1,0:T(8,128)(2,1)}, u32[]{:S(2)}) copy-start(bf16[1024,1024]{1,0:T(8,128)(2,1)} %param.54) | copy-start | bytes 6291460
  7.3 147.7 %all-gather.17.cloned.1.call-start = ((), (), s32[]{:S(2)}) async-start(), calls=%async_computation.6 | async-start | bytes 9437184 | tf_op jit(solution)/shard_map/all_gather | solution.py:1722
  8.0 146.9 %all-gather.19.cloned.1.call-start = ((), (), s32[]{:S(2)}) async-start(), calls=%async_computation.7 | async-start | bytes 9437184 | tf_op jit(solution)/shard_map/all_gather | solution.py:1723
  8.7 50.2 %copy-start.76 = (s32[2]{0:T(128)S(1)}, s32[2]{0:T(128)}, u32[]{:S(2)}) copy-start(s32[2]{0:T(128)} %param.34) | copy-start | bytes 28
  8.7 224.6 %all-gather.21.cloned.1.call-start = ((), (), s32[]{:S(2)}) async-start(), calls=%async_computation.8 | async-start | bytes 9437184 | tf_op jit(solution)/shard_map/all_gather | solution.py:1739
  101.5 20.1 %copy-start.25 = (bf16[256,2,1024]{2,0,1:T(8,128)(2,1)S(1)}, bf16[256,2,1024]{2,0,1:T(8,128)(2,1)}, u32[]{:S(2)}) copy-start(bf16[256,2,1024]{2,0,1:T(8,128)(2,1)} %copy.120) | copy-start | bytes 3145732
  127.7 216.6 %all-gather.25.cloned.1.call-start = ((), (), s32[]{:S(2)}) async-start(), calls=%async_computation.10 | async-start | bytes 4325376 | tf_op jit(solution)/shard_map/all_gather | solution.py:1779
  128.2 5.9 copy-start.29
  129.3 3.2 copy-start.40
  148.8 3.5 copy-start.67
  148.9 3.5 copy-start.72
  258.4 117.7 %all-gather.23.cloned.1.call-start = ((), (), s32[]{:S(2)}) async-start(), calls=%async_computation.9 | async-start | bytes 9437184 | tf_op jit(solution)/shard_map/all_gather | solution.py:1801
  303.5 3.4 copy-start.3
  303.5 3.4 copy-start.20
  303.5 3.4 copy-start.24
  311.1 105.1 %reduce-scatter.5.cloned.1.call-start = ((), (), s32[]{:S(2)}) async-start(), calls=%async_computation.4 | async-start | bytes 2129920 | tf_op jit(solution)/shard_map/reduce_scatter | solution.py:1781
  313.1 23.6 %copy-start.15 = (f32[256,1024]{1,0:T(8,128)S(1)}, f32[256,1024]{1,0:T(8,128)}, u32[]{:S(2)}) copy-start(f32[256,1024]{1,0:T(8,128)} %copy-done.14) | copy-start | bytes 3145732
  354.6 3.4 copy-start.37
  354.6 5.2 copy-start.36
  356.1 9.3 %copy-start.18 = (bf16[256,1024]{1,0:T(8,128)(2,1)}, bf16[256,1024]{1,0:T(8,128)(2,1)S(1)}, u32[]{:S(2)}) copy-start(bf16[256,1024]{1,0:T(8,128)(2,1)S(1)} %convert_element_type.323.earlier) | copy-start | bytes 1572868
  356.1 7.4 %copy-start.39 = (bf16[8,32,1024]{2,1,0:T(8,128)(2,1)S(1)}, bf16[8,32,1024]{2,1,0:T(8,128)(2,1)}, u32[]{:S(2)}) copy-start(bf16[8,32,1024]{2,1,0:T(8,128)(2,1)} %get-tuple-element.77) | copy-start | bytes 1572868
  368.5 115.9 %reduce-scatter.3.cloned.1.call-start = ((), (), s32[]{:S(2)}) async-start(), calls=%async_computation.2 | async-start | bytes 2621440 | tf_op jit(solution)/shard_map/reduce_scatter | solution.py:1781
  407.3 187.0 %all-gather.15.cloned.1.call-start = ((), (), s32[]{:S(2)}) async-start(), calls=%async_computation.5 | async-start | bytes 2129920 | tf_op jit(solution)/shard_map/all_gather | solution.py:1782
  407.3 9.0 %copy-start.49 = (bf16[1024,256]{1,0:T(8,128)(2,1)S(1)}, bf16[1024,256]{1,0:T(8,128)(2,1)}, u32[]{:S(2)}) copy-start(bf16[1024,256]{1,0:T(8,128)(2,1)} %copy-done.48) | copy-start | bytes 1572868
  416.3 7.1 %copy-start.13 = (bf16[512,1024]{1,0:T(8,128)(2,1)S(1)}, bf16[512,1024]{1,0:T(8,128)(2,1)}, u32[]{:S(2)}) copy-start(bf16[512,1024]{1,0:T(8,128)(2,1)} %copy-done.12) | copy-start | bytes 3145732
  416.3 178.0 %all-gather.13.cloned.1.call-start = ((), (), s32[]{:S(2)}) async-start(), calls=%async_computation.3 | async-start | bytes 2621440 | tf_op jit(solution)/shard_map/all_gather | solution.py:1782
  418.9 6.5 copy-start.19
  421.6 3.9 copy-start.35
  421.6 86.4 %collective-permute-start.5 = (bf16[4,256,1024]{2,1,0:T(8,128)(2,1)}, bf16[4,256,1024]{2,1,0:T(8,128)(2,1)}, u32[]{:S(2)}, u32[]{:S(2)}) collective-permute-start(bf16[4,256,1024]{2,1,0:T(8,128)(2,1)} %get-tuple-element.88), channel_id=1, source_target_pairs={{0,1},{1,0},{2,3},{3,2},{4,5},{5,4},{6,7},{7,6},{8,9},{9,8},{10,11... | collective-permute-start | bytes 6291464 | tf_op jit(solution)/shard_map/ppermute | solution.py:1624
  430.4 48.8 %copy-start.5 = (f32[512,1024]{1,0:T(8,128)S(1)}, f32[512,1024]{1,0:T(8,128)}, u32[]{:S(2)}) copy-start(f32[512,1024]{1,0:T(8,128)} %copy-done.4) | copy-start | bytes 6291460
  486.2 4.3 copy-start.26
  507.6 14.8 %collective-permute-start = (bf16[4,128,1024]{2,1,0:T(8,128)(2,1)}, bf16[4,128,1024]{2,1,0:T(8,128)(2,1)S(1)}, u32[]{:S(2)}, u32[]{:S(2)}) collective-permute-start(bf16[4,128,1024]{2,1,0:T(8,128)(2,1)} %get-tuple-element.86), channel_id=1, source_target_pairs={{0,1},{1,0},{2,3},{3,2},{4,5},{5,4},{6,7},{7,6},{8,9},{9,8},{10,11... | collective-permute-start | bytes 3145736 | tf_op jit(solution)/shard_map/ppermute | solution.py:1624
  512.2 5.8 copy-start.16
  512.2 5.8 copy-start.27
  516.1 14.5 %collective-permute-start.6 = (bf16[2,128,1024]{2,1,0:T(8,128)(2,1)}, bf16[2,128,1024]{2,1,0:T(8,128)(2,1)}, u32[]{:S(2)}, u32[]{:S(2)}) collective-permute-start(bf16[2,128,1024]{2,1,0:T(8,128)(2,1)} %pad_maximum_fusion.2), channel_id=1, source_target_pairs={{0,2},{1,3},{2,0},{3,1},{4,6},{5,7},{6,4},{7,5},{8,10},{9,11},{10,... | collective-permute-start | bytes 1572872 | tf_op jit(solution)/shard_map/ppermute | solution.py:1624
  517.7 14.3 %collective-permute-start.8 = (bf16[2,128,1024]{2,1,0:T(8,128)(2,1)}, bf16[2,128,1024]{2,1,0:T(8,128)(2,1)}, u32[]{:S(2)}, u32[]{:S(2)}) collective-permute-start(bf16[2,128,1024]{2,1,0:T(8,128)(2,1)} %stack.82), channel_id=1, source_target_pairs={{0,4},{1,5},{2,6},{3,7},{4,0},{5,1},{6,2},{7,3},{8,12},{9,13},{10,... | collective-permute-start | bytes 1572872 | tf_op jit(solution)/shard_map/ppermute | solution.py:1624
  523.3 8.7 %copy-start.21 = (bf16[4,256,1024]{2,1,0:T(8,128)(2,1)S(1)}, bf16[4,256,1024]{2,1,0:T(8,128)(2,1)}, u32[]{:S(2)}) copy-start(bf16[4,256,1024]{2,1,0:T(8,128)(2,1)} %shard_map.552) | copy-start | bytes 6291460
  528.2 57.5 %collective-permute-start.1 = (bf16[2,64,1024]{2,1,0:T(8,128)(2,1)S(1)}, bf16[2,64,1024]{2,1,0:T(8,128)(2,1)}, u32[]{:S(2)}, u32[]{:S(2)}) collective-permute-start(bf16[2,64,1024]{2,1,0:T(8,128)(2,1)S(1)} %pad_maximum_fusion.4), channel_id=1, source_target_pairs={{0,2},{1,3},{2,0},{3,1},{4,6},{5,7},{6,4},{7,5},{8,10},{9,11},{10,... | collective-permute-start | bytes 786440 | tf_op jit(solution)/shard_map/ppermute | solution.py:1624
  529.9 55.8 %collective-permute-start.3 = (bf16[2,64,1024]{2,1,0:T(8,128)(2,1)S(1)}, bf16[2,64,1024]{2,1,0:T(8,128)(2,1)}, u32[]{:S(2)}, u32[]{:S(2)}) collective-permute-start(bf16[2,64,1024]{2,1,0:T(8,128)(2,1)S(1)} %stack.81), channel_id=1, source_target_pairs={{0,4},{1,5},{2,6},{3,7},{4,0},{5,1},{6,2},{7,3},{8,12},{9,13},{10,... | collective-permute-start | bytes 786440 | tf_op jit(solution)/shard_map/ppermute | solution.py:1624
  534.0 55.1 %collective-permute-start.7 = (bf16[128,1024]{1,0:T(8,128)(2,1)}, bf16[128,1024]{1,0:T(8,128)(2,1)}, u32[]{:S(2)}, u32[]{:S(2)}) collective-permute-start(bf16[128,1024]{1,0:T(8,128)(2,1)} %get-tuple-element.143), channel_id=1, source_target_pairs={{0,4},{1,5},{2,6},{3,7},{4,0},{5,1},{6,2},{7,3},{8,12},{9,13},{10,... | collective-permute-start | bytes 786440 | tf_op jit(solution)/shard_map/ppermute | solution.py:1624
  534.2 54.8 %collective-permute-start.9 = (bf16[128,1024]{1,0:T(8,128)(2,1)S(1)}, bf16[128,1024]{1,0:T(8,128)(2,1)}, u32[]{:S(2)}, u32[]{:S(2)}) collective-permute-start(bf16[128,1024]{1,0:T(8,128)(2,1)S(1)} %get-tuple-element.144), channel_id=1, source_target_pairs={{0,2},{1,3},{2,0},{3,1},{4,6},{5,7},{6,4},{7,5},{8,10},{9,11},{10,... | collective-permute-start | bytes 786440 | tf_op jit(solution)/shard_map/ppermute | solution.py:1624
  536.6 49.2 %copy-start.28 = (bf16[4,128,1024]{2,1,0:T(8,128)(2,1)S(1)}, bf16[4,128,1024]{2,1,0:T(8,128)(2,1)}, u32[]{:S(2)}) copy-start(bf16[4,128,1024]{2,1,0:T(8,128)(2,1)} %shard_map.551) | copy-start | bytes 3145732
  586.8 5.0 collective-permute-start.2
  587.2 5.0 collective-permute-start.4
  674.5 5.1 copy-start.53
  674.5 6.8 copy-start.47
  678.2 3.1 copy-start.8
  691.4 3.7 copy-start.1
  (48 other events, 85.5 us)
Sparse Core Ops, SparseCore 0:
  10.0 76.0 all-gather.16
  88.0 65.2 all-gather.18
  155.7 69.8 all-gather.20
  258.5 62.1 all-gather.24
  323.0 53.0 all-gather.22
  378.9 37.3 reduce-scatter.4
  419.1 42.9 reduce-scatter.2
  463.7 38.5 all-gather.14
  504.0 44.7 all-gather.12
